TPU v7x, 32 devices: a whole 2x2x4 slice. The times are simulated.
32 devices in a mesh: wide: 8 (over y, x, core), narrow: 4 (over z).
Axes of the slice: x: 2, y: 2, z: 4, core: 2. Of those that a mesh axis runs over, the one named last changes fastest.
Arguments:
- dosages: int32 [2048, 6144], P('narrow', 'wide'), may hold values from 0 to 3, as said below
- allele_counts: int32 [2048], P('narrow'), may hold values from 4000 to 384000, as said below
- called_counts: int32 [2048], P('narrow'), may hold values from 200000 to 400000
Outputs:
- relation: float32 [8, 4, 192, 6144], P(None, 'narrow', None, 'wide')
Inputs may be any that keep to these rules, and one draw needn't show every extreme that they name: 3 marks a missing call; 0, 1 and 2 are dosages. `allele_counts`: the floor of the SNP's called_counts times a whole number p from 1 to 48, divided by 50, so that freq lies in (0, 0.5).
All inputs are finite; a program needn't handle non-finite values.
Results may differ from a plain program's by a relative error of at most 0.0043.
Values may be sent and summed in bfloat16 or wider, within the bound.
No kernel may reach another device: no remote copies, remote signals or barrier semaphores. Data moves between devices by JAX's collectives and lax.ppermute only.
A program may use at most 128 MiB of HBM per device.

v0:
```python
import jax
import jax.numpy as jnp
from jax import lax
from jax.sharding import PartitionSpec as P

SNPS = 2048


def standardize(dosages, allele_counts, called_counts):
    freq = allele_counts.astype(jnp.float32) / (2.0 * called_counts.astype(jnp.float32))
    freq = freq[:, None]
    values = (dosages.astype(jnp.float32) - 2.0 * freq) * lax.rsqrt(2.0 * freq * (1.0 - freq))
    values = jnp.where(dosages == 3, jnp.zeros_like(values), values)
    return values.astype(jnp.bfloat16)


def shards(dosages, allele_counts, called_counts):
    standard = standardize(dosages, allele_counts, called_counts)
    sub_width = standard.shape[1] // lax.axis_size("narrow")
    block_rows = lax.all_gather(standard, "narrow", axis=0, tiled=True)
    position = lax.axis_index("narrow") * sub_width
    panel = lax.dynamic_slice_in_dim(block_rows, position, sub_width, 1)
    col_count = block_rows.shape[1]
    gathered = lax.all_gather(panel, "wide", axis=1, tiled=True)
    result = (
        lax.dot_general(
            gathered, block_rows, (((0,), (0,)), ((), ())), preferred_element_type=jnp.float32
        )
        / SNPS
    )
    return result.reshape(lax.axis_size("wide"), 1, sub_width, col_count)


def solution(mesh):
    return jax.shard_map(
        shards,
        mesh=mesh,
        in_specs=(P("narrow", "wide"), P("narrow"), P("narrow")),
        out_specs=P(None, "narrow", None, "wide"),
        check_vma=False,
    )
```

profile of v0, /device:TPU:0, one launch (start us, length us, event | category | flops | bytes accessed | tf_op | source)
XLA Modules:
  0.0 138.9 jit_solution(6937562079051329262)
XLA Ops:
  6.5 0.0 copy-start
  6.5 0.0 copy-start.1
  6.5 0.0 all-gather.3.cloned.1.call-start
  6.5 1.9 %copy.5 = s32[512,768]{0,1:T(8,128)S(1)} copy(s32[512,768]{1,0:T(8,128)} %param.3) | data formatting | bytes 3145728 | tf_op args[0]
  8.4 0.0 copy-done
  8.5 0.0 copy-done.1
  8.5 1.2 select_convert_fusion
  9.7 0.0 all-gather.3.cloned.1.call-update
  9.7 0.0 all-gather.5.cloned.1.call-start
  9.7 66.3 %all-gather.3.cloned.1.call-done = bf16[2048,768]{0,1:T(8,128)(2,1)} async-done(((bf16[512,768]{0,1:T(8,128)(2,1)}), bf16[2048,768]{0,1:T(8,128)(2,1)}) %all-gather.3.cloned.1.call-update) | async-done | bytes 3145744 | tf_op jit(solution)/shard_map/all_gather | solution.py:20
  76.0 2.1 %constant_dynamic-slice_fusion = bf16[2048,192]{0,1:T(8,128)(2,1)} fusion(bf16[2048,768]{0,1:T(8,128)(2,1)} %all-gather.3.cloned.1.call-done, s32[]{:T(128)S(6)} %select_n.8), kind=kLoop, calls=%fused_computation.5 | loop fusion | bytes 1572868 | tf_op jit(solution)/shard_map/dynamic_slice | solution.py:22
  78.1 0.0 all-gather.5.cloned.1.call-update
  78.1 44.4 %all-gather.5.cloned.1.call-done = bf16[2048,1536]{0,1:T(8,128)(2,1)} async-done(((bf16[2048,192]{0,1:T(8,128)(2,1)}), bf16[2048,1536]{0,1:T(8,128)(2,1)}) %all-gather.5.cloned.1.call-update) | async-done | bytes 6291472 | tf_op jit(solution)/shard_map/all_gather | solution.py:24
  122.5 9.5 %convolution_multiply_fusion = f32[1536,768]{1,0:T(8,128)} fusion(bf16[2048,1536]{0,1:T(8,128)(2,1)} %all-gather.5.cloned.1.call-done, bf16[2048,768]{0,1:T(8,128)(2,1)} %all-gather.3.cloned.1.call-done), kind=kOutput, calls=%fused_computation | convolution fusion | flops 4833017856 | bytes 14155776 | tf_op jit(solution)/shard_map/dot_general | solution.py:26
  (1 shorter events, 0.0 us)
Async XLA Ops:
  6.5 1.9 %copy-start = (s32[512]{0:T(512)S(1)}, s32[512]{0:T(512)}, u32[]{:S(2)}) copy-start(s32[512]{0:T(512)} %param.5) | copy-start | bytes 6148
  6.5 1.9 %copy-start.1 = (s32[512]{0:T(512)S(1)}, s32[512]{0:T(512)}, u32[]{:S(2)}) copy-start(s32[512]{0:T(512)} %param.4) | copy-start | bytes 6148
  6.5 69.5 %all-gather.3.cloned.1.call-start = ((), (), s32[]{:S(2)}) async-start(), calls=%async_computation | async-start | bytes 3932160 | tf_op jit(solution)/shard_map/all_gather | solution.py:20
  9.7 112.8 %all-gather.5.cloned.1.call-start = ((), (), s32[]{:S(2)}) async-start(), calls=%async_computation.1 | async-start | bytes 7077888 | tf_op jit(solution)/shard_map/all_gather | solution.py:24
Sparse Core Ops, SparseCore 0:
  9.8 66.1 all-gather.2
  78.2 44.2 all-gather.4
where the time goes:
time: 139 us
  waiting for transfers between devices  111 us (80%)
  between operations  13.4 us (10%)
  matrix products  9.54 us (7%)
  local copies, waits for them, and re-layouts  3.99 us (3%)
    all_gather x1, waiting for transfers between devices, shards(): block_rows = lax.all_gather(standard, 'narrow', axis=0, tiled=True)  66.3 us
    all_gather x1, waiting for transfers between devices, shards(): gathered = lax.all_gather(panel, 'wide', axis=1, tiled=True)  44.4 us
    dot_general x1, matrix products, shards(): lax.dot_general(gathered, block_rows, (((0,), (0,)), ((), ())), preferred...  9.54 us
  transfers between devices with their start and end apart: 2, of which 2 were waited for; matrix products, arithmetic and copies ran while one was open for 0% of the time, Pallas kernels for 0%

commit v1 on v0

v1 whole, which is shorter than its diff:
```python
import functools

import jax
import jax.numpy as jnp
from jax import lax
from jax.experimental import pallas as pl
from jax.experimental.pallas import tpu as pltpu
from jax.sharding import PartitionSpec as P

PARTS = 2
LANES = 128
ANY = pl.BlockSpec(memory_space=pl.ANY)


def partners(z):
    side = lax.rem(z, 2)
    return z + 1 - 2 * side, z - 1 + 2 * side


def trade(value, odd, step):
    n = lax.axis_size("narrow")
    pairs = []
    for low in range(odd, n - 1, 2):
        if low + 1 - step >= 0:
            pairs.append((low, low + 1))
        if low + step <= n - 1:
            pairs.append((low + 1, low))
    return lax.ppermute(value, "narrow", pairs) if pairs else None


def slab_of(z, odd, step):
    side = lax.rem(z + odd, 2)
    return z + step * (1 - 2 * side)


def standardize_kernel(n, dosages, allele, called, own, *without):
    z = lax.axis_index("narrow")
    snps, cols = dosages.shape
    sub = cols // n
    part = snps // PARTS
    for start in range(0, snps, LANES):
        lanes = pl.ds(start, LANES)
        freq = allele[:, lanes].astype(jnp.float32) / (2.0 * called[:, lanes].astype(jnp.float32))
        scale = lax.rsqrt(2.0 * freq * (1.0 - freq))
        dose = dosages[lanes, :].astype(jnp.float32).T
        values = jnp.where(dose == 3.0, 0.0, (dose - 2.0 * freq) * scale).astype(jnp.bfloat16)
        own[:, lanes] = values
        h, rest = start // part, start % part
        for odd in range(2):
            other = jnp.clip(partners(z)[odd], 0, n - 1)
            ref = without[odd * PARTS + h]
            for q in range(n):
                slot = q - (q > other).astype(jnp.int32)

                @pl.when(q != other)
                def _(q=q, slot=slot, ref=ref):
                    rows = pl.ds(pl.multiple_of(slot * sub, sub), sub)
                    ref[rows, pl.ds(rest, LANES)] = values[q * sub : (q + 1) * sub]


def standardize(dosages, allele_counts, called_counts, n):
    snps, cols = dosages.shape
    sub = cols // n
    shapes = [jax.ShapeDtypeStruct((cols, snps), jnp.bfloat16)]
    shapes += [jax.ShapeDtypeStruct((cols - sub, snps // PARTS), jnp.bfloat16)] * (2 * PARTS)
    return pl.pallas_call(
        functools.partial(standardize_kernel, n),
        out_shape=shapes,
        compiler_params=pltpu.CompilerParams(vmem_limit_bytes=32 * 2**20),
        name="standardize",
    )(dosages, allele_counts[None], called_counts[None])


def multiply_kernel(n, wide, plan, keys, own, near, *refs):
    trades, panels = refs[: len(plan)], refs[len(plan) : len(plan) + wide]
    out, panel, block, tile, block_sem, panel_sem, out_sem = refs[len(plan) + wide :]
    z, w = lax.axis_index("narrow"), lax.axis_index("wide")
    cols, snps = own.shape
    sub = cols // n
    part = snps // PARTS

    def block_copies(act):
        def go(src, q, slab, h, width):
            rows = pl.ds(pl.multiple_of(q * sub, sub), sub)
            lanes = pl.ds(pl.multiple_of(slab * snps + h * part, LANES), width)
            act(pltpu.make_async_copy(src, block.at[rows, lanes], block_sem))

        for i in range(n):
            go(near.at[i], z, i, 0, snps)
        for q in range(n):
            pl.when(q != z)(lambda q=q: go(own.at[pl.ds(q * sub, sub), :], q, z, 0, snps))
        for ref, (odd, step, h) in zip(trades, plan):
            slab = slab_of(z, odd, step)
            other = partners(z)[odd]

            @pl.when((slab >= 0) & (slab < n) & (other >= 0) & (other < n))
            def _(ref=ref, slab=slab, h=h):
                for slot in range(n - 1):
                    go(ref.at[pl.ds(slot * sub, sub), :], slot + (slot >= z).astype(jnp.int32), slab, h, part)

    def panel_copies(t, act):
        for m in range(2):
            place = lax.rem(w ^ m, 2)
            rows = pl.ds(pl.multiple_of(place * sub, sub), sub)
            for i in range(n):
                act(pltpu.make_async_copy(
                    panels[2 * t + m].at[i], panel.at[t, rows, pl.ds(i * snps, snps)], panel_sem.at[t]))

    pairs = wide // 2
    block_copies(lambda copy: copy.start())
    for t in range(pairs):
        panel_copies(t, lambda copy: copy.start())
    block_copies(lambda copy: copy.wait())

    def out_copy(t):
        chip = (w ^ jnp.where(lax.rem(w, 2) == 0, *keys[t])) // 2
        rows = pl.ds(pl.multiple_of(chip * (2 * sub), 2 * sub), 2 * sub)
        return pltpu.make_async_copy(tile.at[t % 2], out.at[rows], out_sem.at[t % 2])

    for t in range(pairs):
        panel_copies(t, lambda copy: copy.wait())
        if t >= 2:
            out_copy(t - 2).wait()
        product = lax.dot_general(
            panel[t], block[...], (((1,), (1,)), ((), ())), preferred_element_type=jnp.float32
        )
        tile[t % 2] = product / (n * snps)
        out_copy(t).start()
    for t in range(max(pairs - 2, 0), pairs):
        out_copy(t).wait()


def multiply(own, near, trades, plan, panels, keys, n, wide):
    cols, snps = own.shape
    sub = cols // n
    return pl.pallas_call(
        functools.partial(multiply_kernel, n, wide, plan, keys),
        out_shape=jax.ShapeDtypeStruct((wide * sub, cols), jnp.float32),
        in_specs=[ANY] * (2 + len(trades) + len(panels)),
        out_specs=ANY,
        scratch_shapes=[
            pltpu.VMEM((wide // 2, 2 * sub, n * snps), jnp.bfloat16),
            pltpu.VMEM((cols, n * snps), jnp.bfloat16),
            pltpu.VMEM((2, 2 * sub, cols), jnp.float32),
            pltpu.SemaphoreType.DMA,
            pltpu.SemaphoreType.DMA((wide // 2,)),
            pltpu.SemaphoreType.DMA((2,)),
        ],
        compiler_params=pltpu.CompilerParams(vmem_limit_bytes=48 * 2**20),
        name="multiply",
    )(own, near, *trades, *panels)


def flip(value, masks):
    size = lax.axis_size("wide")
    return lax.ppermute(value, "wide", [(i, i ^ masks[i & 1]) for i in range(size)])


def spread(panel):
    size = lax.axis_size("wide")
    bits = [1 << b for b in range(1, size.bit_length() - 1)]
    got = {(0, 0): panel}
    for i in range(len(bits)):
        masks = (bits[i], bits[-1 - i])
        for key, value in list(got.items()):
            got[key[0] ^ masks[0], key[1] ^ masks[1]] = flip(value, masks)
    return got


def shards(dosages, allele_counts, called_counts):
    n, wide = lax.axis_size("narrow"), lax.axis_size("wide")
    z, w = lax.axis_index("narrow"), lax.axis_index("wide")
    snps, cols = dosages.shape
    sub = cols // n
    part = snps // PARTS
    own, *without = standardize(dosages, allele_counts, called_counts, n)
    near = lax.all_to_all(own.reshape(n, sub, snps), "narrow", 0, 0)

    def hand_on(value, odd, step, h):
        slab = jnp.clip(slab_of(z, odd, step), 0, n - 1)
        mine = lax.dynamic_slice(near, (slab, 0, h * part), (1, sub, part))[0]
        slot = jnp.clip(jnp.minimum(z, partners(z)[1 - odd]), 0, n - 2)
        return lax.dynamic_update_slice(value, mine, (slot * sub, 0))

    got = {}
    for step in range(1, n):
        for h in range(PARTS):
            for odd in range(2):
                if step == 1:
                    value = without[odd * PARTS + h]
                elif (1 - odd, step - 1, h) in got:
                    value = hand_on(got[1 - odd, step - 1, h], 1 - odd, step - 1, h)
                else:
                    continue
                value = trade(value, odd, step)
                if value is not None:
                    got[odd, step, h] = value
    plan = tuple(got)
    held = spread(near)
    partner = {key: flip(value, (1, 1)) for key, value in held.items()}
    keys = tuple(held)
    panels = [array for key in keys for array in (held[key], partner[key[::-1]])]
    result = multiply(own, near, [got[k] for k in plan], plan, panels, keys, n, wide)
    return result.reshape(wide, 1, sub, cols)


def solution(mesh):
    return jax.shard_map(
        shards,
        mesh=mesh,
        in_specs=(P("narrow", "wide"), P("narrow"), P("narrow")),
        out_specs=P(None, "narrow", None, "wide"),
        check_vma=False,
    )
```

time: 139 us -> 97.9 us (0.70)
  waiting for transfers between devices: 111 us -> 37.1 us
  blocking collectives: 0 us -> 26.2 us
  starting transfers between devices: 0.04 us -> 16.9 us
  between operations: 13.4 us -> 0.23 us
  Pallas kernels: 0 us -> 10.8 us
  matrix products: 9.54 us -> 0 us
  local copies, waits for them, and re-layouts: 3.99 us -> 6.3 us
    all_gather x2 -> x0, waiting for transfers between devices: 111 us -> none  [the longest x1 66.3 us: shards(): block_rows = lax.all_gather(standard, 'narrow', axis=0, tiled=True)]
    ppermute x0 -> x17, waiting for transfers between devices: none -> 37.1 us  [the longest x10 37.1 us: trade(): return lax.ppermute(value, 'narrow', pairs) if pairs else None]
    all_to_all x0 -> x1, blocking collectives: none -> 26.2 us  [shards(): near = lax.all_to_all(own.reshape(n, sub, snps), 'narrow', 0, 0)]
    ppermute x0 -> x17, starting transfers between devices: none -> 16.9 us  [the longest x10 9.87 us: trade(): return lax.ppermute(value, 'narrow', pairs) if pairs else None]
    pallas_call x0 -> x2, Pallas kernels: none -> 10.8 us  [the longest x1 9.08 us: multiply(): pl.pallas_call(functools.partial(multiply_kernel, n, wide, plan, keys), o...]
    dot_general x1 -> x0, matrix products: 9.54 us -> none  [shards(): lax.dot_general(gathered, block_rows, (((0,), (0,)), ((), ())), preferred...]
    unnamed x5 -> x18, local copies, waits for them, and re-layouts: 1.9 us -> 5.59 us
    dynamic_slice x1 -> x0, local copies, waits for them, and re-layouts: 2.09 us -> none  [shards(): panel = lax.dynamic_slice_in_dim(block_rows, position, sub_width, 1)]
  transfers between devices with their start and end apart: 2 -> 17, of which waited for: 2 -> 5; matrix products, arithmetic and copies ran while one was open for 0% -> 2% of each run, Pallas kernels for 0% -> 0%
where the time goes in v1:
time: 97.9 us; the launch traced here: 97.5 us
  waiting for transfers between devices  37.1 us (38%)
  blocking collectives  26.2 us (27%)
  starting transfers between devices  16.9 us (17%)
  Pallas kernels  10.8 us (11%)
  local copies, waits for them, and re-layouts  6.3 us (6%)
    ppermute x10, waiting for transfers between devices, trade(): return lax.ppermute(value, 'narrow', pairs) if pairs else None  37.1 us
    all_to_all x1, blocking collectives, shards(): near = lax.all_to_all(own.reshape(n, sub, snps), 'narrow', 0, 0)  26.2 us
    ppermute x10, starting transfers between devices, trade(): return lax.ppermute(value, 'narrow', pairs) if pairs else None  9.87 us
    pallas_call x1, Pallas kernels, multiply(): pl.pallas_call(functools.partial(multiply_kernel, n, wide, plan, keys), o...  9.08 us
    ppermute x7, starting transfers between devices, flip(): lax.ppermute(value, 'wide', [(i, i ^ masks[i & 1]) for i in range(size)])  7 us
    unnamed x18, local copies, waits for them, and re-layouts  5.59 us
  transfers between devices with their start and end apart: 17, of which 5 were waited for; matrix products, arithmetic and copies ran while one was open for 2% of the time, Pallas kernels for 0%

profile of v1, /device:TPU:0, one launch (start us, length us, event | category | flops | bytes accessed | tf_op | source)
XLA Modules:
  0.0 97.5 jit_solution(4220219659396064963)
XLA Ops:
  0.0 1.4 %copy-done = s32[512,768]{1,0:T(8,128)S(1)} copy-done((s32[512,768]{1,0:T(8,128)S(1)}, s32[512,768]{1,0:T(8,128)}, u32[]{:S(2)}) %copy-start) | copy-done | bytes 1572888
  1.4 0.7 copy-done.1
  2.1 0.7 copy-done.2
  2.8 1.7 %standardize.1 = (bf16[768,512]{1,0:T(8,128)(2,1)S(1)}, bf16[576,256]{1,0:T(8,128)(2,1)S(1)}, bf16[576,256]{1,0:T(8,128)(2,1)}, bf16[576,256]{1,0:T(8,128)(2,1)}, bf16[576,256]{1,0:T(8,128)(2,1)S(1)}) custom-call(s32[512,768]{1,0:T(8,128)S(1)} %copy-done, s32[1,512]{1,0:T(1,128)S(1)} %bitcast.19, s32[1,512]{1,0:T(1,128)S(1)} %bitcast.20), custom_call_target="tpu_custom_call" | custom-call | tf_op jit(solution)/shard_map/standardize/pallas_call | solution.py:66
  4.5 26.2 %all_to_all.5.near.refs_10_ = bf16[4,192,512]{2,1,0:T(8,128)(2,1)S(1)} all-to-all(bf16[4,192,512]{2,1,0:T(8,128)(2,1)S(1)} %bitcast.18), channel_id=1, replica_groups=mesh['wide'=8,'narrow'=4] {'narrow'}, dimensions={0} | all-to-all | bytes 1572864 | tf_op jit(solution)/shard_map/all_to_all | solution.py:177
  30.7 1.5 %collective-permute-start.11 = (bf16[4,192,512]{2,1,0:T(8,128)(2,1)S(1)}, bf16[4,192,512]{2,1,0:T(8,128)(2,1)}, u32[]{:S(2)}, u32[]{:S(2)}) collective-permute-start(bf16[4,192,512]{2,1,0:T(8,128)(2,1)S(1)} %all_to_all.5.near.refs_10_), channel_id=1, source_target_pairs={{0,8},{4,20},{8,0},{12,28},{16,24},{20,4},{24,16},{28,12},{1,9},{5... | collective-permute-start | bytes 2359304 | tf_op jit(solution)/shard_map/ppermute | solution.py:156
  32.2 0.2 collective-permute-start.2
  32.4 1.8 %collective-permute-start = (bf16[576,256]{1,0:T(8,128)(2,1)S(1)}, bf16[576,256]{1,0:T(8,128)(2,1)S(1)}, u32[]{:S(2)}, u32[]{:S(2)}) collective-permute-start(bf16[576,256]{1,0:T(8,128)(2,1)S(1)} %get-tuple-element.11), channel_id=1, source_target_pairs={{0,1},{1,0},{2,3},{3,2},{4,5},{5,4},{6,7},{7,6},{8,9},{9,8},{10,11... | collective-permute-start | bytes 884744 | tf_op jit(solution)/shard_map/ppermute | solution.py:28
  34.2 0.7 collective-permute-start.1
  34.9 0.7 collective-permute-start.3
  35.6 6.8 %collective-permute-done.2.refs_2_ = bf16[576,256]{1,0:T(8,128)(2,1)S(1)} collective-permute-done((bf16[576,256]{1,0:T(8,128)(2,1)}, bf16[576,256]{1,0:T(8,128)(2,1)S(1)}, u32[]{:S(2)}, u32[]{:S(2)}) %collective-permute-start.2) | collective-permute-done | bytes 294944 | tf_op jit(solution)/shard_map/ppermute | solution.py:28
  42.4 0.7 copy.5
  43.1 1.1 %collective-permute-start.12 = (bf16[4,192,512]{2,1,0:T(8,128)(2,1)S(1)}, bf16[4,192,512]{2,1,0:T(8,128)(2,1)}, u32[]{:S(2)}, u32[]{:S(2)}) collective-permute-start(bf16[4,192,512]{2,1,0:T(8,128)(2,1)S(1)} %all_to_all.5.near.refs_10_), channel_id=1, source_target_pairs={{0,16},{4,12},{8,24},{12,4},{16,0},{20,28},{24,8},{28,20},{1,17},{... | collective-permute-start | bytes 2359304 | tf_op jit(solution)/shard_map/ppermute | solution.py:156
  44.2 3.4 %collective-permute-start.15 = (bf16[4,192,512]{2,1,0:T(8,128)(2,1)}, bf16[4,192,512]{2,1,0:T(8,128)(2,1)}, u32[]{:S(2)}, u32[]{:S(2)}) collective-permute-start(bf16[4,192,512]{2,1,0:T(8,128)(2,1)} %collective-permute-done.11.refs_12_), channel_id=1, source_target_pairs={{0,16},{4,12},{8,24},{12,4},{16,0},{20,28},{24,8},{28,20},{1,17},{... | collective-permute-start | bytes 2359304 | tf_op jit(solution)/shard_map/ppermute | solution.py:156
  47.6 0.6 bitcast_dynamic-update-slice_fusion.2
  48.2 0.7 collective-permute-start.7
  49.1 1.3 %collective-permute-start.9 = (bf16[576,256]{1,0:T(8,128)(2,1)S(1)}, bf16[576,256]{1,0:T(8,128)(2,1)S(1)}, u32[]{:S(2)}, u32[]{:S(2)}) collective-permute-start(bf16[576,256]{1,0:T(8,128)(2,1)S(1)} %get-tuple-element.15), channel_id=1, source_target_pairs={{1,0},{2,3},{5,4},{6,7},{9,8},{10,11},{13,12},{14,15},{17,16},{18,... | collective-permute-start | bytes 884744 | tf_op jit(solution)/shard_map/ppermute | solution.py:28
  50.4 0.7 collective-permute-start.5
  51.1 1.3 %collective-permute-start.6 = (bf16[576,256]{1,0:T(8,128)(2,1)S(1)}, bf16[576,256]{1,0:T(8,128)(2,1)S(1)}, u32[]{:S(2)}, u32[]{:S(2)}) collective-permute-start(bf16[576,256]{1,0:T(8,128)(2,1)S(1)} %get-tuple-element.17), channel_id=1, source_target_pairs={{1,0},{2,3},{5,4},{6,7},{9,8},{10,11},{13,12},{14,15},{17,16},{18,... | collective-permute-start | bytes 884744 | tf_op jit(solution)/shard_map/ppermute | solution.py:28
  52.4 13.4 %collective-permute-done.9.refs_9_ = bf16[576,256]{1,0:T(8,128)(2,1)S(1)} collective-permute-done((bf16[576,256]{1,0:T(8,128)(2,1)S(1)}, bf16[576,256]{1,0:T(8,128)(2,1)S(1)}, u32[]{:S(2)}, u32[]{:S(2)}) %collective-permute-start.9) | collective-permute-done | bytes 294944 | tf_op jit(solution)/shard_map/ppermute | solution.py:28
  65.8 0.5 collective-permute-start.14
  66.3 0.1 collective-permute-start.13
  66.4 0.4 collective-permute-start.16
  66.8 2.4 %collective-permute-done.6.refs_6_ = bf16[576,256]{1,0:T(8,128)(2,1)S(1)} collective-permute-done((bf16[576,256]{1,0:T(8,128)(2,1)S(1)}, bf16[576,256]{1,0:T(8,128)(2,1)S(1)}, u32[]{:S(2)}, u32[]{:S(2)}) %collective-permute-start.6) | collective-permute-done | bytes 294944 | tf_op jit(solution)/shard_map/ppermute | solution.py:28
  69.2 1.3 %collective-permute-start.4 = (bf16[576,256]{1,0:T(8,128)(2,1)S(1)}, bf16[576,256]{1,0:T(8,128)(2,1)S(1)}, u32[]{:S(2)}, u32[]{:S(2)}) collective-permute-start(bf16[576,256]{1,0:T(8,128)(2,1)S(1)} %get-tuple-element.18), channel_id=1, source_target_pairs={{1,0},{2,3},{5,4},{6,7},{9,8},{10,11},{13,12},{14,15},{17,16},{18,... | collective-permute-start | bytes 884744 | tf_op jit(solution)/shard_map/ppermute | solution.py:28
  70.5 7.3 %collective-permute-done.4.refs_4_ = bf16[576,256]{1,0:T(8,128)(2,1)S(1)} collective-permute-done((bf16[576,256]{1,0:T(8,128)(2,1)S(1)}, bf16[576,256]{1,0:T(8,128)(2,1)S(1)}, u32[]{:S(2)}, u32[]{:S(2)}) %collective-permute-start.4) | collective-permute-done | bytes 294944 | tf_op jit(solution)/shard_map/ppermute | solution.py:28
  77.8 1.3 %collective-permute-start.8 = (bf16[576,256]{1,0:T(8,128)(2,1)S(1)}, bf16[576,256]{1,0:T(8,128)(2,1)S(1)}, u32[]{:S(2)}, u32[]{:S(2)}) collective-permute-start(bf16[576,256]{1,0:T(8,128)(2,1)S(1)} %bitcast_dynamic-update-slice_fusion.1), channel_id=1, source_target_pairs={{1,0},{2,3},{5,4},{6,7},{9,8},{10,11},{13,12},{14,15},{17,16},{18,... | collective-permute-start | bytes 884744 | tf_op jit(solution)/shard_map/ppermute | solution.py:28
  79.1 7.3 %collective-permute-done.8.refs_8_ = bf16[576,256]{1,0:T(8,128)(2,1)S(1)} collective-permute-done((bf16[576,256]{1,0:T(8,128)(2,1)S(1)}, bf16[576,256]{1,0:T(8,128)(2,1)S(1)}, u32[]{:S(2)}, u32[]{:S(2)}) %collective-permute-start.8) | collective-permute-done | bytes 294944 | tf_op jit(solution)/shard_map/ppermute | solution.py:28
  86.4 0.9 copy-done.4
  87.3 0.2 copy-done.3
  87.5 0.9 copy-done.5
  88.4 9.1 %multiply.1 = f32[1536,768]{1,0:T(8,128)} custom-call(bf16[768,512]{1,0:T(8,128)(2,1)S(1)} %get-tuple-element.10.own, bf16[4,192,512]{2,1,0:T(8,128)(2,1)S(1)} %all_to_all.5.near.refs_10_, bf16[576,256]{1,0:T(8,128)(2,1)S(1)} %collective-permute-done.refs_0_, bf16[576,256]{1,0:T(8,128)(2,1)S(1)} %collective-permute-done.1.refs_1_, ...), custom_call_target="tpu_custom_call" | custom-call | tf_op jit(solution)/shard_map/multiply/pallas_call | solution.py:136
  (26 shorter events, 0.2 us)
Async XLA Ops:
  0.0 1.4 %copy-start = (s32[512,768]{1,0:T(8,128)S(1)}, s32[512,768]{1,0:T(8,128)}, u32[]{:S(2)}) copy-start(s32[512,768]{1,0:T(8,128)} %dosages.1) | copy-start | bytes 4718596
  1.4 0.7 copy-start.1
  2.1 0.7 copy-start.2
  30.7 13.4 %collective-permute-start.11 = (bf16[4,192,512]{2,1,0:T(8,128)(2,1)S(1)}, bf16[4,192,512]{2,1,0:T(8,128)(2,1)}, u32[]{:S(2)}, u32[]{:S(2)}) collective-permute-start(bf16[4,192,512]{2,1,0:T(8,128)(2,1)S(1)} %all_to_all.5.near.refs_10_), channel_id=1, source_target_pairs={{0,8},{4,20},{8,0},{12,28},{16,24},{20,4},{24,16},{28,12},{1,9},{5... | collective-permute-start | bytes 2359304 | tf_op jit(solution)/shard_map/ppermute | solution.py:156
  32.2 10.2 %collective-permute-start.2 = (bf16[576,256]{1,0:T(8,128)(2,1)}, bf16[576,256]{1,0:T(8,128)(2,1)S(1)}, u32[]{:S(2)}, u32[]{:S(2)}) collective-permute-start(bf16[576,256]{1,0:T(8,128)(2,1)} %get-tuple-element.13), channel_id=1, source_target_pairs={{0,1},{1,0},{2,3},{3,2},{4,5},{5,4},{6,7},{7,6},{8,9},{9,8},{10,11... | collective-permute-start | bytes 884744 | tf_op jit(solution)/shard_map/ppermute | solution.py:28
  32.4 15.8 %collective-permute-start = (bf16[576,256]{1,0:T(8,128)(2,1)S(1)}, bf16[576,256]{1,0:T(8,128)(2,1)S(1)}, u32[]{:S(2)}, u32[]{:S(2)}) collective-permute-start(bf16[576,256]{1,0:T(8,128)(2,1)S(1)} %get-tuple-element.11), channel_id=1, source_target_pairs={{0,1},{1,0},{2,3},{3,2},{4,5},{5,4},{6,7},{7,6},{8,9},{9,8},{10,11... | collective-permute-start | bytes 884744 | tf_op jit(solution)/shard_map/ppermute | solution.py:28
  34.2 14.7 %collective-permute-start.1 = (bf16[576,256]{1,0:T(8,128)(2,1)}, bf16[576,256]{1,0:T(8,128)(2,1)S(1)}, u32[]{:S(2)}, u32[]{:S(2)}) collective-permute-start(bf16[576,256]{1,0:T(8,128)(2,1)} %get-tuple-element.12), channel_id=1, source_target_pairs={{1,2},{2,1},{5,6},{6,5},{9,10},{10,9},{13,14},{14,13},{17,18},{18,... | collective-permute-start | bytes 884744 | tf_op jit(solution)/shard_map/ppermute | solution.py:28
  34.9 14.1 %collective-permute-start.3 = (bf16[576,256]{1,0:T(8,128)(2,1)S(1)}, bf16[576,256]{1,0:T(8,128)(2,1)S(1)}, u32[]{:S(2)}, u32[]{:S(2)}) collective-permute-start(bf16[576,256]{1,0:T(8,128)(2,1)S(1)} %get-tuple-element.14), channel_id=1, source_target_pairs={{1,2},{2,1},{5,6},{6,5},{9,10},{10,9},{13,14},{14,13},{17,18},{18,... | collective-permute-start | bytes 884744 | tf_op jit(solution)/shard_map/ppermute | solution.py:28
  43.1 23.2 %collective-permute-start.12 = (bf16[4,192,512]{2,1,0:T(8,128)(2,1)S(1)}, bf16[4,192,512]{2,1,0:T(8,128)(2,1)}, u32[]{:S(2)}, u32[]{:S(2)}) collective-permute-start(bf16[4,192,512]{2,1,0:T(8,128)(2,1)S(1)} %all_to_all.5.near.refs_10_), channel_id=1, source_target_pairs={{0,16},{4,12},{8,24},{12,4},{16,0},{20,28},{24,8},{28,20},{1,17},{... | collective-permute-start | bytes 2359304 | tf_op jit(solution)/shard_map/ppermute | solution.py:156
  44.2 22.2 %collective-permute-start.15 = (bf16[4,192,512]{2,1,0:T(8,128)(2,1)}, bf16[4,192,512]{2,1,0:T(8,128)(2,1)}, u32[]{:S(2)}, u32[]{:S(2)}) collective-permute-start(bf16[4,192,512]{2,1,0:T(8,128)(2,1)} %collective-permute-done.11.refs_12_), channel_id=1, source_target_pairs={{0,16},{4,12},{8,24},{12,4},{16,0},{20,28},{24,8},{28,20},{1,17},{... | collective-permute-start | bytes 2359304 | tf_op jit(solution)/shard_map/ppermute | solution.py:156
  48.2 0.8 collective-permute-start.7
  49.1 16.7 %collective-permute-start.9 = (bf16[576,256]{1,0:T(8,128)(2,1)S(1)}, bf16[576,256]{1,0:T(8,128)(2,1)S(1)}, u32[]{:S(2)}, u32[]{:S(2)}) collective-permute-start(bf16[576,256]{1,0:T(8,128)(2,1)S(1)} %get-tuple-element.15), channel_id=1, source_target_pairs={{1,0},{2,3},{5,4},{6,7},{9,8},{10,11},{13,12},{14,15},{17,16},{18,... | collective-permute-start | bytes 884744 | tf_op jit(solution)/shard_map/ppermute | solution.py:28
  50.4 15.4 %collective-permute-start.5 = (bf16[576,256]{1,0:T(8,128)(2,1)S(1)}, bf16[576,256]{1,0:T(8,128)(2,1)S(1)}, u32[]{:S(2)}, u32[]{:S(2)}) collective-permute-start(bf16[576,256]{1,0:T(8,128)(2,1)S(1)} %get-tuple-element.16), channel_id=1, source_target_pairs={{1,2},{2,1},{5,6},{6,5},{9,10},{10,9},{13,14},{14,13},{17,18},{18,... | collective-permute-start | bytes 884744 | tf_op jit(solution)/shard_map/ppermute | solution.py:28
  51.1 18.1 %collective-permute-start.6 = (bf16[576,256]{1,0:T(8,128)(2,1)S(1)}, bf16[576,256]{1,0:T(8,128)(2,1)S(1)}, u32[]{:S(2)}, u32[]{:S(2)}) collective-permute-start(bf16[576,256]{1,0:T(8,128)(2,1)S(1)} %get-tuple-element.17), channel_id=1, source_target_pairs={{1,0},{2,3},{5,4},{6,7},{9,8},{10,11},{13,12},{14,15},{17,16},{18,... | collective-permute-start | bytes 884744 | tf_op jit(solution)/shard_map/ppermute | solution.py:28
  65.8 13.3 %collective-permute-start.10 = (bf16[4,192,512]{2,1,0:T(8,128)(2,1)S(1)}, bf16[4,192,512]{2,1,0:T(8,128)(2,1)S(1)}, u32[]{:S(2)}, u32[]{:S(2)}) collective-permute-start(bf16[4,192,512]{2,1,0:T(8,128)(2,1)S(1)} %all_to_all.5.near.refs_10_), channel_id=1, source_target_pairs={{0,4},{4,0},{8,12},{12,8},{16,20},{20,16},{24,28},{28,24},{1,5},{5... | collective-permute-start | bytes 2359304 | tf_op jit(solution)/shard_map/ppermute | solution.py:156
  65.8 20.6 %collective-permute-start.14 = (bf16[4,192,512]{2,1,0:T(8,128)(2,1)}, bf16[4,192,512]{2,1,0:T(8,128)(2,1)S(1)}, u32[]{:S(2)}, u32[]{:S(2)}) collective-permute-start(bf16[4,192,512]{2,1,0:T(8,128)(2,1)} %collective-permute-done.11.refs_12_), channel_id=1, source_target_pairs={{0,4},{4,0},{8,12},{12,8},{16,20},{20,16},{24,28},{28,24},{1,5},{5... | collective-permute-start | bytes 2359304 | tf_op jit(solution)/shard_map/ppermute | solution.py:156
  66.3 20.1 %collective-permute-start.13 = (bf16[4,192,512]{2,1,0:T(8,128)(2,1)}, bf16[4,192,512]{2,1,0:T(8,128)(2,1)S(1)}, u32[]{:S(2)}, u32[]{:S(2)}) collective-permute-start(bf16[4,192,512]{2,1,0:T(8,128)(2,1)} %collective-permute-done.12.refs_14_), channel_id=1, source_target_pairs={{0,4},{4,0},{8,12},{12,8},{16,20},{20,16},{24,28},{28,24},{1,5},{5... | collective-permute-start | bytes 2359304 | tf_op jit(solution)/shard_map/ppermute | solution.py:156
  66.4 20.0 %collective-permute-start.16 = (bf16[4,192,512]{2,1,0:T(8,128)(2,1)}, bf16[4,192,512]{2,1,0:T(8,128)(2,1)S(1)}, u32[]{:S(2)}, u32[]{:S(2)}) collective-permute-start(bf16[4,192,512]{2,1,0:T(8,128)(2,1)} %collective-permute-done.15.refs_16_), channel_id=1, source_target_pairs={{0,4},{4,0},{8,12},{12,8},{16,20},{20,16},{24,28},{28,24},{1,5},{5... | collective-permute-start | bytes 2359304 | tf_op jit(solution)/shard_map/ppermute | solution.py:156
  69.2 8.6 %collective-permute-start.4 = (bf16[576,256]{1,0:T(8,128)(2,1)S(1)}, bf16[576,256]{1,0:T(8,128)(2,1)S(1)}, u32[]{:S(2)}, u32[]{:S(2)}) collective-permute-start(bf16[576,256]{1,0:T(8,128)(2,1)S(1)} %get-tuple-element.18), channel_id=1, source_target_pairs={{1,0},{2,3},{5,4},{6,7},{9,8},{10,11},{13,12},{14,15},{17,16},{18,... | collective-permute-start | bytes 884744 | tf_op jit(solution)/shard_map/ppermute | solution.py:28
  77.8 8.6 %collective-permute-start.8 = (bf16[576,256]{1,0:T(8,128)(2,1)S(1)}, bf16[576,256]{1,0:T(8,128)(2,1)S(1)}, u32[]{:S(2)}, u32[]{:S(2)}) collective-permute-start(bf16[576,256]{1,0:T(8,128)(2,1)S(1)} %bitcast_dynamic-update-slice_fusion.1), channel_id=1, source_target_pairs={{1,0},{2,3},{5,4},{6,7},{9,8},{10,11},{13,12},{14,15},{17,16},{18,... | collective-permute-start | bytes 884744 | tf_op jit(solution)/shard_map/ppermute | solution.py:28
  86.4 0.9 copy-start.4
  86.4 1.1 %copy-start.3 = (bf16[4,192,512]{2,1,0:T(8,128)(2,1)}, bf16[4,192,512]{2,1,0:T(8,128)(2,1)S(1)}, u32[]{:S(2)}) copy-start(bf16[4,192,512]{2,1,0:T(8,128)(2,1)S(1)} %collective-permute-done.14.refs_15_) | copy-start | bytes 2359300
  87.5 0.9 copy-start.5

commit v2 on v0

v2 whole, which is shorter than its diff:
```python
import functools
import math

import jax
import jax.numpy as jnp
from jax import lax
from jax.experimental import pallas as pl
from jax.experimental.pallas import tpu as pltpu
from jax.sharding import PartitionSpec as P

LANES = 128
HOP = 6_000_000_000
STACK = 0
EARLY = 6_000_000_000
ANY = pl.BlockSpec(memory_space=pl.ANY)
VMEM = pl.BlockSpec(memory_space=pltpu.VMEM)


def trade(value, swapped, step):
    n, wide = lax.axis_size("narrow"), lax.axis_size("wide")
    pairs = []
    for w in range(wide):
        for low in range((w + swapped) % 2, n - 1, 2):
            if low + 1 - step >= 0:
                pairs.append((w * n + low, w * n + low + 1))
            if low + step <= n - 1:
                pairs.append((w * n + low + 1, w * n + low))
    return lax.ppermute(value, ("wide", "narrow"), pairs)


def side_of(swapped):
    return lax.rem(lax.axis_index("wide") + swapped, 2)


def partner_on(z, odd):
    side = lax.rem(z + odd, 2)
    return z + 1 - 2 * side


def swap(value, mask):
    n = lax.axis_size("narrow")
    return lax.ppermute(value, "narrow", [(i, i ^ mask) for i in range(n)])


def slab_of(z, odd, step):
    side = lax.rem(z + odd, 2)
    return z + step * (1 - 2 * side)


def standardize_kernel(n, dosages_ref, allele_ref, called_ref, own, *refs):
    hops, panels, (dosages, allele, called, sem) = refs[:2], refs[2 : n + 1], refs[n + 1 :]
    z = lax.axis_index("narrow")
    snps, cols = dosages.shape
    sub = cols // n
    counts = [
        pltpu.make_async_copy(allele_ref, allele, sem.at[0]),
        pltpu.make_async_copy(called_ref, called, sem.at[1]),
    ]
    starts = range(0, snps, LANES)
    doses = [
        pltpu.make_async_copy(dosages_ref.at[pl.ds(start, LANES), :], dosages.at[pl.ds(start, LANES), :], sem.at[2 + i])
        for i, start in enumerate(starts)
    ]
    for copy in counts + doses:
        copy.start()
    for copy in counts:
        copy.wait()

    def put(values, ref, start, other):
        for q in range(n):
            slot = q - (q > other).astype(jnp.int32)

            @pl.when(q != other)
            def _():
                rows = pl.ds(pl.multiple_of(slot * sub, sub), sub)
                ref[rows, pl.ds(start, LANES)] = values[q * sub : (q + 1) * sub]

    for i, start in enumerate(starts):
        doses[i].wait()
        lanes = pl.ds(start, LANES)
        freq = allele[:, lanes].astype(jnp.float32) / (2.0 * called[:, lanes].astype(jnp.float32))
        scale = lax.rsqrt(2.0 * freq * (1.0 - freq))
        dose = dosages[lanes, :].astype(jnp.float32).T
        values = jnp.where(dose == 3.0, 0.0, (dose - 2.0 * freq) * scale).astype(jnp.bfloat16)
        own[:, lanes] = values
        for swapped, ref in enumerate(hops):
            put(values, ref, start, jnp.clip(partner_on(z, side_of(swapped)), 0, n - 1))
    for m, ref in enumerate(panels, 1):
        ref[...] = own[pl.ds(pl.multiple_of((z ^ m) * sub, sub), sub), :]


def standardize(dosages, allele_counts, called_counts, n):
    snps, cols = dosages.shape
    sub = cols // n
    shapes = [(cols, snps)] + [(cols - sub, snps)] * 2 + [(sub, snps)] * (n - 1)
    outs = pl.pallas_call(
        functools.partial(standardize_kernel, n),
        out_shape=[jax.ShapeDtypeStruct(shape, jnp.bfloat16) for shape in shapes],
        in_specs=[pl.BlockSpec(memory_space=pltpu.HBM)] * 3,
        scratch_shapes=[
            pltpu.VMEM((snps, cols), jnp.int32),
            pltpu.VMEM((1, snps), jnp.int32),
            pltpu.VMEM((1, snps), jnp.int32),
            pltpu.SemaphoreType.DMA((2 + snps // LANES,)),
        ],
        compiler_params=pltpu.CompilerParams(vmem_limit_bytes=60 * 2**20),
        name="standardize",
    )(dosages, allele_counts[None], called_counts[None])
    return outs[0], outs[1:3], outs[3:]


def stack_kernel(n, own, *refs):
    pieces, out = refs[: n - 1], refs[n - 1]
    z = lax.axis_index("narrow")
    sub = own.shape[0] // n
    out[z] = own[pl.ds(pl.multiple_of(z * sub, sub), sub), :]
    for m, piece in enumerate(pieces, 1):
        out[z ^ m] = piece[...]


def stack(own, pieces):
    n = len(pieces) + 1
    return pl.pallas_call(
        functools.partial(stack_kernel, n),
        out_shape=jax.ShapeDtypeStruct((n, own.shape[0] // n, own.shape[1]), own.dtype),
        compiler_params=pltpu.CompilerParams(vmem_limit_bytes=8 * 2**20),
        cost_estimate=pl.CostEstimate(flops=STACK, bytes_accessed=0, transcendentals=0),
        name="stack",
    )(own, *pieces)


def hand_on_kernel(n, step, first, second, near, *outs):
    z, sub = lax.axis_index("narrow"), near.shape[1]
    for swapped, value, out in ((1, second, outs[0]), (0, first, outs[1])):
        odd = side_of(swapped)
        slab = jnp.clip(slab_of(z, odd, step), 0, n - 1)
        to = jnp.clip(jnp.minimum(z, partner_on(z, 1 - odd)), 0, n - 2)
        out[...] = value[...]
        out[pl.ds(pl.multiple_of(to * sub, sub), sub), :] = near[slab]


def hand_on(first, second, near, step):
    n = near.shape[0]
    return pl.pallas_call(
        functools.partial(hand_on_kernel, n, step),
        out_shape=[jax.ShapeDtypeStruct(first.shape, first.dtype)] * 2,
        compiler_params=pltpu.CompilerParams(vmem_limit_bytes=12 * 2**20),
        cost_estimate=pl.CostEstimate(flops=HOP, bytes_accessed=0, transcendentals=0),
        name="hand_on",
    )(first, second, near)


def last_slab(z, n):
    return jnp.where(z < n // 2, n - 1, 0)


def block_copies(n, plan, own, near, trades, z, go):
    sub = near.shape[1]
    for i in range(n):
        go(near.at[i], z, i)
    if own is not None:
        for q in range(n):
            pl.when(q != z)(lambda q=q: go(own.at[pl.ds(q * sub, sub), :], q, z))
    for ref, (swapped, step) in zip(trades, plan):
        slab, other = slab_of(z, side_of(swapped), step), partner_on(z, side_of(swapped))

        @pl.when((slab >= 0) & (slab < n) & (other >= 0) & (other < n))
        def _(ref=ref, slab=slab):
            for slot in range(n - 1):
                go(ref.at[pl.ds(slot * sub, sub), :], slot + (slot >= z).astype(jnp.int32), slab)


def panel_rows(m, w, sub):
    return pl.ds(pl.multiple_of((m // 2 * 2 + (w + m) % 2) * sub, sub), sub)


def early_kernel(n, plan, own, near, *refs):
    trades, (*panels, out, rest, block, panel, tile, out_sem) = refs[: len(plan)], refs[len(plan) :]
    z, w = lax.axis_index("narrow"), lax.axis_index("wide")
    cols, snps = own.shape
    sub = cols // n
    last = last_slab(z, n)

    def place(slab):
        index = slab - (slab > last).astype(jnp.int32)
        return pl.ds(pl.multiple_of(index * snps, snps), snps)

    def go(src, q, slab):
        @pl.when(slab != last)
        def _():
            block[pl.ds(pl.multiple_of(q * sub, sub), sub), place(slab)] = src[...]

    block_copies(n, plan, own, near, trades, z, go)
    for m, ref in enumerate(panels):
        rows = panel_rows(m, w, sub)
        rest[rows, :] = ref[last]
        for i in range(n):

            @pl.when(i != last)
            def _(i=i, ref=ref, rows=rows):
                panel[rows, place(i)] = ref[i]

    width = tile.shape[2]
    outs = [
        pltpu.make_async_copy(tile.at[i % 2], out.at[:, pl.ds(start, width)], out_sem.at[i % 2])
        for i, start in enumerate(range(0, cols, width))
    ]
    for i, copy in enumerate(outs):
        if i >= 2:
            outs[i - 2].wait()
        tile[i % 2] = lax.dot_general(
            panel[...], block[pl.ds(i * width, width), :], (((1,), (1,)), ((), ())), preferred_element_type=jnp.float32
        )
        copy.start()
    for copy in outs[-2:]:
        copy.wait()


def late_kernel(n, plan, keys, near, early, rest, begun, first, second, *refs):
    trades, (out, block, panel, tile, out_sem) = refs[: len(plan)], refs[len(plan) :]
    z, w = lax.axis_index("narrow"), lax.axis_index("wide")
    cols, snps = block.shape
    sub = cols // n
    last = last_slab(z, n)
    dims = (((1,), (1,)), ((), ()))

    def out_copy(t):
        chip = (w ^ jnp.where(lax.rem(w, 2) == 0, *keys[t])) // 2
        rows = pl.ds(pl.multiple_of(chip * (2 * sub), 2 * sub), 2 * sub)
        return pltpu.make_async_copy(tile.at[t % 2], out.at[rows], out_sem.at[t % 2])

    def go(src, q, slab):
        @pl.when(slab == last)
        def _():
            block[pl.ds(pl.multiple_of(q * sub, sub), sub), :] = src[...]

    for m, ref in enumerate((first, second)):
        rows = panel_rows(m, w, sub)
        panel[rows, pl.ds((n - 1) * snps, snps)] = ref[last]
        for i in range(n):

            @pl.when(i != last)
            def _(i=i, ref=ref, rows=rows):
                index = i - (i > last).astype(jnp.int32)
                panel[rows, pl.ds(pl.multiple_of(index * snps, snps), snps)] = ref[i]

    block_copies(n, plan, None, near, trades, z, go)
    order = [len(keys) - 1, *range(len(keys) - 1)]
    for i, t in enumerate(order):
        if i >= 2:
            out_copy(order[i - 2]).wait()
        if i == 0:
            before = lax.dot_general(
                panel[:, : (n - 1) * snps], begun[...], dims, preferred_element_type=jnp.float32
            )
            left = panel[:, (n - 1) * snps :]
        else:
            rows = pl.ds(t * 2 * sub, 2 * sub)
            before, left = early[rows, :], rest[rows, :]
        product = lax.dot_general(left, block[...], dims, preferred_element_type=jnp.float32)
        tile[t % 2] = (before + product) / (n * snps)
        out_copy(t).start()
    for t in order[-2:]:
        out_copy(t).wait()


def limit(arrays):
    return min(sum(math.prod(a.shape) * a.dtype.itemsize for a in arrays) + 4 * 2**20, 60 * 2**20)


def multiply(own, near, got, panels, keys):
    n, sub, snps = near.shape
    rows, cols = (len(panels) - 2) * sub, own.shape[0]
    plan = tuple(key for key in got if key[1] < n - 1)
    width = 256 if cols % 256 == 0 else cols
    scratch = [
        pltpu.VMEM((rows, (n - 1) * snps), jnp.bfloat16),
        pltpu.VMEM((2, rows, width), jnp.float32),
    ]
    operands = [own, near, *[got[key] for key in plan], *panels[:-2]]
    outs = [
        jax.ShapeDtypeStruct((rows, cols), jnp.float32),
        jax.ShapeDtypeStruct((rows, snps), jnp.bfloat16),
        jax.ShapeDtypeStruct((cols, (n - 1) * snps), jnp.bfloat16),
    ]
    early = pl.pallas_call(
        functools.partial(early_kernel, n, plan),
        out_shape=outs,
        in_specs=[VMEM] * len(operands),
        out_specs=[ANY, VMEM, VMEM],
        scratch_shapes=scratch + [pltpu.SemaphoreType.DMA((2,))],
        compiler_params=pltpu.CompilerParams(vmem_limit_bytes=limit([*operands, *scratch, *outs[1:]])),
        cost_estimate=pl.CostEstimate(flops=EARLY, bytes_accessed=0, transcendentals=0),
        name="early",
    )(*operands)
    plan = tuple(key for key in got if key[1] >= n // 2)
    operands = [near, *early, *panels[-2:], *[got[key] for key in plan]]
    scratch = [
        pltpu.VMEM((cols, snps), jnp.bfloat16),
        pltpu.VMEM((2 * sub, n * snps), jnp.bfloat16),
        pltpu.VMEM((2, 2 * sub, cols), jnp.float32),
    ]
    return pl.pallas_call(
        functools.partial(late_kernel, n, plan, keys),
        out_shape=jax.ShapeDtypeStruct((len(panels) * sub, cols), jnp.float32),
        in_specs=[VMEM] * len(operands),
        out_specs=ANY,
        scratch_shapes=scratch + [pltpu.SemaphoreType.DMA((2,))],
        compiler_params=pltpu.CompilerParams(vmem_limit_bytes=limit([*operands, *scratch])),
        name="late",
    )(*operands)


def after(value, *earlier):
    return lax.optimization_barrier((value, *earlier))[0]


def flip(value, masks):
    size = lax.axis_size("wide")
    return lax.ppermute(value, "wide", [(i, i ^ masks[i & 1]) for i in range(size)])


def spread(panel):
    size = lax.axis_size("wide")
    bits = [1 << b for b in range(1, size.bit_length() - 1)]
    got = {(0, 0): panel}
    for i in range(len(bits)):
        masks = (bits[i], bits[-1 - i])
        for key, value in list(got.items()):
            got[key[0] ^ masks[0], key[1] ^ masks[1]] = flip(value, masks)
    return got


def shards(dosages, allele_counts, called_counts):
    n, wide = lax.axis_size("narrow"), lax.axis_size("wide")
    z, w = lax.axis_index("narrow"), lax.axis_index("wide")
    snps, cols = dosages.shape
    sub = cols // n
    own, hops, panels = standardize(dosages, allele_counts, called_counts, n)
    pieces = [swap(value, m) for m, value in enumerate(panels, 1)]
    near = stack(own, pieces)
    got = {(swapped, 1): trade(value, swapped, 1) for swapped, value in enumerate(hops)}
    for step in range(2, n):
        values = hand_on(got[0, step - 1], got[1, step - 1], near, step - 1)
        for swapped, value in enumerate(values):
            got[swapped, step] = trade(value, swapped, step)
    held = spread(near)
    partner = {key: flip(value, (1, 1)) for key, value in held.items()}
    keys = tuple(held)
    panels = [array for key in keys for array in (held[key], partner[key[::-1]])]
    result = multiply(own, near, got, panels, keys)
    return result.reshape(wide, 1, sub, cols)


def solution(mesh):
    return jax.shard_map(
        shards,
        mesh=mesh,
        in_specs=(P("narrow", "wide"), P("narrow"), P("narrow")),
        out_specs=P(None, "narrow", None, "wide"),
        check_vma=False,
    )
```

time: 139 us -> 86.8 us (0.62)
  waiting for transfers between devices: 111 us -> 46.3 us
  starting transfers between devices: 0.04 us -> 23.1 us
  Pallas kernels: 0 us -> 15.3 us
  between operations: 13.4 us -> 0.13 us
  matrix products: 9.54 us -> 0 us
  local copies, waits for them, and re-layouts: 3.99 us -> 1.14 us
    all_gather x2 -> x0, waiting for transfers between devices: 111 us -> none  [the longest x1 66.3 us: shards(): block_rows = lax.all_gather(standard, 'narrow', axis=0, tiled=True)]
    ppermute x0 -> x16, waiting for transfers between devices: none -> 46.3 us  [the longest x6 27.4 us: trade(): return lax.ppermute(value, ('wide', 'narrow'), pairs)]
    ppermute x0 -> x16, starting transfers between devices: none -> 23.1 us  [the longest x6 10 us: trade(): return lax.ppermute(value, ('wide', 'narrow'), pairs)]
    pallas_call x0 -> x6, Pallas kernels: none -> 15.3 us  [the longest x1 6.22 us: multiply(): pl.pallas_call(functools.partial(early_kernel, n, plan), out_shape=outs,...]
    dot_general x1 -> x0, matrix products: 9.54 us -> none  [shards(): lax.dot_general(gathered, block_rows, (((0,), (0,)), ((), ())), preferred...]
    dynamic_slice x1 -> x0, local copies, waits for them, and re-layouts: 2.09 us -> none  [shards(): panel = lax.dynamic_slice_in_dim(block_rows, position, sub_width, 1)]
  transfers between devices with their start and end apart: 2 -> 16, of which waited for: 2 -> 6; matrix products, arithmetic and copies ran while one was open for 0% -> 0% of each run, Pallas kernels for 0% -> 7%
where the time goes in v2:
time: 86.8 us; the launch traced here: 85.9 us
  waiting for transfers between devices  46.3 us (53%)
  starting transfers between devices  23.1 us (27%)
  Pallas kernels  15.3 us (18%)
  local copies, waits for them, and re-layouts  1.14 us (1%)
    ppermute x6, waiting for transfers between devices, trade(): return lax.ppermute(value, ('wide', 'narrow'), pairs)  27.4 us
    ppermute x3, waiting for transfers between devices, swap(): return lax.ppermute(value, 'narrow', [(i, i ^ mask) for i in range(n)])  14.8 us
    ppermute x6, starting transfers between devices, trade(): return lax.ppermute(value, ('wide', 'narrow'), pairs)  10 us
    ppermute x7, starting transfers between devices, flip(): lax.ppermute(value, 'wide', [(i, i ^ masks[i & 1]) for i in range(size)])  7.38 us
    pallas_call x1, Pallas kernels, multiply(): pl.pallas_call(functools.partial(early_kernel, n, plan), out_shape=outs,...  6.22 us
    ppermute x3, starting transfers between devices, swap(): return lax.ppermute(value, 'narrow', [(i, i ^ mask) for i in range(n)])  5.67 us
    pallas_call x1, Pallas kernels, multiply(): pl.pallas_call(functools.partial(late_kernel, n, plan, keys), out_shape=j...  5.29 us
    ppermute x7, waiting for transfers between devices, flip(): lax.ppermute(value, 'wide', [(i, i ^ masks[i & 1]) for i in range(size)])  4.15 us
  transfers between devices with their start and end apart: 16, of which 6 were waited for; matrix products, arithmetic and copies ran while one was open for 0% of the time, Pallas kernels for 7%

profile of v2, /device:TPU:0, one launch (start us, length us, event | category | flops | bytes accessed | tf_op | source)
XLA Modules:
  0.0 85.9 jit_solution(11795140550427429238)
XLA Ops:
  0.0 3.5 %standardize.1 = (bf16[768,512]{1,0:T(8,128)(2,1)}, bf16[576,512]{1,0:T(8,128)(2,1)}, bf16[576,512]{1,0:T(8,128)(2,1)}, bf16[192,512]{1,0:T(8,128)(2,1)}, bf16[1...) custom-call(s32[512,768]{1,0:T(8,128)} %dosages_ref.1, s32[1,512]{1,0:T(1,128)} %bitcast.5, s32[1,512]{1,0:T(1,128)} %bitcast.6), custom_call_target="tpu_custom_call" | custom-call | tf_op jit(solution)/shard_map/standardize/pallas_call | solution.py:96
  3.5 3.1 %collective-permute-start = (bf16[192,512]{1,0:T(8,128)(2,1)}, bf16[192,512]{1,0:T(8,128)(2,1)S(1)}, u32[]{:S(2)}, u32[]{:S(2)}) collective-permute-start(bf16[192,512]{1,0:T(8,128)(2,1)} %get-tuple-element.19), channel_id=1, source_target_pairs={{0,1},{1,0},{2,3},{3,2},{4,5},{5,4},{6,7},{7,6},{8,9},{9,8},{10,11... | collective-permute-start | bytes 589832 | tf_op jit(solution)/shard_map/ppermute | solution.py:42
  6.6 2.6 %collective-permute-start.1 = (bf16[192,512]{1,0:T(8,128)(2,1)}, bf16[192,512]{1,0:T(8,128)(2,1)S(1)}, u32[]{:S(2)}, u32[]{:S(2)}) collective-permute-start(bf16[192,512]{1,0:T(8,128)(2,1)} %get-tuple-element.20), channel_id=1, source_target_pairs={{0,2},{1,3},{2,0},{3,1},{4,6},{5,7},{6,4},{7,5},{8,10},{9,11},{10,... | collective-permute-start | bytes 589832 | tf_op jit(solution)/shard_map/ppermute | solution.py:42
  9.2 0.0 collective-permute-start.2
  9.2 6.0 %collective-permute-done.refs_0_ = bf16[192,512]{1,0:T(8,128)(2,1)S(1)} collective-permute-done((bf16[192,512]{1,0:T(8,128)(2,1)}, bf16[192,512]{1,0:T(8,128)(2,1)S(1)}, u32[]{:S(2)}, u32[]{:S(2)}) %collective-permute-start) | collective-permute-done | bytes 196640 | tf_op jit(solution)/shard_map/ppermute | solution.py:42
  15.1 8.8 %collective-permute-done.1.refs_1_ = bf16[192,512]{1,0:T(8,128)(2,1)S(1)} collective-permute-done((bf16[192,512]{1,0:T(8,128)(2,1)}, bf16[192,512]{1,0:T(8,128)(2,1)S(1)}, u32[]{:S(2)}, u32[]{:S(2)}) %collective-permute-start.1) | collective-permute-done | bytes 196640 | tf_op jit(solution)/shard_map/ppermute | solution.py:42
  24.0 0.0 collective-permute-done.2.refs_2_
  24.0 1.1 %copy-done = bf16[768,512]{1,0:T(8,128)(2,1)S(1)} copy-done((bf16[768,512]{1,0:T(8,128)(2,1)S(1)}, bf16[768,512]{1,0:T(8,128)(2,1)}, u32[]{:S(2)}) %copy-start) | copy-done | bytes 786456
  25.1 0.1 stack.1.near.refs_4_
  25.2 1.6 %collective-permute-start.8 = (bf16[4,192,512]{2,1,0:T(8,128)(2,1)S(1)}, bf16[4,192,512]{2,1,0:T(8,128)(2,1)S(1)}, u32[]{:S(2)}, u32[]{:S(2)}) collective-permute-start(bf16[4,192,512]{2,1,0:T(8,128)(2,1)S(1)} %stack.1.near.refs_4_), channel_id=1, source_target_pairs={{0,8},{4,20},{8,0},{12,28},{16,24},{20,4},{24,16},{28,12},{1,9},{5... | collective-permute-start | bytes 2359304 | tf_op jit(solution)/shard_map/ppermute | solution.py:320
  26.7 5.2 %collective-permute-start.3 = (bf16[576,512]{1,0:T(8,128)(2,1)}, bf16[576,512]{1,0:T(8,128)(2,1)S(1)}, u32[]{:S(2)}, u32[]{:S(2)}) collective-permute-start(bf16[576,512]{1,0:T(8,128)(2,1)} %get-tuple-element.22), channel_id=1, source_target_pairs={{0,1},{1,0},{2,3},{3,2},{5,6},{6,5},{8,9},{9,8},{10,11},{11,10},{1... | collective-permute-start | bytes 1769480 | tf_op jit(solution)/shard_map/ppermute | solution.py:28
  32.0 0.7 collective-permute-start.4
  32.7 1.6 %collective-permute-start.9 = (bf16[4,192,512]{2,1,0:T(8,128)(2,1)S(1)}, bf16[4,192,512]{2,1,0:T(8,128)(2,1)S(1)}, u32[]{:S(2)}, u32[]{:S(2)}) collective-permute-start(bf16[4,192,512]{2,1,0:T(8,128)(2,1)S(1)} %stack.1.near.refs_4_), channel_id=1, source_target_pairs={{0,16},{4,12},{8,24},{12,4},{16,0},{20,28},{24,8},{28,20},{1,17},{... | collective-permute-start | bytes 2359304 | tf_op jit(solution)/shard_map/ppermute | solution.py:320
  34.3 4.1 %collective-permute-done.8.refs_6_ = bf16[4,192,512]{2,1,0:T(8,128)(2,1)S(1)} collective-permute-done((bf16[4,192,512]{2,1,0:T(8,128)(2,1)S(1)}, bf16[4,192,512]{2,1,0:T(8,128)(2,1)S(1)}, u32[]{:S(2)}, u32[]{:S(2)}) %collective-permute-start.8) | collective-permute-done | bytes 786464 | tf_op jit(solution)/shard_map/ppermute | solution.py:320
  38.4 2.5 %collective-permute-start.12 = (bf16[4,192,512]{2,1,0:T(8,128)(2,1)S(1)}, bf16[4,192,512]{2,1,0:T(8,128)(2,1)S(1)}, u32[]{:S(2)}, u32[]{:S(2)}) collective-permute-start(bf16[4,192,512]{2,1,0:T(8,128)(2,1)S(1)} %collective-permute-done.8.refs_6_), channel_id=1, source_target_pairs={{0,16},{4,12},{8,24},{12,4},{16,0},{20,28},{24,8},{28,20},{1,17},{... | collective-permute-start | bytes 2359304 | tf_op jit(solution)/shard_map/ppermute | solution.py:320
  40.9 4.5 %collective-permute-done.3.first.refs_0_ = bf16[576,512]{1,0:T(8,128)(2,1)S(1)} collective-permute-done((bf16[576,512]{1,0:T(8,128)(2,1)}, bf16[576,512]{1,0:T(8,128)(2,1)S(1)}, u32[]{:S(2)}, u32[]{:S(2)}) %collective-permute-start.3) | collective-permute-done | bytes 589856 | tf_op jit(solution)/shard_map/ppermute | solution.py:28
  45.4 0.1 hand_on.2
  45.5 1.3 %collective-permute-start.5 = (bf16[576,512]{1,0:T(8,128)(2,1)S(1)}, bf16[576,512]{1,0:T(8,128)(2,1)S(1)}, u32[]{:S(2)}, u32[]{:S(2)}) collective-permute-start(bf16[576,512]{1,0:T(8,128)(2,1)S(1)} %get-tuple-element.24), channel_id=1, source_target_pairs={{1,0},{2,3},{5,6},{6,5},{9,8},{10,11},{13,14},{14,13},{17,16},{18,... | collective-permute-start | bytes 1769480 | tf_op jit(solution)/shard_map/ppermute | solution.py:28
  46.8 0.0 copy-start.1
  46.8 0.8 collective-permute-start.6
  47.7 1.1 %collective-permute-start.7 = (bf16[4,192,512]{2,1,0:T(8,128)(2,1)S(1)}, bf16[4,192,512]{2,1,0:T(8,128)(2,1)S(1)}, u32[]{:S(2)}, u32[]{:S(2)}) collective-permute-start(bf16[4,192,512]{2,1,0:T(8,128)(2,1)S(1)} %stack.1.near.refs_4_), channel_id=1, source_target_pairs={{0,4},{4,0},{8,12},{12,8},{16,20},{20,16},{24,28},{28,24},{1,5},{5... | collective-permute-start | bytes 2359304 | tf_op jit(solution)/shard_map/ppermute | solution.py:320
  48.8 0.0 collective-permute-done.9.refs_8_
  48.8 0.1 collective-permute-start.11
  48.9 12.4 %collective-permute-done.5.refs_2_.first.refs_0_ = bf16[576,512]{1,0:T(8,128)(2,1)S(1)} collective-permute-done((bf16[576,512]{1,0:T(8,128)(2,1)S(1)}, bf16[576,512]{1,0:T(8,128)(2,1)S(1)}, u32[]{:S(2)}, u32[]{:S(2)}) %collective-permute-start.5) | collective-permute-done | bytes 589856 | tf_op jit(solution)/shard_map/ppermute | solution.py:28
  61.3 0.0 collective-permute-start.10
  61.3 0.5 collective-permute-start.13
  61.8 0.1 hand_on.3
  61.9 1.3 %collective-permute-start.14 = (bf16[576,512]{1,0:T(8,128)(2,1)S(1)}, bf16[576,512]{1,0:T(8,128)(2,1)S(1)}, u32[]{:S(2)}, u32[]{:S(2)}) collective-permute-start(bf16[576,512]{1,0:T(8,128)(2,1)S(1)} %get-tuple-element.29), channel_id=1, source_target_pairs={{1,0},{2,3},{9,8},{10,11},{17,16},{18,19},{25,24},{26,27}} | collective-permute-start | bytes 1769480 | tf_op jit(solution)/shard_map/ppermute | solution.py:28
  63.2 0.7 collective-permute-start.15
  64.0 6.2 %early.1 = (f32[1152,768]{1,0:T(8,128)S(1)}, bf16[1152,512]{1,0:T(8,128)(2,1)S(1)}, bf16[768,1536]{1,0:T(8,128)(2,1)S(1)}) custom-call(bf16[768,512]{1,0:T(8,128)(2,1)S(1)} %copy-done.1, bf16[4,192,512]{2,1,0:T(8,128)(2,1)S(1)} %stack.1.near.refs_4_, bf16[576,512]{1,0:T(8,128)(2,1)S(1)} %collective-permute-done.3.first.refs_0_, ...), custom_call_target="tpu_custom_call" | custom-call | flops 6000000000 | tf_op jit(solution)/shard_map/early/pallas_call | solution.py:286
  70.2 10.5 %collective-permute-done.14.refs_2_ = bf16[576,512]{1,0:T(8,128)(2,1)S(1)} collective-permute-done((bf16[576,512]{1,0:T(8,128)(2,1)S(1)}, bf16[576,512]{1,0:T(8,128)(2,1)S(1)}, u32[]{:S(2)}, u32[]{:S(2)}) %collective-permute-start.14) | collective-permute-done | bytes 589856 | tf_op jit(solution)/shard_map/ppermute | solution.py:28
  80.6 5.3 %late.1 = f32[1536,768]{1,0:T(8,128)} custom-call(bf16[4,192,512]{2,1,0:T(8,128)(2,1)S(1)} %stack.1.near.refs_4_, f32[1152,768]{1,0:T(8,128)S(1)} %get-tuple-element.26.early, bf16[1152,512]{1,0:T(8,128)(2,1)S(1)} %get-tuple-element.27.rest, bf16[768,1536]{1,0:T(8,128)(2,1)S(1)} %get-tuple-element.28.begun, ...), custom_call_target="tpu_custom_call" | custom-call | tf_op jit(solution)/shard_map/late/pallas_call | solution.py:303
  (10 shorter events, 0.0 us)
Async XLA Ops:
  3.5 11.6 %collective-permute-start = (bf16[192,512]{1,0:T(8,128)(2,1)}, bf16[192,512]{1,0:T(8,128)(2,1)S(1)}, u32[]{:S(2)}, u32[]{:S(2)}) collective-permute-start(bf16[192,512]{1,0:T(8,128)(2,1)} %get-tuple-element.19), channel_id=1, source_target_pairs={{0,1},{1,0},{2,3},{3,2},{4,5},{5,4},{6,7},{7,6},{8,9},{9,8},{10,11... | collective-permute-start | bytes 589832 | tf_op jit(solution)/shard_map/ppermute | solution.py:42
  6.6 17.4 %collective-permute-start.1 = (bf16[192,512]{1,0:T(8,128)(2,1)}, bf16[192,512]{1,0:T(8,128)(2,1)S(1)}, u32[]{:S(2)}, u32[]{:S(2)}) collective-permute-start(bf16[192,512]{1,0:T(8,128)(2,1)} %get-tuple-element.20), channel_id=1, source_target_pairs={{0,2},{1,3},{2,0},{3,1},{4,6},{5,7},{6,4},{7,5},{8,10},{9,11},{10,... | collective-permute-start | bytes 589832 | tf_op jit(solution)/shard_map/ppermute | solution.py:42
  9.2 14.8 %collective-permute-start.2 = (bf16[192,512]{1,0:T(8,128)(2,1)}, bf16[192,512]{1,0:T(8,128)(2,1)S(1)}, u32[]{:S(2)}, u32[]{:S(2)}) collective-permute-start(bf16[192,512]{1,0:T(8,128)(2,1)} %get-tuple-element.21), channel_id=1, source_target_pairs={{0,3},{1,2},{2,1},{3,0},{4,7},{5,6},{6,5},{7,4},{8,11},{9,10},{10,... | collective-permute-start | bytes 589832 | tf_op jit(solution)/shard_map/ppermute | solution.py:42
  24.0 1.1 %copy-start = (bf16[768,512]{1,0:T(8,128)(2,1)S(1)}, bf16[768,512]{1,0:T(8,128)(2,1)}, u32[]{:S(2)}) copy-start(bf16[768,512]{1,0:T(8,128)(2,1)} %get-tuple-element.18.own) | copy-start | bytes 2359300
  25.2 13.2 %collective-permute-start.8 = (bf16[4,192,512]{2,1,0:T(8,128)(2,1)S(1)}, bf16[4,192,512]{2,1,0:T(8,128)(2,1)S(1)}, u32[]{:S(2)}, u32[]{:S(2)}) collective-permute-start(bf16[4,192,512]{2,1,0:T(8,128)(2,1)S(1)} %stack.1.near.refs_4_), channel_id=1, source_target_pairs={{0,8},{4,20},{8,0},{12,28},{16,24},{20,4},{24,16},{28,12},{1,9},{5... | collective-permute-start | bytes 2359304 | tf_op jit(solution)/shard_map/ppermute | solution.py:320
  26.7 18.7 %collective-permute-start.3 = (bf16[576,512]{1,0:T(8,128)(2,1)}, bf16[576,512]{1,0:T(8,128)(2,1)S(1)}, u32[]{:S(2)}, u32[]{:S(2)}) collective-permute-start(bf16[576,512]{1,0:T(8,128)(2,1)} %get-tuple-element.22), channel_id=1, source_target_pairs={{0,1},{1,0},{2,3},{3,2},{5,6},{6,5},{8,9},{9,8},{10,11},{11,10},{1... | collective-permute-start | bytes 1769480 | tf_op jit(solution)/shard_map/ppermute | solution.py:28
  32.0 13.4 %collective-permute-start.4 = (bf16[576,512]{1,0:T(8,128)(2,1)}, bf16[576,512]{1,0:T(8,128)(2,1)S(1)}, u32[]{:S(2)}, u32[]{:S(2)}) collective-permute-start(bf16[576,512]{1,0:T(8,128)(2,1)} %get-tuple-element.23), channel_id=1, source_target_pairs={{1,2},{2,1},{4,5},{5,4},{6,7},{7,6},{9,10},{10,9},{12,13},{13,12},... | collective-permute-start | bytes 1769480 | tf_op jit(solution)/shard_map/ppermute | solution.py:28
  32.7 16.1 %collective-permute-start.9 = (bf16[4,192,512]{2,1,0:T(8,128)(2,1)S(1)}, bf16[4,192,512]{2,1,0:T(8,128)(2,1)S(1)}, u32[]{:S(2)}, u32[]{:S(2)}) collective-permute-start(bf16[4,192,512]{2,1,0:T(8,128)(2,1)S(1)} %stack.1.near.refs_4_), channel_id=1, source_target_pairs={{0,16},{4,12},{8,24},{12,4},{16,0},{20,28},{24,8},{28,20},{1,17},{... | collective-permute-start | bytes 2359304 | tf_op jit(solution)/shard_map/ppermute | solution.py:320
  38.4 22.9 %collective-permute-start.12 = (bf16[4,192,512]{2,1,0:T(8,128)(2,1)S(1)}, bf16[4,192,512]{2,1,0:T(8,128)(2,1)S(1)}, u32[]{:S(2)}, u32[]{:S(2)}) collective-permute-start(bf16[4,192,512]{2,1,0:T(8,128)(2,1)S(1)} %collective-permute-done.8.refs_6_), channel_id=1, source_target_pairs={{0,16},{4,12},{8,24},{12,4},{16,0},{20,28},{24,8},{28,20},{1,17},{... | collective-permute-start | bytes 2359304 | tf_op jit(solution)/shard_map/ppermute | solution.py:320
  45.5 15.8 %collective-permute-start.5 = (bf16[576,512]{1,0:T(8,128)(2,1)S(1)}, bf16[576,512]{1,0:T(8,128)(2,1)S(1)}, u32[]{:S(2)}, u32[]{:S(2)}) collective-permute-start(bf16[576,512]{1,0:T(8,128)(2,1)S(1)} %get-tuple-element.24), channel_id=1, source_target_pairs={{1,0},{2,3},{5,6},{6,5},{9,8},{10,11},{13,14},{14,13},{17,16},{18,... | collective-permute-start | bytes 1769480 | tf_op jit(solution)/shard_map/ppermute | solution.py:28
  46.8 17.1 %copy-start.1 = (bf16[768,512]{1,0:T(8,128)(2,1)S(1)}, bf16[768,512]{1,0:T(8,128)(2,1)}, u32[]{:S(2)}) copy-start(bf16[768,512]{1,0:T(8,128)(2,1)} %get-tuple-element.18.own) | copy-start | bytes 2359300
  46.8 15.0 %collective-permute-start.6 = (bf16[576,512]{1,0:T(8,128)(2,1)S(1)}, bf16[576,512]{1,0:T(8,128)(2,1)S(1)}, u32[]{:S(2)}, u32[]{:S(2)}) collective-permute-start(bf16[576,512]{1,0:T(8,128)(2,1)S(1)} %get-tuple-element.25), channel_id=1, source_target_pairs={{1,2},{2,1},{5,4},{6,7},{9,10},{10,9},{13,12},{14,15},{17,18},{18,... | collective-permute-start | bytes 1769480 | tf_op jit(solution)/shard_map/ppermute | solution.py:28
  47.7 15.5 %collective-permute-start.7 = (bf16[4,192,512]{2,1,0:T(8,128)(2,1)S(1)}, bf16[4,192,512]{2,1,0:T(8,128)(2,1)S(1)}, u32[]{:S(2)}, u32[]{:S(2)}) collective-permute-start(bf16[4,192,512]{2,1,0:T(8,128)(2,1)S(1)} %stack.1.near.refs_4_), channel_id=1, source_target_pairs={{0,4},{4,0},{8,12},{12,8},{16,20},{20,16},{24,28},{28,24},{1,5},{5... | collective-permute-start | bytes 2359304 | tf_op jit(solution)/shard_map/ppermute | solution.py:320
  48.8 15.1 %collective-permute-start.11 = (bf16[4,192,512]{2,1,0:T(8,128)(2,1)S(1)}, bf16[4,192,512]{2,1,0:T(8,128)(2,1)S(1)}, u32[]{:S(2)}, u32[]{:S(2)}) collective-permute-start(bf16[4,192,512]{2,1,0:T(8,128)(2,1)S(1)} %collective-permute-done.8.refs_6_), channel_id=1, source_target_pairs={{0,4},{4,0},{8,12},{12,8},{16,20},{20,16},{24,28},{28,24},{1,5},{5... | collective-permute-start | bytes 2359304 | tf_op jit(solution)/shard_map/ppermute | solution.py:320
  61.3 2.7 %collective-permute-start.10 = (bf16[4,192,512]{2,1,0:T(8,128)(2,1)S(1)}, bf16[4,192,512]{2,1,0:T(8,128)(2,1)S(1)}, u32[]{:S(2)}, u32[]{:S(2)}) collective-permute-start(bf16[4,192,512]{2,1,0:T(8,128)(2,1)S(1)} %collective-permute-done.9.refs_8_), channel_id=1, source_target_pairs={{0,4},{4,0},{8,12},{12,8},{16,20},{20,16},{24,28},{28,24},{1,5},{5... | collective-permute-start | bytes 2359304 | tf_op jit(solution)/shard_map/ppermute | solution.py:320
  61.3 19.4 %collective-permute-start.13 = (bf16[4,192,512]{2,1,0:T(8,128)(2,1)S(1)}, bf16[4,192,512]{2,1,0:T(8,128)(2,1)S(1)}, u32[]{:S(2)}, u32[]{:S(2)}) collective-permute-start(bf16[4,192,512]{2,1,0:T(8,128)(2,1)S(1)} %collective-permute-done.12.first), channel_id=1, source_target_pairs={{0,4},{4,0},{8,12},{12,8},{16,20},{20,16},{24,28},{28,24},{1,5},{5... | collective-permute-start | bytes 2359304 | tf_op jit(solution)/shard_map/ppermute | solution.py:320
  61.9 18.7 %collective-permute-start.14 = (bf16[576,512]{1,0:T(8,128)(2,1)S(1)}, bf16[576,512]{1,0:T(8,128)(2,1)S(1)}, u32[]{:S(2)}, u32[]{:S(2)}) collective-permute-start(bf16[576,512]{1,0:T(8,128)(2,1)S(1)} %get-tuple-element.29), channel_id=1, source_target_pairs={{1,0},{2,3},{9,8},{10,11},{17,16},{18,19},{25,24},{26,27}} | collective-permute-start | bytes 1769480 | tf_op jit(solution)/shard_map/ppermute | solution.py:28
  63.2 17.4 %collective-permute-start.15 = (bf16[576,512]{1,0:T(8,128)(2,1)S(1)}, bf16[576,512]{1,0:T(8,128)(2,1)S(1)}, u32[]{:S(2)}, u32[]{:S(2)}) collective-permute-start(bf16[576,512]{1,0:T(8,128)(2,1)S(1)} %get-tuple-element.30), channel_id=1, source_target_pairs={{5,4},{6,7},{13,12},{14,15},{21,20},{22,23},{29,28},{30,31}} | collective-permute-start | bytes 1769480 | tf_op jit(solution)/shard_map/ppermute | solution.py:28

commit v3 on v2

--- a/solution.py
+++ b/solution.py
@@ -9,11 +9,12 @@
 from jax.sharding import PartitionSpec as P
 
 LANES = 128
-HOP = 6_000_000_000
-STACK = 0
-EARLY = 6_000_000_000
+HOP = 20_000_000_000
+PACE = 10_000_000_000
+EARLY = 12_000_000_000
 ANY = pl.BlockSpec(memory_space=pl.ANY)
 VMEM = pl.BlockSpec(memory_space=pltpu.VMEM)
+HBM = pl.BlockSpec(memory_space=pltpu.HBM)
 
 
 def trade(value, swapped, step):
@@ -37,9 +38,9 @@
     return z + 1 - 2 * side
 
 
-def swap(value, mask):
-    n = lax.axis_size("narrow")
-    return lax.ppermute(value, "narrow", [(i, i ^ mask) for i in range(n)])
+def far_swap(value, mask):
+    pairs = [(i, i ^ mask) for i in range(lax.axis_size("narrow"))]
+    return lax.ppermute(value, "narrow", [(i, j) for i, j in pairs if abs(i - j) > 1])
 
 
 def slab_of(z, odd, step):
@@ -48,7 +49,7 @@
 
 
 def standardize_kernel(n, dosages_ref, allele_ref, called_ref, own, *refs):
-    hops, panels, (dosages, allele, called, sem) = refs[:2], refs[2 : n + 1], refs[n + 1 :]
+    panels, (dosages, allele, called, sem) = refs[: n - 2], refs[n - 2 :]
     z = lax.axis_index("narrow")
     snps, cols = dosages.shape
     sub = cols // n
@@ -65,15 +66,6 @@
         copy.start()
     for copy in counts:
         copy.wait()
-
-    def put(values, ref, start, other):
-        for q in range(n):
-            slot = q - (q > other).astype(jnp.int32)
-
-            @pl.when(q != other)
-            def _():
-                rows = pl.ds(pl.multiple_of(slot * sub, sub), sub)
-                ref[rows, pl.ds(start, LANES)] = values[q * sub : (q + 1) * sub]
 
     for i, start in enumerate(starts):
         doses[i].wait()
@@ -83,16 +75,14 @@
         dose = dosages[lanes, :].astype(jnp.float32).T
         values = jnp.where(dose == 3.0, 0.0, (dose - 2.0 * freq) * scale).astype(jnp.bfloat16)
         own[:, lanes] = values
-        for swapped, ref in enumerate(hops):
-            put(values, ref, start, jnp.clip(partner_on(z, side_of(swapped)), 0, n - 1))
-    for m, ref in enumerate(panels, 1):
+    for m, ref in enumerate(panels, 2):
         ref[...] = own[pl.ds(pl.multiple_of((z ^ m) * sub, sub), sub), :]
 
 
 def standardize(dosages, allele_counts, called_counts, n):
     snps, cols = dosages.shape
     sub = cols // n
-    shapes = [(cols, snps)] + [(cols - sub, snps)] * 2 + [(sub, snps)] * (n - 1)
+    shapes = [(cols, snps)] + [(sub, snps)] * (n - 2)
     outs = pl.pallas_call(
         functools.partial(standardize_kernel, n),
         out_shape=[jax.ShapeDtypeStruct(shape, jnp.bfloat16) for shape in shapes],
@@ -106,44 +96,87 @@
         compiler_params=pltpu.CompilerParams(vmem_limit_bytes=60 * 2**20),
         name="standardize",
     )(dosages, allele_counts[None], called_counts[None])
-    return outs[0], outs[1:3], outs[3:]
-
-
-def stack_kernel(n, own, *refs):
-    pieces, out = refs[: n - 1], refs[n - 1]
+    return outs[0], outs[1:]
+
+
+def pick_kernel(own, out, sem):
+    sub = out.shape[0]
+    rows = pl.ds(pl.multiple_of(lax.axis_index("narrow") * sub, sub), sub)
+    copy = pltpu.make_async_copy(own.at[rows, :], out, sem)
+    copy.start()
+    copy.wait()
+
+
+def pick(own, sub):
+    return pl.pallas_call(
+        pick_kernel,
+        out_shape=jax.ShapeDtypeStruct((sub, own.shape[1]), own.dtype),
+        in_specs=[ANY],
+        out_specs=VMEM,
+        scratch_shapes=[pltpu.SemaphoreType.DMA],
+        name="pick",
+    )(own)
+
+
+def stack_kernel(n, mine, first, second, *refs):
+    pieces, out, sem = refs[: n - 2], refs[n - 2], refs[n - 1]
     z = lax.axis_index("narrow")
-    sub = own.shape[0] // n
-    out[z] = own[pl.ds(pl.multiple_of(z * sub, sub), sub), :]
-    for m, piece in enumerate(pieces, 1):
-        out[z ^ m] = piece[...]
-
-
-def stack(own, pieces):
-    n = len(pieces) + 1
+    sub = out.shape[1]
+    rows = pl.ds(pl.multiple_of(z * sub, sub), sub)
+
+    def hops(act):
+        for swapped, value in enumerate((first, second)):
+            other = partner_on(z, side_of(swapped))
+
+            @pl.when((other >= 0) & (other < n))
+            def _(swapped=swapped, value=value, other=other):
+                act(pltpu.make_async_copy(value.at[rows, :], out.at[other], sem.at[swapped]))
+
+    hops(lambda copy: copy.start())
+    out[z] = mine[...]
+    for m, piece in enumerate(pieces, 2):
+
+        @pl.when(jnp.abs((z ^ m) - z) > 1)
+        def _(m=m, piece=piece):
+            out[z ^ m] = piece[...]
+
+    hops(lambda copy: copy.wait())
+
+
+def stack(mine, first, second, pieces):
+    n = len(pieces) + 2
     return pl.pallas_call(
         functools.partial(stack_kernel, n),
-        out_shape=jax.ShapeDtypeStruct((n, own.shape[0] // n, own.shape[1]), own.dtype),
-        compiler_params=pltpu.CompilerParams(vmem_limit_bytes=8 * 2**20),
-        cost_estimate=pl.CostEstimate(flops=STACK, bytes_accessed=0, transcendentals=0),
+        out_shape=jax.ShapeDtypeStruct((n, *mine.shape), mine.dtype),
+        in_specs=[VMEM, ANY, ANY] + [VMEM] * (n - 2),
+        out_specs=VMEM,
+        scratch_shapes=[pltpu.SemaphoreType.DMA((2,))],
+        compiler_params=pltpu.CompilerParams(vmem_limit_bytes=10 * 2**20),
         name="stack",
-    )(own, *pieces)
+    )(mine, first, second, *pieces)
 
 
 def hand_on_kernel(n, step, first, second, near, *outs):
     z, sub = lax.axis_index("narrow"), near.shape[1]
     for swapped, value, out in ((1, second, outs[0]), (0, first, outs[1])):
         odd = side_of(swapped)
-        slab = jnp.clip(slab_of(z, odd, step), 0, n - 1)
-        to = jnp.clip(jnp.minimum(z, partner_on(z, 1 - odd)), 0, n - 2)
-        out[...] = value[...]
-        out[pl.ds(pl.multiple_of(to * sub, sub), sub), :] = near[slab]
+        to = jnp.clip(partner_on(z, 1 - odd), 0, n - 1)
+        if step == 1:
+            for slot in range(n - 1):
+                q = slot + (slot >= to).astype(jnp.int32)
+                out[pl.ds(slot * sub, sub), :] = value[pl.ds(pl.multiple_of(q * sub, sub), sub), :]
+        else:
+            out[...] = value[...]
+            slab = jnp.clip(slab_of(z, odd, step), 0, n - 1)
+            slot = jnp.minimum(jnp.minimum(z, to), n - 2)
+            out[pl.ds(pl.multiple_of(slot * sub, sub), sub), :] = near[slab]
 
 
 def hand_on(first, second, near, step):
-    n = near.shape[0]
+    n, sub, snps = near.shape
     return pl.pallas_call(
         functools.partial(hand_on_kernel, n, step),
-        out_shape=[jax.ShapeDtypeStruct(first.shape, first.dtype)] * 2,
+        out_shape=[jax.ShapeDtypeStruct(((n - 1) * sub, snps), first.dtype)] * 2,
         compiler_params=pltpu.CompilerParams(vmem_limit_bytes=12 * 2**20),
         cost_estimate=pl.CostEstimate(flops=HOP, bytes_accessed=0, transcendentals=0),
         name="hand_on",
@@ -154,20 +187,21 @@
     return jnp.where(z < n // 2, n - 1, 0)
 
 
-def block_copies(n, plan, own, near, trades, z, go):
+def block_copies(n, plan, near, trades, z, go):
     sub = near.shape[1]
     for i in range(n):
         go(near.at[i], z, i)
-    if own is not None:
-        for q in range(n):
-            pl.when(q != z)(lambda q=q: go(own.at[pl.ds(q * sub, sub), :], q, z))
     for ref, (swapped, step) in zip(trades, plan):
         slab, other = slab_of(z, side_of(swapped), step), partner_on(z, side_of(swapped))
 
         @pl.when((slab >= 0) & (slab < n) & (other >= 0) & (other < n))
-        def _(ref=ref, slab=slab):
-            for slot in range(n - 1):
-                go(ref.at[pl.ds(slot * sub, sub), :], slot + (slot >= z).astype(jnp.int32), slab)
+        def _(ref=ref, slab=slab, step=step):
+            if step == 1:
+                for q in range(n):
+                    pl.when(q != z)(lambda q=q: go(ref.at[pl.ds(q * sub, sub), :], q, slab))
+            else:
+                for slot in range(n - 1):
+                    go(ref.at[pl.ds(slot * sub, sub), :], slot + (slot >= z).astype(jnp.int32), slab)
 
 
 def panel_rows(m, w, sub):
@@ -175,7 +209,7 @@
 
 
 def early_kernel(n, plan, own, near, *refs):
-    trades, (*panels, out, rest, block, panel, tile, out_sem) = refs[: len(plan)], refs[len(plan) :]
+    trades, (*panels, out, rest, block, panel, tile, own_sem, out_sem) = refs[: len(plan)], refs[len(plan) :]
     z, w = lax.axis_index("narrow"), lax.axis_index("wide")
     cols, snps = own.shape
     sub = cols // n
@@ -190,7 +224,16 @@
         def _():
             block[pl.ds(pl.multiple_of(q * sub, sub), sub), place(slab)] = src[...]
 
-    block_copies(n, plan, own, near, trades, z, go)
+    def own_copies(act):
+        for q in range(n):
+            rows = pl.ds(q * sub, sub)
+
+            @pl.when(q != z)
+            def _(rows=rows):
+                act(pltpu.make_async_copy(own.at[rows, :], block.at[rows, place(z)], own_sem))
+
+    own_copies(lambda copy: copy.start())
+    block_copies(n, plan, near, trades, z, go)
     for m, ref in enumerate(panels):
         rows = panel_rows(m, w, sub)
         rest[rows, :] = ref[last]
@@ -200,6 +243,7 @@
             def _(i=i, ref=ref, rows=rows):
                 panel[rows, place(i)] = ref[i]
 
+    own_copies(lambda copy: copy.wait())
     width = tile.shape[2]
     outs = [
         pltpu.make_async_copy(tile.at[i % 2], out.at[:, pl.ds(start, width)], out_sem.at[i % 2])
@@ -216,8 +260,20 @@
         copy.wait()
 
 
-def late_kernel(n, plan, keys, near, early, rest, begun, first, second, *refs):
-    trades, (out, block, panel, tile, out_sem) = refs[: len(plan)], refs[len(plan) :]
+def last_block_kernel(n, plan, near, *refs):
+    trades, block = refs[:-1], refs[-1]
+    z, sub = lax.axis_index("narrow"), near.shape[1]
+    last = last_slab(z, n)
+
+    def go(src, q, slab):
+        @pl.when(slab == last)
+        def _():
+            block[pl.ds(pl.multiple_of(q * sub, sub), sub), :] = src[...]
+
+    block_copies(n, plan, near, trades, z, go)
+
+
+def late_kernel(n, keys, block, early, rest, begun, first, second, out, panel, tile, out_sem):
     z, w = lax.axis_index("narrow"), lax.axis_index("wide")
     cols, snps = block.shape
     sub = cols // n
@@ -229,11 +285,6 @@
         rows = pl.ds(pl.multiple_of(chip * (2 * sub), 2 * sub), 2 * sub)
         return pltpu.make_async_copy(tile.at[t % 2], out.at[rows], out_sem.at[t % 2])
 
-    def go(src, q, slab):
-        @pl.when(slab == last)
-        def _():
-            block[pl.ds(pl.multiple_of(q * sub, sub), sub), :] = src[...]
-
     for m, ref in enumerate((first, second)):
         rows = panel_rows(m, w, sub)
         panel[rows, pl.ds((n - 1) * snps, snps)] = ref[last]
@@ -244,7 +295,6 @@
                 index = i - (i > last).astype(jnp.int32)
                 panel[rows, pl.ds(pl.multiple_of(index * snps, snps), snps)] = ref[i]
 
-    block_copies(n, plan, None, near, trades, z, go)
     order = [len(keys) - 1, *range(len(keys) - 1)]
     for i, t in enumerate(order):
         if i >= 2:
@@ -286,22 +336,29 @@
     early = pl.pallas_call(
         functools.partial(early_kernel, n, plan),
         out_shape=outs,
-        in_specs=[VMEM] * len(operands),
+        in_specs=[HBM] + [VMEM] * (len(operands) - 1),
         out_specs=[ANY, VMEM, VMEM],
-        scratch_shapes=scratch + [pltpu.SemaphoreType.DMA((2,))],
-        compiler_params=pltpu.CompilerParams(vmem_limit_bytes=limit([*operands, *scratch, *outs[1:]])),
+        scratch_shapes=scratch + [pltpu.SemaphoreType.DMA, pltpu.SemaphoreType.DMA((2,))],
+        compiler_params=pltpu.CompilerParams(vmem_limit_bytes=limit([*operands[1:], *scratch, *outs[1:]])),
         cost_estimate=pl.CostEstimate(flops=EARLY, bytes_accessed=0, transcendentals=0),
         name="early",
     )(*operands)
     plan = tuple(key for key in got if key[1] >= n // 2)
-    operands = [near, *early, *panels[-2:], *[got[key] for key in plan]]
+    operands = [after(near, early[1]), *[got[key] for key in plan]]
+    block = pl.pallas_call(
+        functools.partial(last_block_kernel, n, plan),
+        out_shape=jax.ShapeDtypeStruct((cols, snps), jnp.bfloat16),
+        compiler_params=pltpu.CompilerParams(vmem_limit_bytes=limit(operands)),
+        cost_estimate=pl.CostEstimate(flops=PACE, bytes_accessed=0, transcendentals=0),
+        name="last_block",
+    )(*operands)
+    operands = [block, *early, *panels[-2:]]
     scratch = [
-        pltpu.VMEM((cols, snps), jnp.bfloat16),
         pltpu.VMEM((2 * sub, n * snps), jnp.bfloat16),
         pltpu.VMEM((2, 2 * sub, cols), jnp.float32),
     ]
     return pl.pallas_call(
-        functools.partial(late_kernel, n, plan, keys),
+        functools.partial(late_kernel, n, keys),
         out_shape=jax.ShapeDtypeStruct((len(panels) * sub, cols), jnp.float32),
         in_specs=[VMEM] * len(operands),
         out_specs=ANY,
@@ -320,13 +377,15 @@
     return lax.ppermute(value, "wide", [(i, i ^ masks[i & 1]) for i in range(size)])
 
 
-def spread(panel):
+def spread(panel, earlier):
     size = lax.axis_size("wide")
     bits = [1 << b for b in range(1, size.bit_length() - 1)]
     got = {(0, 0): panel}
     for i in range(len(bits)):
         masks = (bits[i], bits[-1 - i])
         for key, value in list(got.items()):
+            if any(key):
+                value = after(value, *earlier)
             got[key[0] ^ masks[0], key[1] ^ masks[1]] = flip(value, masks)
     return got
 
@@ -336,15 +395,18 @@
     z, w = lax.axis_index("narrow"), lax.axis_index("wide")
     snps, cols = dosages.shape
     sub = cols // n
-    own, hops, panels = standardize(dosages, allele_counts, called_counts, n)
-    pieces = [swap(value, m) for m, value in enumerate(panels, 1)]
-    near = stack(own, pieces)
-    got = {(swapped, 1): trade(value, swapped, 1) for swapped, value in enumerate(hops)}
+    own, panels = standardize(dosages, allele_counts, called_counts, n)
+    got = {(swapped, 1): trade(own, swapped, 1) for swapped in range(2)}
+    mine = pick(own, sub)
+    pieces = [far_swap(after(value, mine), m) for m, value in enumerate(panels, 2)]
+    near = stack(mine, got[0, 1], got[1, 1], pieces)
+    ready = []
     for step in range(2, n):
         values = hand_on(got[0, step - 1], got[1, step - 1], near, step - 1)
+        ready = values if step == min(3, n - 1) else ready
         for swapped, value in enumerate(values):
             got[swapped, step] = trade(value, swapped, step)
-    held = spread(near)
+    held = spread(near, ready)
     partner = {key: flip(value, (1, 1)) for key, value in held.items()}
     keys = tuple(held)
     panels = [array for key in keys for array in (held[key], partner[key[::-1]])]

time: 86.8 us -> 82.7 us (0.953)
  waiting for transfers between devices: 46.3 us -> 42.5 us
  Pallas kernels: 15.3 us -> 16.4 us
    ppermute x6, waiting for transfers between devices: 27.4 us -> 3.8 us  [trade(): return lax.ppermute(value, ('wide', 'narrow'), pairs)]
    ppermute x7, waiting for transfers between devices: 4.15 us -> 18.2 us  [flip(): lax.ppermute(value, 'wide', [(i, i ^ masks[i & 1]) for i in range(size)])]
    ppermute x3 -> x2, waiting for transfers between devices: 14.8 us -> 20.5 us  [far_swap(): lax.ppermute(value, 'narrow', [(i, j) for i, j in pairs if abs(i - j) > 1])]
    ppermute x7, starting transfers between devices: 7.38 us -> 4 us  [flip(): lax.ppermute(value, 'wide', [(i, i ^ masks[i & 1]) for i in range(size)])]
    ppermute x3 -> x2, starting transfers between devices: 5.67 us -> 8.67 us  [far_swap(): lax.ppermute(value, 'narrow', [(i, j) for i, j in pairs if abs(i - j) > 1])]
    pallas_call x1 -> x3, Pallas kernels: 5.29 us -> 6.93 us  [the longest x1 5.17 us: multiply(): pl.pallas_call(functools.partial(late_kernel, n, keys), out_shape=jax.Sha...]
  transfers between devices with their start and end apart: 16 -> 15, of which waited for: 6 -> 5; matrix products, arithmetic and copies ran while one was open for 0% -> 0% of each run, Pallas kernels for 7% -> 10%
where the time goes in v3:
time: 82.7 us; the launch traced here: 82.4 us
  waiting for transfers between devices  42.5 us (51%)
  starting transfers between devices  22.4 us (27%)
  Pallas kernels  16.4 us (20%)
  local copies, waits for them, and re-layouts  0.93 us (1%)
    ppermute x2, waiting for transfers between devices, far_swap(): lax.ppermute(value, 'narrow', [(i, j) for i, j in pairs if abs(i - j) > 1])  20.5 us
    ppermute x7, waiting for transfers between devices, flip(): lax.ppermute(value, 'wide', [(i, i ^ masks[i & 1]) for i in range(size)])  18.2 us
    ppermute x6, starting transfers between devices, trade(): return lax.ppermute(value, ('wide', 'narrow'), pairs)  9.76 us
    ppermute x2, starting transfers between devices, far_swap(): lax.ppermute(value, 'narrow', [(i, j) for i, j in pairs if abs(i - j) > 1])  8.67 us
    pallas_call x1, Pallas kernels, multiply(): pl.pallas_call(functools.partial(early_kernel, n, plan), out_shape=outs,...  6.24 us
    pallas_call x1, Pallas kernels, multiply(): pl.pallas_call(functools.partial(late_kernel, n, keys), out_shape=jax.Sha...  5.17 us
    ppermute x7, starting transfers between devices, flip(): lax.ppermute(value, 'wide', [(i, i ^ masks[i & 1]) for i in range(size)])  4 us
    ppermute x6, waiting for transfers between devices, trade(): return lax.ppermute(value, ('wide', 'narrow'), pairs)  3.8 us
  transfers between devices with their start and end apart: 15, of which 5 were waited for; matrix products, arithmetic and copies ran while one was open for 0% of the time, Pallas kernels for 10%

profile of v3, /device:TPU:0, one launch (start us, length us, event | category | flops | bytes accessed | tf_op | source)
XLA Modules:
  0.0 82.4 jit_solution(1043378516275456497)
XLA Ops:
  0.0 2.8 %standardize.1 = (bf16[768,512]{1,0:T(8,128)(2,1)}, bf16[192,512]{1,0:T(8,128)(2,1)}, bf16[192,512]{1,0:T(8,128)(2,1)}) custom-call(s32[512,768]{1,0:T(8,128)} %dosages_ref.1, s32[1,512]{1,0:T(1,128)} %bitcast.5, s32[1,512]{1,0:T(1,128)} %bitcast.6), custom_call_target="tpu_custom_call" | custom-call | tf_op jit(solution)/shard_map/standardize/pallas_call | solution.py:86
  2.8 4.9 %collective-permute-start = (bf16[768,512]{1,0:T(8,128)(2,1)}, bf16[768,512]{1,0:T(8,128)(2,1)S(1)}, u32[]{:S(2)}, u32[]{:S(2)}) collective-permute-start(bf16[768,512]{1,0:T(8,128)(2,1)} %get-tuple-element.19.own), channel_id=1, source_target_pairs={{0,1},{1,0},{2,3},{3,2},{5,6},{6,5},{8,9},{9,8},{10,11},{11,10},{1... | collective-permute-start | bytes 2359304 | tf_op jit(solution)/shard_map/ppermute | solution.py:29
  7.7 0.7 collective-permute-start.1
  8.4 1.6 %pick.1.mine = bf16[192,512]{1,0:T(8,128)(2,1)} custom-call(bf16[768,512]{1,0:T(8,128)(2,1)} %get-tuple-element.19.own), custom_call_target="tpu_custom_call" | custom-call | tf_op jit(solution)/shard_map/pick/pallas_call | solution.py:111
  10.1 3.9 %collective-permute-start.2 = (bf16[192,512]{1,0:T(8,128)(2,1)}, bf16[192,512]{1,0:T(8,128)(2,1)S(1)}, u32[]{:S(2)}, u32[]{:S(2)}) collective-permute-start(bf16[192,512]{1,0:T(8,128)(2,1)} %get-tuple-element.21), channel_id=1, source_target_pairs={{0,2},{1,3},{2,0},{3,1},{4,6},{5,7},{6,4},{7,5},{8,10},{9,11},{10,... | collective-permute-start | bytes 589832 | tf_op jit(solution)/shard_map/ppermute | solution.py:43
  13.9 4.8 %collective-permute-start.3 = (bf16[192,512]{1,0:T(8,128)(2,1)}, bf16[192,512]{1,0:T(8,128)(2,1)S(1)}, u32[]{:S(2)}, u32[]{:S(2)}) collective-permute-start(bf16[192,512]{1,0:T(8,128)(2,1)} %get-tuple-element.23), channel_id=1, source_target_pairs={{0,3},{3,0},{4,7},{7,4},{8,11},{11,8},{12,15},{15,12},{16,19},{19,... | collective-permute-start | bytes 589832 | tf_op jit(solution)/shard_map/ppermute | solution.py:43
  18.8 20.5 %collective-permute-done.2.refs_0_ = bf16[192,512]{1,0:T(8,128)(2,1)S(1)} collective-permute-done((bf16[192,512]{1,0:T(8,128)(2,1)}, bf16[192,512]{1,0:T(8,128)(2,1)S(1)}, u32[]{:S(2)}, u32[]{:S(2)}) %collective-permute-start.2) | collective-permute-done | bytes 196640 | tf_op jit(solution)/shard_map/ppermute | solution.py:43
  39.3 0.0 collective-permute-done.3.refs_1_
  39.3 0.0 collective-permute-done.first.refs_0_
  39.3 0.0 collective-permute-done.1.second.refs_1_
  39.3 0.9 %copy-done.1 = bf16[192,512]{1,0:T(8,128)(2,1)S(1)} copy-done((bf16[192,512]{1,0:T(8,128)(2,1)S(1)}, bf16[192,512]{1,0:T(8,128)(2,1)}, u32[]{:S(2)}) %copy-start.1) | copy-done | bytes 196632
  40.2 0.3 stack.1.near.refs_4_
  40.5 1.6 %collective-permute-start.7 = (bf16[4,192,512]{2,1,0:T(8,128)(2,1)S(1)}, bf16[4,192,512]{2,1,0:T(8,128)(2,1)S(1)}, u32[]{:S(2)}, u32[]{:S(2)}) collective-permute-start(bf16[4,192,512]{2,1,0:T(8,128)(2,1)S(1)} %stack.1.near.refs_4_), channel_id=1, source_target_pairs={{0,8},{4,20},{8,0},{12,28},{16,24},{20,4},{24,16},{28,12},{1,9},{5... | collective-permute-start | bytes 2359304 | tf_op jit(solution)/shard_map/ppermute | solution.py:377
  42.1 1.5 %collective-permute-start.8 = (bf16[4,192,512]{2,1,0:T(8,128)(2,1)S(1)}, bf16[4,192,512]{2,1,0:T(8,128)(2,1)S(1)}, u32[]{:S(2)}, u32[]{:S(2)}) collective-permute-start(bf16[4,192,512]{2,1,0:T(8,128)(2,1)S(1)} %stack.1.near.refs_4_), channel_id=1, source_target_pairs={{0,16},{4,12},{8,24},{12,4},{16,0},{20,28},{24,8},{28,20},{1,17},{... | collective-permute-start | bytes 2359304 | tf_op jit(solution)/shard_map/ppermute | solution.py:377
  43.6 0.1 hand_on.2
  43.7 1.3 %collective-permute-start.4 = (bf16[576,512]{1,0:T(8,128)(2,1)S(1)}, bf16[576,512]{1,0:T(8,128)(2,1)S(1)}, u32[]{:S(2)}, u32[]{:S(2)}) collective-permute-start(bf16[576,512]{1,0:T(8,128)(2,1)S(1)} %get-tuple-element.24), channel_id=1, source_target_pairs={{1,0},{2,3},{5,6},{6,5},{9,8},{10,11},{13,14},{14,13},{17,16},{18,... | collective-permute-start | bytes 1769480 | tf_op jit(solution)/shard_map/ppermute | solution.py:29
  45.0 0.0 copy-start
  45.0 0.8 %collective-permute-start.5 = (bf16[576,512]{1,0:T(8,128)(2,1)S(1)}, bf16[576,512]{1,0:T(8,128)(2,1)S(1)}, u32[]{:S(2)}, u32[]{:S(2)}) collective-permute-start(bf16[576,512]{1,0:T(8,128)(2,1)S(1)} %get-tuple-element.25), channel_id=1, source_target_pairs={{1,2},{2,1},{5,4},{6,7},{9,10},{10,9},{13,12},{14,15},{17,18},{18,... | collective-permute-start | bytes 1769480 | tf_op jit(solution)/shard_map/ppermute | solution.py:29
  45.8 0.1 collective-permute-start.6
  45.9 12.0 %collective-permute-done.8.refs_8_ = bf16[4,192,512]{2,1,0:T(8,128)(2,1)S(1)} collective-permute-done((bf16[4,192,512]{2,1,0:T(8,128)(2,1)S(1)}, bf16[4,192,512]{2,1,0:T(8,128)(2,1)S(1)}, u32[]{:S(2)}, u32[]{:S(2)}) %collective-permute-start.8) | collective-permute-done | bytes 786464 | tf_op jit(solution)/shard_map/ppermute | solution.py:377
  57.9 0.0 collective-permute-start.9
  57.9 1.2 %collective-permute-done.7.refs_6_ = bf16[4,192,512]{2,1,0:T(8,128)(2,1)S(1)} collective-permute-done((bf16[4,192,512]{2,1,0:T(8,128)(2,1)S(1)}, bf16[4,192,512]{2,1,0:T(8,128)(2,1)S(1)}, u32[]{:S(2)}, u32[]{:S(2)}) %collective-permute-start.7) | collective-permute-done | bytes 786464 | tf_op jit(solution)/shard_map/ppermute | solution.py:377
  59.1 0.0 collective-permute-start.10
  59.1 0.1 hand_on.3
  59.2 1.3 %collective-permute-start.11 = (bf16[576,512]{1,0:T(8,128)(2,1)S(1)}, bf16[576,512]{1,0:T(8,128)(2,1)S(1)}, u32[]{:S(2)}, u32[]{:S(2)}) collective-permute-start(bf16[576,512]{1,0:T(8,128)(2,1)S(1)} %get-tuple-element.28), channel_id=1, source_target_pairs={{1,0},{2,3},{9,8},{10,11},{17,16},{18,19},{25,24},{26,27}} | collective-permute-start | bytes 1769480 | tf_op jit(solution)/shard_map/ppermute | solution.py:29
  60.5 0.7 collective-permute-start.12
  61.2 0.8 %collective-permute-start.13 = (bf16[4,192,512]{2,1,0:T(8,128)(2,1)S(1)}, bf16[4,192,512]{2,1,0:T(8,128)(2,1)S(1)}, u32[]{:S(2)}, u32[]{:S(2)}) collective-permute-start(bf16[4,192,512]{2,1,0:T(8,128)(2,1)S(1)} %collective-permute-done.7.refs_6_), channel_id=1, source_target_pairs={{0,16},{4,12},{8,24},{12,4},{16,0},{20,28},{24,8},{28,20},{1,17},{... | collective-permute-start | bytes 2359304 | tf_op jit(solution)/shard_map/ppermute | solution.py:377
  62.1 6.2 %early.1 = (f32[1152,768]{1,0:T(8,128)S(1)}, bf16[1152,512]{1,0:T(8,128)(2,1)S(1)}, bf16[768,1536]{1,0:T(8,128)(2,1)S(1)}) custom-call(bf16[768,512]{1,0:T(8,128)(2,1)S(1)} %copy-done, bf16[4,192,512]{2,1,0:T(8,128)(2,1)S(1)} %stack.1.near.refs_4_, bf16[768,512]{1,0:T(8,128)(2,1)S(1)} %collective-permute-done.first.refs_0_, ...), custom_call_target="tpu_custom_call" | custom-call | flops 12000000000 | tf_op jit(solution)/shard_map/early/pallas_call | solution.py:336
  68.3 5.0 %collective-permute-done.13.first = bf16[4,192,512]{2,1,0:T(8,128)(2,1)S(1)} collective-permute-done((bf16[4,192,512]{2,1,0:T(8,128)(2,1)S(1)}, bf16[4,192,512]{2,1,0:T(8,128)(2,1)S(1)}, u32[]{:S(2)}, u32[]{:S(2)}) %collective-permute-start.13) | collective-permute-done | bytes 786464 | tf_op jit(solution)/shard_map/ppermute | solution.py:377
  73.3 3.8 %collective-permute-done.11.refs_2_ = bf16[576,512]{1,0:T(8,128)(2,1)S(1)} collective-permute-done((bf16[576,512]{1,0:T(8,128)(2,1)S(1)}, bf16[576,512]{1,0:T(8,128)(2,1)S(1)}, u32[]{:S(2)}, u32[]{:S(2)}) %collective-permute-start.11) | collective-permute-done | bytes 589856 | tf_op jit(solution)/shard_map/ppermute | solution.py:29
  77.1 0.1 last_block.1.block
  77.2 5.2 %late.1 = f32[1536,768]{1,0:T(8,128)} custom-call(bf16[768,512]{1,0:T(8,128)(2,1)S(1)} %last_block.1.block, f32[1152,768]{1,0:T(8,128)S(1)} %get-tuple-element.30.early, bf16[1152,512]{1,0:T(8,128)(2,1)S(1)} %get-tuple-element.26.rest, bf16[768,1536]{1,0:T(8,128)(2,1)S(1)} %get-tuple-element.31.begun, ...), custom_call_target="tpu_custom_call" | custom-call | tf_op jit(solution)/shard_map/late/pallas_call | solution.py:360
  (10 shorter events, 0.0 us)
Async XLA Ops:
  2.8 36.5 %collective-permute-start = (bf16[768,512]{1,0:T(8,128)(2,1)}, bf16[768,512]{1,0:T(8,128)(2,1)S(1)}, u32[]{:S(2)}, u32[]{:S(2)}) collective-permute-start(bf16[768,512]{1,0:T(8,128)(2,1)} %get-tuple-element.19.own), channel_id=1, source_target_pairs={{0,1},{1,0},{2,3},{3,2},{5,6},{6,5},{8,9},{9,8},{10,11},{11,10},{1... | collective-permute-start | bytes 2359304 | tf_op jit(solution)/shard_map/ppermute | solution.py:29
  7.7 31.6 %collective-permute-start.1 = (bf16[768,512]{1,0:T(8,128)(2,1)}, bf16[768,512]{1,0:T(8,128)(2,1)S(1)}, u32[]{:S(2)}, u32[]{:S(2)}) collective-permute-start(bf16[768,512]{1,0:T(8,128)(2,1)} %get-tuple-element.19.own), channel_id=1, source_target_pairs={{1,2},{2,1},{4,5},{5,4},{6,7},{7,6},{9,10},{10,9},{12,13},{13,12},... | collective-permute-start | bytes 2359304 | tf_op jit(solution)/shard_map/ppermute | solution.py:29
  10.1 29.2 %collective-permute-start.2 = (bf16[192,512]{1,0:T(8,128)(2,1)}, bf16[192,512]{1,0:T(8,128)(2,1)S(1)}, u32[]{:S(2)}, u32[]{:S(2)}) collective-permute-start(bf16[192,512]{1,0:T(8,128)(2,1)} %get-tuple-element.21), channel_id=1, source_target_pairs={{0,2},{1,3},{2,0},{3,1},{4,6},{5,7},{6,4},{7,5},{8,10},{9,11},{10,... | collective-permute-start | bytes 589832 | tf_op jit(solution)/shard_map/ppermute | solution.py:43
  13.9 25.3 %collective-permute-start.3 = (bf16[192,512]{1,0:T(8,128)(2,1)}, bf16[192,512]{1,0:T(8,128)(2,1)S(1)}, u32[]{:S(2)}, u32[]{:S(2)}) collective-permute-start(bf16[192,512]{1,0:T(8,128)(2,1)} %get-tuple-element.23), channel_id=1, source_target_pairs={{0,3},{3,0},{4,7},{7,4},{8,11},{11,8},{12,15},{15,12},{16,19},{19,... | collective-permute-start | bytes 589832 | tf_op jit(solution)/shard_map/ppermute | solution.py:43
  39.3 0.9 %copy-start.1 = (bf16[192,512]{1,0:T(8,128)(2,1)S(1)}, bf16[192,512]{1,0:T(8,128)(2,1)}, u32[]{:S(2)}) copy-start(bf16[192,512]{1,0:T(8,128)(2,1)} %pick.1.mine) | copy-start | bytes 589828
  40.5 18.6 %collective-permute-start.7 = (bf16[4,192,512]{2,1,0:T(8,128)(2,1)S(1)}, bf16[4,192,512]{2,1,0:T(8,128)(2,1)S(1)}, u32[]{:S(2)}, u32[]{:S(2)}) collective-permute-start(bf16[4,192,512]{2,1,0:T(8,128)(2,1)S(1)} %stack.1.near.refs_4_), channel_id=1, source_target_pairs={{0,8},{4,20},{8,0},{12,28},{16,24},{20,4},{24,16},{28,12},{1,9},{5... | collective-permute-start | bytes 2359304 | tf_op jit(solution)/shard_map/ppermute | solution.py:377
  42.1 15.8 %collective-permute-start.8 = (bf16[4,192,512]{2,1,0:T(8,128)(2,1)S(1)}, bf16[4,192,512]{2,1,0:T(8,128)(2,1)S(1)}, u32[]{:S(2)}, u32[]{:S(2)}) collective-permute-start(bf16[4,192,512]{2,1,0:T(8,128)(2,1)S(1)} %stack.1.near.refs_4_), channel_id=1, source_target_pairs={{0,16},{4,12},{8,24},{12,4},{16,0},{20,28},{24,8},{28,20},{1,17},{... | collective-permute-start | bytes 2359304 | tf_op jit(solution)/shard_map/ppermute | solution.py:377
  43.7 15.4 %collective-permute-start.4 = (bf16[576,512]{1,0:T(8,128)(2,1)S(1)}, bf16[576,512]{1,0:T(8,128)(2,1)S(1)}, u32[]{:S(2)}, u32[]{:S(2)}) collective-permute-start(bf16[576,512]{1,0:T(8,128)(2,1)S(1)} %get-tuple-element.24), channel_id=1, source_target_pairs={{1,0},{2,3},{5,6},{6,5},{9,8},{10,11},{13,14},{14,13},{17,16},{18,... | collective-permute-start | bytes 1769480 | tf_op jit(solution)/shard_map/ppermute | solution.py:29
  45.0 17.1 %copy-start = (bf16[768,512]{1,0:T(8,128)(2,1)S(1)}, bf16[768,512]{1,0:T(8,128)(2,1)}, u32[]{:S(2)}) copy-start(bf16[768,512]{1,0:T(8,128)(2,1)} %get-tuple-element.19.own) | copy-start | bytes 2359300
  45.0 14.1 %collective-permute-start.5 = (bf16[576,512]{1,0:T(8,128)(2,1)S(1)}, bf16[576,512]{1,0:T(8,128)(2,1)S(1)}, u32[]{:S(2)}, u32[]{:S(2)}) collective-permute-start(bf16[576,512]{1,0:T(8,128)(2,1)S(1)} %get-tuple-element.25), channel_id=1, source_target_pairs={{1,2},{2,1},{5,4},{6,7},{9,10},{10,9},{13,12},{14,15},{17,18},{18,... | collective-permute-start | bytes 1769480 | tf_op jit(solution)/shard_map/ppermute | solution.py:29
  45.8 15.4 %collective-permute-start.6 = (bf16[4,192,512]{2,1,0:T(8,128)(2,1)S(1)}, bf16[4,192,512]{2,1,0:T(8,128)(2,1)S(1)}, u32[]{:S(2)}, u32[]{:S(2)}) collective-permute-start(bf16[4,192,512]{2,1,0:T(8,128)(2,1)S(1)} %stack.1.near.refs_4_), channel_id=1, source_target_pairs={{0,4},{4,0},{8,12},{12,8},{16,20},{20,16},{24,28},{28,24},{1,5},{5... | collective-permute-start | bytes 2359304 | tf_op jit(solution)/shard_map/ppermute | solution.py:377
  57.9 4.2 %collective-permute-start.9 = (bf16[4,192,512]{2,1,0:T(8,128)(2,1)S(1)}, bf16[4,192,512]{2,1,0:T(8,128)(2,1)S(1)}, u32[]{:S(2)}, u32[]{:S(2)}) collective-permute-start(bf16[4,192,512]{2,1,0:T(8,128)(2,1)S(1)} %collective-permute-done.8.refs_8_), channel_id=1, source_target_pairs={{0,4},{4,0},{8,12},{12,8},{16,20},{20,16},{24,28},{28,24},{1,5},{5... | collective-permute-start | bytes 2359304 | tf_op jit(solution)/shard_map/ppermute | solution.py:377
  59.1 3.0 %collective-permute-start.10 = (bf16[4,192,512]{2,1,0:T(8,128)(2,1)S(1)}, bf16[4,192,512]{2,1,0:T(8,128)(2,1)S(1)}, u32[]{:S(2)}, u32[]{:S(2)}) collective-permute-start(bf16[4,192,512]{2,1,0:T(8,128)(2,1)S(1)} %collective-permute-done.7.refs_6_), channel_id=1, source_target_pairs={{0,4},{4,0},{8,12},{12,8},{16,20},{20,16},{24,28},{28,24},{1,5},{5... | collective-permute-start | bytes 2359304 | tf_op jit(solution)/shard_map/ppermute | solution.py:377
  59.2 17.9 %collective-permute-start.11 = (bf16[576,512]{1,0:T(8,128)(2,1)S(1)}, bf16[576,512]{1,0:T(8,128)(2,1)S(1)}, u32[]{:S(2)}, u32[]{:S(2)}) collective-permute-start(bf16[576,512]{1,0:T(8,128)(2,1)S(1)} %get-tuple-element.28), channel_id=1, source_target_pairs={{1,0},{2,3},{9,8},{10,11},{17,16},{18,19},{25,24},{26,27}} | collective-permute-start | bytes 1769480 | tf_op jit(solution)/shard_map/ppermute | solution.py:29
  60.5 16.6 %collective-permute-start.12 = (bf16[576,512]{1,0:T(8,128)(2,1)S(1)}, bf16[576,512]{1,0:T(8,128)(2,1)S(1)}, u32[]{:S(2)}, u32[]{:S(2)}) collective-permute-start(bf16[576,512]{1,0:T(8,128)(2,1)S(1)} %get-tuple-element.29), channel_id=1, source_target_pairs={{5,4},{6,7},{13,12},{14,15},{21,20},{22,23},{29,28},{30,31}} | collective-permute-start | bytes 1769480 | tf_op jit(solution)/shard_map/ppermute | solution.py:29
  61.2 12.1 %collective-permute-start.13 = (bf16[4,192,512]{2,1,0:T(8,128)(2,1)S(1)}, bf16[4,192,512]{2,1,0:T(8,128)(2,1)S(1)}, u32[]{:S(2)}, u32[]{:S(2)}) collective-permute-start(bf16[4,192,512]{2,1,0:T(8,128)(2,1)S(1)} %collective-permute-done.7.refs_6_), channel_id=1, source_target_pairs={{0,16},{4,12},{8,24},{12,4},{16,0},{20,28},{24,8},{28,20},{1,17},{... | collective-permute-start | bytes 2359304 | tf_op jit(solution)/shard_map/ppermute | solution.py:377
  73.3 3.9 %collective-permute-start.14 = (bf16[4,192,512]{2,1,0:T(8,128)(2,1)S(1)}, bf16[4,192,512]{2,1,0:T(8,128)(2,1)S(1)}, u32[]{:S(2)}, u32[]{:S(2)}) collective-permute-start(bf16[4,192,512]{2,1,0:T(8,128)(2,1)S(1)} %collective-permute-done.13.first), channel_id=1, source_target_pairs={{0,4},{4,0},{8,12},{12,8},{16,20},{20,16},{24,28},{28,24},{1,5},{5... | collective-permute-start | bytes 2359304 | tf_op jit(solution)/shard_map/ppermute | solution.py:377

commit v4 on v3

--- a/solution.py
+++ b/solution.py
@@ -22,10 +22,8 @@
     pairs = []
     for w in range(wide):
         for low in range((w + swapped) % 2, n - 1, 2):
-            if low + 1 - step >= 0:
-                pairs.append((w * n + low, w * n + low + 1))
-            if low + step <= n - 1:
-                pairs.append((w * n + low + 1, w * n + low))
+            if low + 1 >= step or low + step <= n - 1:
+                pairs += [(w * n + low, w * n + low + 1), (w * n + low + 1, w * n + low)]
     return lax.ppermute(value, ("wide", "narrow"), pairs)
 
 
@@ -114,6 +112,7 @@
         in_specs=[ANY],
         out_specs=VMEM,
         scratch_shapes=[pltpu.SemaphoreType.DMA],
+        compiler_params=pltpu.CompilerParams(vmem_limit_bytes=2**20),
         name="pick",
     )(own)
 
@@ -273,7 +272,8 @@
     block_copies(n, plan, near, trades, z, go)
 
 
-def late_kernel(n, keys, block, early, rest, begun, first, second, out, panel, tile, out_sem):
+def late_kernel(n, keys, block, early, rest, begun, *refs):
+    halves, (out, panel, tile, out_sem) = refs[:4], refs[4:]
     z, w = lax.axis_index("narrow"), lax.axis_index("wide")
     cols, snps = block.shape
     sub = cols // n
@@ -285,15 +285,12 @@
         rows = pl.ds(pl.multiple_of(chip * (2 * sub), 2 * sub), 2 * sub)
         return pltpu.make_async_copy(tile.at[t % 2], out.at[rows], out_sem.at[t % 2])
 
-    for m, ref in enumerate((first, second)):
+    for m in range(2):
         rows = panel_rows(m, w, sub)
-        panel[rows, pl.ds((n - 1) * snps, snps)] = ref[last]
         for i in range(n):
-
-            @pl.when(i != last)
-            def _(i=i, ref=ref, rows=rows):
-                index = i - (i > last).astype(jnp.int32)
-                panel[rows, pl.ds(pl.multiple_of(index * snps, snps), snps)] = ref[i]
+            index = jnp.where(i == last, n - 1, i - (i > last).astype(jnp.int32))
+            ref = halves[2 * m + i // (n // 2)]
+            panel[rows, pl.ds(pl.multiple_of(index * snps, snps), snps)] = ref[i % (n // 2)]
 
     order = [len(keys) - 1, *range(len(keys) - 1)]
     for i, t in enumerate(order):
@@ -318,16 +315,16 @@
     return min(sum(math.prod(a.shape) * a.dtype.itemsize for a in arrays) + 4 * 2**20, 60 * 2**20)
 
 
-def multiply(own, near, got, panels, keys):
+def multiply(own, near, got, panels, halves, keys):
     n, sub, snps = near.shape
-    rows, cols = (len(panels) - 2) * sub, own.shape[0]
+    rows, cols = len(panels) * sub, own.shape[0]
     plan = tuple(key for key in got if key[1] < n - 1)
     width = 256 if cols % 256 == 0 else cols
     scratch = [
         pltpu.VMEM((rows, (n - 1) * snps), jnp.bfloat16),
         pltpu.VMEM((2, rows, width), jnp.float32),
     ]
-    operands = [own, near, *[got[key] for key in plan], *panels[:-2]]
+    operands = [own, near, *[got[key] for key in plan], *panels]
     outs = [
         jax.ShapeDtypeStruct((rows, cols), jnp.float32),
         jax.ShapeDtypeStruct((rows, snps), jnp.bfloat16),
@@ -352,14 +349,14 @@
         cost_estimate=pl.CostEstimate(flops=PACE, bytes_accessed=0, transcendentals=0),
         name="last_block",
     )(*operands)
-    operands = [block, *early, *panels[-2:]]
+    operands = [block, *early, *halves, *[flip(after(half, early[1]), (1, 1)) for half in halves]]
     scratch = [
         pltpu.VMEM((2 * sub, n * snps), jnp.bfloat16),
         pltpu.VMEM((2, 2 * sub, cols), jnp.float32),
     ]
     return pl.pallas_call(
         functools.partial(late_kernel, n, keys),
-        out_shape=jax.ShapeDtypeStruct((len(panels) * sub, cols), jnp.float32),
+        out_shape=jax.ShapeDtypeStruct((rows + 2 * sub, cols), jnp.float32),
         in_specs=[VMEM] * len(operands),
         out_specs=ANY,
         scratch_shapes=scratch + [pltpu.SemaphoreType.DMA((2,))],
@@ -386,7 +383,12 @@
         for key, value in list(got.items()):
             if any(key):
                 value = after(value, *earlier)
-            got[key[0] ^ masks[0], key[1] ^ masks[1]] = flip(value, masks)
+            to = key[0] ^ masks[0], key[1] ^ masks[1]
+            if to == (size - 2, size - 2):
+                half = value.shape[0] // 2
+                got[to] = [flip(value[:half], masks), flip(value[half:], masks)]
+            else:
+                got[to] = flip(value, masks)
     return got
 
 
@@ -407,10 +409,10 @@
         for swapped, value in enumerate(values):
             got[swapped, step] = trade(value, swapped, step)
     held = spread(near, ready)
-    partner = {key: flip(value, (1, 1)) for key, value in held.items()}
-    keys = tuple(held)
+    *keys, final = held
+    partner = {key: flip(held[key], (1, 1)) for key in keys}
     panels = [array for key in keys for array in (held[key], partner[key[::-1]])]
-    result = multiply(own, near, got, panels, keys)
+    result = multiply(own, near, got, panels, held[final], tuple(held))
     return result.reshape(wide, 1, sub, cols)
 
 

time: 82.7 us -> 81.7 us (0.988)
  starting transfers between devices: 22.4 us -> 25.4 us
  waiting for transfers between devices: 42.5 us -> 39.7 us
  Pallas kernels: 16.4 us -> 14.9 us
    ppermute x7 -> x9, waiting for transfers between devices: 18.2 us -> 16.2 us  [flip(): lax.ppermute(value, 'wide', [(i, i ^ masks[i & 1]) for i in range(size)])]
    ppermute x6, starting transfers between devices: 9.76 us -> 11.4 us  [trade(): return lax.ppermute(value, ('wide', 'narrow'), pairs)]
    pallas_call x1, Pallas kernels: 1.63 us -> 0.23 us  [pick(): pl.pallas_call(pick_kernel, out_shape=jax.ShapeDtypeStruct((sub, own.shap...]
    ppermute x7 -> x9, starting transfers between devices: 4 us -> 5.32 us  [flip(): lax.ppermute(value, 'wide', [(i, i ^ masks[i & 1]) for i in range(size)])]
    ppermute x6, waiting for transfers between devices: 3.8 us -> 2.68 us  [trade(): return lax.ppermute(value, ('wide', 'narrow'), pairs)]
  transfers between devices with their start and end apart: 15 -> 17, of which waited for: 5 -> 5; matrix products, arithmetic and copies ran while one was open for 0% -> 0% of each run, Pallas kernels for 10% -> 8%
where the time goes in v4:
time: 81.7 us; the launch traced here: 81.4 us
  waiting for transfers between devices  39.7 us (49%)
  starting transfers between devices  25.4 us (31%)
  Pallas kernels  14.9 us (18%)
  local copies, waits for them, and re-layouts  1.19 us (1%)
    ppermute x2, waiting for transfers between devices, far_swap(): lax.ppermute(value, 'narrow', [(i, j) for i, j in pairs if abs(i - j) > 1])  20.8 us
    ppermute x9, waiting for transfers between devices, flip(): lax.ppermute(value, 'wide', [(i, i ^ masks[i & 1]) for i in range(size)])  16.2 us
    ppermute x6, starting transfers between devices, trade(): return lax.ppermute(value, ('wide', 'narrow'), pairs)  11.4 us
    ppermute x2, starting transfers between devices, far_swap(): lax.ppermute(value, 'narrow', [(i, j) for i, j in pairs if abs(i - j) > 1])  8.68 us
    pallas_call x1, Pallas kernels, multiply(): pl.pallas_call(functools.partial(early_kernel, n, plan), out_shape=outs,...  6.21 us
    ppermute x9, starting transfers between devices, flip(): lax.ppermute(value, 'wide', [(i, i ^ masks[i & 1]) for i in range(size)])  5.32 us
    pallas_call x1, Pallas kernels, multiply(): pl.pallas_call(functools.partial(late_kernel, n, keys), out_shape=jax.Sha...  5.06 us
    pallas_call x1, Pallas kernels, standardize(): pl.pallas_call(functools.partial(standardize_kernel, n), out_shape=[jax.S...  2.77 us
  transfers between devices with their start and end apart: 17, of which 5 were waited for; matrix products, arithmetic and copies ran while one was open for 0% of the time, Pallas kernels for 8%

profile of v4, /device:TPU:0, one launch (start us, length us, event | category | flops | bytes accessed | tf_op | source)
XLA Modules:
  0.0 81.4 jit_solution(13049768184098503630)
XLA Ops:
  0.0 2.8 %standardize.1 = (bf16[768,512]{1,0:T(8,128)(2,1)}, bf16[192,512]{1,0:T(8,128)(2,1)}, bf16[192,512]{1,0:T(8,128)(2,1)}) custom-call(s32[512,768]{1,0:T(8,128)} %dosages_ref.1, s32[1,512]{1,0:T(1,128)} %bitcast.5, s32[1,512]{1,0:T(1,128)} %bitcast.6), custom_call_target="tpu_custom_call" | custom-call | tf_op jit(solution)/shard_map/standardize/pallas_call | solution.py:84
  2.8 4.9 %collective-permute-start = (bf16[768,512]{1,0:T(8,128)(2,1)}, bf16[768,512]{1,0:T(8,128)(2,1)S(1)}, u32[]{:S(2)}, u32[]{:S(2)}) collective-permute-start(bf16[768,512]{1,0:T(8,128)(2,1)} %get-tuple-element.21.own), channel_id=1, source_target_pairs={{0,1},{1,0},{2,3},{3,2},{5,6},{6,5},{8,9},{9,8},{10,11},{11,10},{1... | collective-permute-start | bytes 2359304 | tf_op jit(solution)/shard_map/ppermute | solution.py:27
  7.7 0.7 collective-permute-start.1
  8.4 0.0 copy-start
  8.4 1.1 %copy-done = bf16[768,512]{1,0:T(8,128)(2,1)S(1)} copy-done((bf16[768,512]{1,0:T(8,128)(2,1)S(1)}, bf16[768,512]{1,0:T(8,128)(2,1)}, u32[]{:S(2)}) %copy-start) | copy-done | bytes 786456
  9.6 0.2 pick.1.mine
  9.8 3.9 %collective-permute-start.2 = (bf16[192,512]{1,0:T(8,128)(2,1)}, bf16[192,512]{1,0:T(8,128)(2,1)S(1)}, u32[]{:S(2)}, u32[]{:S(2)}) collective-permute-start(bf16[192,512]{1,0:T(8,128)(2,1)} %get-tuple-element.23), channel_id=1, source_target_pairs={{0,2},{1,3},{2,0},{3,1},{4,6},{5,7},{6,4},{7,5},{8,10},{9,11},{10,... | collective-permute-start | bytes 589832 | tf_op jit(solution)/shard_map/ppermute | solution.py:41
  13.7 4.8 %collective-permute-start.3 = (bf16[192,512]{1,0:T(8,128)(2,1)}, bf16[192,512]{1,0:T(8,128)(2,1)S(1)}, u32[]{:S(2)}, u32[]{:S(2)}) collective-permute-start(bf16[192,512]{1,0:T(8,128)(2,1)} %get-tuple-element.25), channel_id=1, source_target_pairs={{0,3},{3,0},{4,7},{7,4},{8,11},{11,8},{12,15},{15,12},{16,19},{19,... | collective-permute-start | bytes 589832 | tf_op jit(solution)/shard_map/ppermute | solution.py:41
  18.5 20.8 %collective-permute-done.2.refs_0_ = bf16[192,512]{1,0:T(8,128)(2,1)S(1)} collective-permute-done((bf16[192,512]{1,0:T(8,128)(2,1)}, bf16[192,512]{1,0:T(8,128)(2,1)S(1)}, u32[]{:S(2)}, u32[]{:S(2)}) %collective-permute-start.2) | collective-permute-done | bytes 196640 | tf_op jit(solution)/shard_map/ppermute | solution.py:41
  39.3 0.4 stack.1.near.refs_4_
  39.6 1.6 %collective-permute-start.7 = (bf16[4,192,512]{2,1,0:T(8,128)(2,1)S(1)}, bf16[4,192,512]{2,1,0:T(8,128)(2,1)S(1)}, u32[]{:S(2)}, u32[]{:S(2)}) collective-permute-start(bf16[4,192,512]{2,1,0:T(8,128)(2,1)S(1)} %stack.1.near.refs_4_), channel_id=1, source_target_pairs={{0,8},{4,20},{8,0},{12,28},{16,24},{20,4},{24,16},{28,12},{1,9},{5... | collective-permute-start | bytes 2359304 | tf_op jit(solution)/shard_map/ppermute | solution.py:374
  41.2 1.5 %collective-permute-start.8 = (bf16[4,192,512]{2,1,0:T(8,128)(2,1)S(1)}, bf16[4,192,512]{2,1,0:T(8,128)(2,1)S(1)}, u32[]{:S(2)}, u32[]{:S(2)}) collective-permute-start(bf16[4,192,512]{2,1,0:T(8,128)(2,1)S(1)} %stack.1.near.refs_4_), channel_id=1, source_target_pairs={{0,16},{4,12},{8,24},{12,4},{16,0},{20,28},{24,8},{28,20},{1,17},{... | collective-permute-start | bytes 2359304 | tf_op jit(solution)/shard_map/ppermute | solution.py:374
  42.7 0.1 hand_on.2
  42.8 1.9 %collective-permute-start.4 = (bf16[576,512]{1,0:T(8,128)(2,1)S(1)}, bf16[576,512]{1,0:T(8,128)(2,1)S(1)}, u32[]{:S(2)}, u32[]{:S(2)}) collective-permute-start(bf16[576,512]{1,0:T(8,128)(2,1)S(1)} %get-tuple-element.26), channel_id=1, source_target_pairs={{0,1},{1,0},{2,3},{3,2},{5,6},{6,5},{8,9},{9,8},{10,11},{11,10},{1... | collective-permute-start | bytes 1769480 | tf_op jit(solution)/shard_map/ppermute | solution.py:27
  44.7 0.0 copy-start.1
  44.7 0.8 %collective-permute-start.5 = (bf16[576,512]{1,0:T(8,128)(2,1)S(1)}, bf16[576,512]{1,0:T(8,128)(2,1)S(1)}, u32[]{:S(2)}, u32[]{:S(2)}) collective-permute-start(bf16[576,512]{1,0:T(8,128)(2,1)S(1)} %get-tuple-element.27), channel_id=1, source_target_pairs={{1,2},{2,1},{4,5},{5,4},{6,7},{7,6},{9,10},{10,9},{12,13},{13,12},... | collective-permute-start | bytes 1769480 | tf_op jit(solution)/shard_map/ppermute | solution.py:27
  45.6 0.1 collective-permute-start.6
  45.7 11.3 %collective-permute-done.8.refs_8_ = bf16[4,192,512]{2,1,0:T(8,128)(2,1)S(1)} collective-permute-done((bf16[4,192,512]{2,1,0:T(8,128)(2,1)S(1)}, bf16[4,192,512]{2,1,0:T(8,128)(2,1)S(1)}, u32[]{:S(2)}, u32[]{:S(2)}) %collective-permute-start.8) | collective-permute-done | bytes 786464 | tf_op jit(solution)/shard_map/ppermute | solution.py:374
  57.0 0.0 collective-permute-start.9
  57.0 1.2 %collective-permute-done.7.refs_6_ = bf16[4,192,512]{2,1,0:T(8,128)(2,1)S(1)} collective-permute-done((bf16[4,192,512]{2,1,0:T(8,128)(2,1)S(1)}, bf16[4,192,512]{2,1,0:T(8,128)(2,1)S(1)}, u32[]{:S(2)}, u32[]{:S(2)}) %collective-permute-start.7) | collective-permute-done | bytes 786464 | tf_op jit(solution)/shard_map/ppermute | solution.py:374
  58.2 0.1 hand_on.3
  58.3 2.3 %collective-permute-start.11 = (bf16[576,512]{1,0:T(8,128)(2,1)S(1)}, bf16[576,512]{1,0:T(8,128)(2,1)S(1)}, u32[]{:S(2)}, u32[]{:S(2)}) collective-permute-start(bf16[576,512]{1,0:T(8,128)(2,1)S(1)} %get-tuple-element.30), channel_id=1, source_target_pairs={{0,1},{1,0},{2,3},{3,2},{8,9},{9,8},{10,11},{11,10},{16,17},{17,16... | collective-permute-start | bytes 1769480 | tf_op jit(solution)/shard_map/ppermute | solution.py:27
  60.7 0.7 collective-permute-start.12
  61.4 0.1 fusion
  61.5 0.6 collective-permute-start.13
  62.0 1.5 %collective-permute-start.14 = (bf16[2,192,512]{2,1,0:T(8,128)(2,1)S(1)}, bf16[2,192,512]{2,1,0:T(8,128)(2,1)S(1)}, u32[]{:S(2)}, u32[]{:S(2)}) collective-permute-start(bf16[2,192,512]{2,1,0:T(8,128)(2,1)S(1)} %get-tuple-element.37), channel_id=1, source_target_pairs={{0,16},{4,12},{8,24},{12,4},{16,0},{20,28},{24,8},{28,20},{1,17},{... | collective-permute-start | bytes 1179656 | tf_op jit(solution)/shard_map/ppermute | solution.py:374
  63.6 6.2 %early.1 = (f32[1152,768]{1,0:T(8,128)S(1)}, bf16[1152,512]{1,0:T(8,128)(2,1)S(1)}, bf16[768,1536]{1,0:T(8,128)(2,1)S(1)}) custom-call(bf16[768,512]{1,0:T(8,128)(2,1)S(1)} %copy-done.1, bf16[4,192,512]{2,1,0:T(8,128)(2,1)S(1)} %stack.1.near.refs_4_, bf16[768,512]{1,0:T(8,128)(2,1)S(1)} %collective-permute-done.first.refs_0_, ...), custom_call_target="tpu_custom_call" | custom-call | flops 12000000000 | tf_op jit(solution)/shard_map/early/pallas_call | solution.py:333
  69.8 0.1 collective-permute-start.15
  69.9 3.6 %collective-permute-done.14.refs_1_ = bf16[2,192,512]{2,1,0:T(8,128)(2,1)S(1)} collective-permute-done((bf16[2,192,512]{2,1,0:T(8,128)(2,1)S(1)}, bf16[2,192,512]{2,1,0:T(8,128)(2,1)S(1)}, u32[]{:S(2)}, u32[]{:S(2)}) %collective-permute-start.14) | collective-permute-done | bytes 393248 | tf_op jit(solution)/shard_map/ppermute | solution.py:374
  73.5 2.7 %collective-permute-done.11.refs_2_ = bf16[576,512]{1,0:T(8,128)(2,1)S(1)} collective-permute-done((bf16[576,512]{1,0:T(8,128)(2,1)S(1)}, bf16[576,512]{1,0:T(8,128)(2,1)S(1)}, u32[]{:S(2)}, u32[]{:S(2)}) %collective-permute-start.11) | collective-permute-done | bytes 589856 | tf_op jit(solution)/shard_map/ppermute | solution.py:27
  76.2 0.1 last_block.1.block
  76.3 5.1 %late.1 = f32[1536,768]{1,0:T(8,128)} custom-call(bf16[768,512]{1,0:T(8,128)(2,1)S(1)} %last_block.1.block, f32[1152,768]{1,0:T(8,128)S(1)} %get-tuple-element.32.early, bf16[1152,512]{1,0:T(8,128)(2,1)S(1)} %get-tuple-element.28.rest, bf16[768,1536]{1,0:T(8,128)(2,1)S(1)} %get-tuple-element.33.begun, ...), custom_call_target="tpu_custom_call" | custom-call | tf_op jit(solution)/shard_map/late/pallas_call | solution.py:357
  (15 shorter events, 0.0 us)
Async XLA Ops:
  2.8 36.5 %collective-permute-start = (bf16[768,512]{1,0:T(8,128)(2,1)}, bf16[768,512]{1,0:T(8,128)(2,1)S(1)}, u32[]{:S(2)}, u32[]{:S(2)}) collective-permute-start(bf16[768,512]{1,0:T(8,128)(2,1)} %get-tuple-element.21.own), channel_id=1, source_target_pairs={{0,1},{1,0},{2,3},{3,2},{5,6},{6,5},{8,9},{9,8},{10,11},{11,10},{1... | collective-permute-start | bytes 2359304 | tf_op jit(solution)/shard_map/ppermute | solution.py:27
  7.7 31.6 %collective-permute-start.1 = (bf16[768,512]{1,0:T(8,128)(2,1)}, bf16[768,512]{1,0:T(8,128)(2,1)S(1)}, u32[]{:S(2)}, u32[]{:S(2)}) collective-permute-start(bf16[768,512]{1,0:T(8,128)(2,1)} %get-tuple-element.21.own), channel_id=1, source_target_pairs={{1,2},{2,1},{4,5},{5,4},{6,7},{7,6},{9,10},{10,9},{12,13},{13,12},... | collective-permute-start | bytes 2359304 | tf_op jit(solution)/shard_map/ppermute | solution.py:27
  8.4 1.1 %copy-start = (bf16[768,512]{1,0:T(8,128)(2,1)S(1)}, bf16[768,512]{1,0:T(8,128)(2,1)}, u32[]{:S(2)}) copy-start(bf16[768,512]{1,0:T(8,128)(2,1)} %get-tuple-element.21.own) | copy-start | bytes 2359300
  9.8 29.5 %collective-permute-start.2 = (bf16[192,512]{1,0:T(8,128)(2,1)}, bf16[192,512]{1,0:T(8,128)(2,1)S(1)}, u32[]{:S(2)}, u32[]{:S(2)}) collective-permute-start(bf16[192,512]{1,0:T(8,128)(2,1)} %get-tuple-element.23), channel_id=1, source_target_pairs={{0,2},{1,3},{2,0},{3,1},{4,6},{5,7},{6,4},{7,5},{8,10},{9,11},{10,... | collective-permute-start | bytes 589832 | tf_op jit(solution)/shard_map/ppermute | solution.py:41
  13.7 25.6 %collective-permute-start.3 = (bf16[192,512]{1,0:T(8,128)(2,1)}, bf16[192,512]{1,0:T(8,128)(2,1)S(1)}, u32[]{:S(2)}, u32[]{:S(2)}) collective-permute-start(bf16[192,512]{1,0:T(8,128)(2,1)} %get-tuple-element.25), channel_id=1, source_target_pairs={{0,3},{3,0},{4,7},{7,4},{8,11},{11,8},{12,15},{15,12},{16,19},{19,... | collective-permute-start | bytes 589832 | tf_op jit(solution)/shard_map/ppermute | solution.py:41
  39.6 18.6 %collective-permute-start.7 = (bf16[4,192,512]{2,1,0:T(8,128)(2,1)S(1)}, bf16[4,192,512]{2,1,0:T(8,128)(2,1)S(1)}, u32[]{:S(2)}, u32[]{:S(2)}) collective-permute-start(bf16[4,192,512]{2,1,0:T(8,128)(2,1)S(1)} %stack.1.near.refs_4_), channel_id=1, source_target_pairs={{0,8},{4,20},{8,0},{12,28},{16,24},{20,4},{24,16},{28,12},{1,9},{5... | collective-permute-start | bytes 2359304 | tf_op jit(solution)/shard_map/ppermute | solution.py:374
  41.2 15.8 %collective-permute-start.8 = (bf16[4,192,512]{2,1,0:T(8,128)(2,1)S(1)}, bf16[4,192,512]{2,1,0:T(8,128)(2,1)S(1)}, u32[]{:S(2)}, u32[]{:S(2)}) collective-permute-start(bf16[4,192,512]{2,1,0:T(8,128)(2,1)S(1)} %stack.1.near.refs_4_), channel_id=1, source_target_pairs={{0,16},{4,12},{8,24},{12,4},{16,0},{20,28},{24,8},{28,20},{1,17},{... | collective-permute-start | bytes 2359304 | tf_op jit(solution)/shard_map/ppermute | solution.py:374
  42.8 15.4 %collective-permute-start.4 = (bf16[576,512]{1,0:T(8,128)(2,1)S(1)}, bf16[576,512]{1,0:T(8,128)(2,1)S(1)}, u32[]{:S(2)}, u32[]{:S(2)}) collective-permute-start(bf16[576,512]{1,0:T(8,128)(2,1)S(1)} %get-tuple-element.26), channel_id=1, source_target_pairs={{0,1},{1,0},{2,3},{3,2},{5,6},{6,5},{8,9},{9,8},{10,11},{11,10},{1... | collective-permute-start | bytes 1769480 | tf_op jit(solution)/shard_map/ppermute | solution.py:27
  44.7 18.8 %copy-start.1 = (bf16[768,512]{1,0:T(8,128)(2,1)S(1)}, bf16[768,512]{1,0:T(8,128)(2,1)}, u32[]{:S(2)}) copy-start(bf16[768,512]{1,0:T(8,128)(2,1)} %get-tuple-element.21.own) | copy-start | bytes 2359300
  44.7 13.5 %collective-permute-start.5 = (bf16[576,512]{1,0:T(8,128)(2,1)S(1)}, bf16[576,512]{1,0:T(8,128)(2,1)S(1)}, u32[]{:S(2)}, u32[]{:S(2)}) collective-permute-start(bf16[576,512]{1,0:T(8,128)(2,1)S(1)} %get-tuple-element.27), channel_id=1, source_target_pairs={{1,2},{2,1},{4,5},{5,4},{6,7},{7,6},{9,10},{10,9},{12,13},{13,12},... | collective-permute-start | bytes 1769480 | tf_op jit(solution)/shard_map/ppermute | solution.py:27
  45.6 15.9 %collective-permute-start.6 = (bf16[4,192,512]{2,1,0:T(8,128)(2,1)S(1)}, bf16[4,192,512]{2,1,0:T(8,128)(2,1)S(1)}, u32[]{:S(2)}, u32[]{:S(2)}) collective-permute-start(bf16[4,192,512]{2,1,0:T(8,128)(2,1)S(1)} %stack.1.near.refs_4_), channel_id=1, source_target_pairs={{0,4},{4,0},{8,12},{12,8},{16,20},{20,16},{24,28},{28,24},{1,5},{5... | collective-permute-start | bytes 2359304 | tf_op jit(solution)/shard_map/ppermute | solution.py:374
  57.0 5.1 %collective-permute-start.9 = (bf16[4,192,512]{2,1,0:T(8,128)(2,1)S(1)}, bf16[4,192,512]{2,1,0:T(8,128)(2,1)S(1)}, u32[]{:S(2)}, u32[]{:S(2)}) collective-permute-start(bf16[4,192,512]{2,1,0:T(8,128)(2,1)S(1)} %collective-permute-done.8.refs_8_), channel_id=1, source_target_pairs={{0,4},{4,0},{8,12},{12,8},{16,20},{20,16},{24,28},{28,24},{1,5},{5... | collective-permute-start | bytes 2359304 | tf_op jit(solution)/shard_map/ppermute | solution.py:374
  58.2 5.4 %collective-permute-start.10 = (bf16[4,192,512]{2,1,0:T(8,128)(2,1)S(1)}, bf16[4,192,512]{2,1,0:T(8,128)(2,1)S(1)}, u32[]{:S(2)}, u32[]{:S(2)}) collective-permute-start(bf16[4,192,512]{2,1,0:T(8,128)(2,1)S(1)} %collective-permute-done.7.refs_6_), channel_id=1, source_target_pairs={{0,4},{4,0},{8,12},{12,8},{16,20},{20,16},{24,28},{28,24},{1,5},{5... | collective-permute-start | bytes 2359304 | tf_op jit(solution)/shard_map/ppermute | solution.py:374
  58.3 17.9 %collective-permute-start.11 = (bf16[576,512]{1,0:T(8,128)(2,1)S(1)}, bf16[576,512]{1,0:T(8,128)(2,1)S(1)}, u32[]{:S(2)}, u32[]{:S(2)}) collective-permute-start(bf16[576,512]{1,0:T(8,128)(2,1)S(1)} %get-tuple-element.30), channel_id=1, source_target_pairs={{0,1},{1,0},{2,3},{3,2},{8,9},{9,8},{10,11},{11,10},{16,17},{17,16... | collective-permute-start | bytes 1769480 | tf_op jit(solution)/shard_map/ppermute | solution.py:27
  60.7 15.5 %collective-permute-start.12 = (bf16[576,512]{1,0:T(8,128)(2,1)S(1)}, bf16[576,512]{1,0:T(8,128)(2,1)S(1)}, u32[]{:S(2)}, u32[]{:S(2)}) collective-permute-start(bf16[576,512]{1,0:T(8,128)(2,1)S(1)} %get-tuple-element.31), channel_id=1, source_target_pairs={{4,5},{5,4},{6,7},{7,6},{12,13},{13,12},{14,15},{15,14},{20,21},{2... | collective-permute-start | bytes 1769480 | tf_op jit(solution)/shard_map/ppermute | solution.py:27
  61.5 8.3 %collective-permute-start.13 = (bf16[2,192,512]{2,1,0:T(8,128)(2,1)S(1)}, bf16[2,192,512]{2,1,0:T(8,128)(2,1)S(1)}, u32[]{:S(2)}, u32[]{:S(2)}) collective-permute-start(bf16[2,192,512]{2,1,0:T(8,128)(2,1)S(1)} %get-tuple-element.38), channel_id=1, source_target_pairs={{0,16},{4,12},{8,24},{12,4},{16,0},{20,28},{24,8},{28,20},{1,17},{... | collective-permute-start | bytes 1179656 | tf_op jit(solution)/shard_map/ppermute | solution.py:374
  62.0 11.5 %collective-permute-start.14 = (bf16[2,192,512]{2,1,0:T(8,128)(2,1)S(1)}, bf16[2,192,512]{2,1,0:T(8,128)(2,1)S(1)}, u32[]{:S(2)}, u32[]{:S(2)}) collective-permute-start(bf16[2,192,512]{2,1,0:T(8,128)(2,1)S(1)} %get-tuple-element.37), channel_id=1, source_target_pairs={{0,16},{4,12},{8,24},{12,4},{16,0},{20,28},{24,8},{28,20},{1,17},{... | collective-permute-start | bytes 1179656 | tf_op jit(solution)/shard_map/ppermute | solution.py:374
  69.8 6.5 %collective-permute-start.15 = (bf16[2,192,512]{2,1,0:T(8,128)(2,1)S(1)}, bf16[2,192,512]{2,1,0:T(8,128)(2,1)S(1)}, u32[]{:S(2)}, u32[]{:S(2)}) collective-permute-start(bf16[2,192,512]{2,1,0:T(8,128)(2,1)S(1)} %collective-permute-done.13.refs_0_), channel_id=1, source_target_pairs={{0,4},{4,0},{8,12},{12,8},{16,20},{20,16},{24,28},{28,24},{1,5},{5... | collective-permute-start | bytes 1179656 | tf_op jit(solution)/shard_map/ppermute | solution.py:374
  73.5 2.8 %collective-permute-start.16 = (bf16[2,192,512]{2,1,0:T(8,128)(2,1)S(1)}, bf16[2,192,512]{2,1,0:T(8,128)(2,1)S(1)}, u32[]{:S(2)}, u32[]{:S(2)}) collective-permute-start(bf16[2,192,512]{2,1,0:T(8,128)(2,1)S(1)} %collective-permute-done.14.refs_1_), channel_id=1, source_target_pairs={{0,4},{4,0},{8,12},{12,8},{16,20},{20,16},{24,28},{28,24},{1,5},{5... | collective-permute-start | bytes 1179656 | tf_op jit(solution)/shard_map/ppermute | solution.py:374

commit v5 on v4

--- a/solution.py
+++ b/solution.py
@@ -10,7 +10,7 @@
 
 LANES = 128
 HOP = 20_000_000_000
-PACE = 10_000_000_000
+MIDDLE = 0
 EARLY = 12_000_000_000
 ANY = pl.BlockSpec(memory_space=pl.ANY)
 VMEM = pl.BlockSpec(memory_space=pltpu.VMEM)
@@ -272,42 +272,49 @@
     block_copies(n, plan, near, trades, z, go)
 
 
-def late_kernel(n, keys, block, early, rest, begun, *refs):
-    halves, (out, panel, tile, out_sem) = refs[:4], refs[4:]
-    z, w = lax.axis_index("narrow"), lax.axis_index("wide")
-    cols, snps = block.shape
-    sub = cols // n
-    last = last_slab(z, n)
-    dims = (((1,), (1,)), ((), ()))
-
-    def out_copy(t):
-        chip = (w ^ jnp.where(lax.rem(w, 2) == 0, *keys[t])) // 2
-        rows = pl.ds(pl.multiple_of(chip * (2 * sub), 2 * sub), 2 * sub)
-        return pltpu.make_async_copy(tile.at[t % 2], out.at[rows], out_sem.at[t % 2])
-
+def middle_kernel(n, begun, *refs):
+    halves, (out, rest, panel) = refs[:4], refs[4:]
+    w, last = lax.axis_index("wide"), last_slab(lax.axis_index("narrow"), n)
+    _, sub, snps = halves[0].shape
     for m in range(2):
         rows = panel_rows(m, w, sub)
         for i in range(n):
-            index = jnp.where(i == last, n - 1, i - (i > last).astype(jnp.int32))
             ref = halves[2 * m + i // (n // 2)]
-            panel[rows, pl.ds(pl.multiple_of(index * snps, snps), snps)] = ref[i % (n // 2)]
-
-    order = [len(keys) - 1, *range(len(keys) - 1)]
-    for i, t in enumerate(order):
-        if i >= 2:
-            out_copy(order[i - 2]).wait()
-        if i == 0:
-            before = lax.dot_general(
-                panel[:, : (n - 1) * snps], begun[...], dims, preferred_element_type=jnp.float32
-            )
-            left = panel[:, (n - 1) * snps :]
+
+            @pl.when(i == last)
+            def _(i=i, ref=ref, rows=rows):
+                rest[rows, :] = ref[i % (n // 2)]
+
+            @pl.when(i != last)
+            def _(i=i, ref=ref, rows=rows):
+                index = i - (i > last).astype(jnp.int32)
+                panel[rows, pl.ds(pl.multiple_of(index * snps, snps), snps)] = ref[i % (n // 2)]
+
+    out[...] = lax.dot_general(panel[...], begun[...], (((1,), (1,)), ((), ())), preferred_element_type=jnp.float32)
+
+
+def late_kernel(n, keys, block, early, early_rest, middle, middle_rest, out, tile, out_sem):
+    w = lax.axis_index("wide")
+    snps, size = block.shape[1], middle.shape[0]
+    slots = tile.shape[0]
+
+    def out_copy(t):
+        chip = (w ^ jnp.where(lax.rem(w, 2) == 0, *keys[t])) // 2
+        rows = pl.ds(pl.multiple_of(chip * size, size), size)
+        return pltpu.make_async_copy(tile.at[t % slots], out.at[rows], out_sem.at[t % slots])
+
+    for t in range(len(keys)):
+        if t >= slots:
+            out_copy(t - slots).wait()
+        if t < len(keys) - 1:
+            rows = pl.ds(t * size, size)
+            before, left = early[rows, :], early_rest[rows, :]
         else:
-            rows = pl.ds(t * 2 * sub, 2 * sub)
-            before, left = early[rows, :], rest[rows, :]
-        product = lax.dot_general(left, block[...], dims, preferred_element_type=jnp.float32)
-        tile[t % 2] = (before + product) / (n * snps)
+            before, left = middle[...], middle_rest[...]
+        product = lax.dot_general(left, block[...], (((1,), (1,)), ((), ())), preferred_element_type=jnp.float32)
+        tile[t % slots] = (before + product) / (n * snps)
         out_copy(t).start()
-    for t in order[-2:]:
+    for t in range(max(len(keys) - slots, 0), len(keys)):
         out_copy(t).wait()
 
 
@@ -341,25 +348,36 @@
         name="early",
     )(*operands)
     plan = tuple(key for key in got if key[1] >= n // 2)
-    operands = [after(near, early[1]), *[got[key] for key in plan]]
+    operands = [early[2], *halves, *[flip(after(half, early[1]), (1, 1)) for half in halves]]
+    outs = [
+        jax.ShapeDtypeStruct((2 * sub, cols), jnp.float32),
+        jax.ShapeDtypeStruct((2 * sub, snps), jnp.bfloat16),
+    ]
+    scratch = [pltpu.VMEM((2 * sub, (n - 1) * snps), jnp.bfloat16)]
+    middle = pl.pallas_call(
+        functools.partial(middle_kernel, n),
+        out_shape=outs,
+        scratch_shapes=scratch,
+        compiler_params=pltpu.CompilerParams(vmem_limit_bytes=limit([*operands, *scratch, *outs])),
+        cost_estimate=pl.CostEstimate(flops=MIDDLE, bytes_accessed=0, transcendentals=0),
+        name="middle",
+    )(*operands)
+    operands = [after(near, middle[1]), *[got[key] for key in plan]]
     block = pl.pallas_call(
         functools.partial(last_block_kernel, n, plan),
         out_shape=jax.ShapeDtypeStruct((cols, snps), jnp.bfloat16),
         compiler_params=pltpu.CompilerParams(vmem_limit_bytes=limit(operands)),
-        cost_estimate=pl.CostEstimate(flops=PACE, bytes_accessed=0, transcendentals=0),
         name="last_block",
     )(*operands)
-    operands = [block, *early, *halves, *[flip(after(half, early[1]), (1, 1)) for half in halves]]
-    scratch = [
-        pltpu.VMEM((2 * sub, n * snps), jnp.bfloat16),
-        pltpu.VMEM((2, 2 * sub, cols), jnp.float32),
-    ]
+    operands = [block, *early[:2], *middle]
+    slots = min(4, len(keys))
+    scratch = [pltpu.VMEM((slots, 2 * sub, cols), jnp.float32)]
     return pl.pallas_call(
         functools.partial(late_kernel, n, keys),
         out_shape=jax.ShapeDtypeStruct((rows + 2 * sub, cols), jnp.float32),
         in_specs=[VMEM] * len(operands),
         out_specs=ANY,
-        scratch_shapes=scratch + [pltpu.SemaphoreType.DMA((2,))],
+        scratch_shapes=scratch + [pltpu.SemaphoreType.DMA((slots,))],
         compiler_params=pltpu.CompilerParams(vmem_limit_bytes=limit([*operands, *scratch])),
         name="late",
     )(*operands)

time: 81.7 us -> 79.8 us (0.977)
  waiting for transfers between devices: 39.7 us -> 38.7 us
  Pallas kernels: 14.9 us -> 14 us
    ppermute x6, waiting for transfers between devices: 2.68 us -> 0.02 us  [trade(): return lax.ppermute(value, ('wide', 'narrow'), pairs)]
    pallas_call x1, Pallas kernels: 5.06 us -> 2.82 us  [multiply(): pl.pallas_call(functools.partial(late_kernel, n, keys), out_shape=jax.Sha...]
    ppermute x9, waiting for transfers between devices: 16.2 us -> 17.9 us  [flip(): lax.ppermute(value, 'wide', [(i, i ^ masks[i & 1]) for i in range(size)])]
    pallas_call x0 -> x1, Pallas kernels: none -> 1.28 us  [multiply(): pl.pallas_call(functools.partial(middle_kernel, n), out_shape=outs, scrat...]
  transfers between devices with their start and end apart: 17 -> 17, of which waited for: 5 -> 5; matrix products, arithmetic and copies ran while one was open for 0% -> 0% of each run, Pallas kernels for 8% -> 10%
where the time goes in v5:
time: 79.8 us; the launch traced here: 79.5 us
  waiting for transfers between devices  38.7 us (48%)
  starting transfers between devices  25.4 us (32%)
  Pallas kernels  14 us (18%)
  local copies, waits for them, and re-layouts  1.19 us (1%)
    ppermute x2, waiting for transfers between devices, far_swap(): lax.ppermute(value, 'narrow', [(i, j) for i, j in pairs if abs(i - j) > 1])  20.8 us
    ppermute x9, waiting for transfers between devices, flip(): lax.ppermute(value, 'wide', [(i, i ^ masks[i & 1]) for i in range(size)])  17.9 us
    ppermute x6, starting transfers between devices, trade(): return lax.ppermute(value, ('wide', 'narrow'), pairs)  11.4 us
    ppermute x2, starting transfers between devices, far_swap(): lax.ppermute(value, 'narrow', [(i, j) for i, j in pairs if abs(i - j) > 1])  8.68 us
    pallas_call x1, Pallas kernels, multiply(): pl.pallas_call(functools.partial(early_kernel, n, plan), out_shape=outs,...  6.21 us
    ppermute x9, starting transfers between devices, flip(): lax.ppermute(value, 'wide', [(i, i ^ masks[i & 1]) for i in range(size)])  5.32 us
    pallas_call x1, Pallas kernels, multiply(): pl.pallas_call(functools.partial(late_kernel, n, keys), out_shape=jax.Sha...  2.82 us
    pallas_call x1, Pallas kernels, standardize(): pl.pallas_call(functools.partial(standardize_kernel, n), out_shape=[jax.S...  2.77 us
  transfers between devices with their start and end apart: 17, of which 5 were waited for; matrix products, arithmetic and copies ran while one was open for 0% of the time, Pallas kernels for 10%

profile of v5, /device:TPU:0, one launch (start us, length us, event | category | flops | bytes accessed | tf_op | source)
XLA Modules:
  0.0 79.5 jit_solution(12423950791917552864)
XLA Ops:
  0.0 2.8 %standardize.1 = (bf16[768,512]{1,0:T(8,128)(2,1)}, bf16[192,512]{1,0:T(8,128)(2,1)}, bf16[192,512]{1,0:T(8,128)(2,1)}) custom-call(s32[512,768]{1,0:T(8,128)} %dosages_ref.1, s32[1,512]{1,0:T(1,128)} %bitcast.5, s32[1,512]{1,0:T(1,128)} %bitcast.6), custom_call_target="tpu_custom_call" | custom-call | tf_op jit(solution)/shard_map/standardize/pallas_call | solution.py:84
  2.8 4.9 %collective-permute-start = (bf16[768,512]{1,0:T(8,128)(2,1)}, bf16[768,512]{1,0:T(8,128)(2,1)S(1)}, u32[]{:S(2)}, u32[]{:S(2)}) collective-permute-start(bf16[768,512]{1,0:T(8,128)(2,1)} %get-tuple-element.23.own), channel_id=1, source_target_pairs={{0,1},{1,0},{2,3},{3,2},{5,6},{6,5},{8,9},{9,8},{10,11},{11,10},{1... | collective-permute-start | bytes 2359304 | tf_op jit(solution)/shard_map/ppermute | solution.py:27
  7.7 0.7 collective-permute-start.1
  8.4 0.0 copy-start
  8.4 1.1 %copy-done = bf16[768,512]{1,0:T(8,128)(2,1)S(1)} copy-done((bf16[768,512]{1,0:T(8,128)(2,1)S(1)}, bf16[768,512]{1,0:T(8,128)(2,1)}, u32[]{:S(2)}) %copy-start) | copy-done | bytes 786456
  9.6 0.2 pick.1.mine
  9.8 3.9 %collective-permute-start.2 = (bf16[192,512]{1,0:T(8,128)(2,1)}, bf16[192,512]{1,0:T(8,128)(2,1)S(1)}, u32[]{:S(2)}, u32[]{:S(2)}) collective-permute-start(bf16[192,512]{1,0:T(8,128)(2,1)} %get-tuple-element.25), channel_id=1, source_target_pairs={{0,2},{1,3},{2,0},{3,1},{4,6},{5,7},{6,4},{7,5},{8,10},{9,11},{10,... | collective-permute-start | bytes 589832 | tf_op jit(solution)/shard_map/ppermute | solution.py:41
  13.7 4.8 %collective-permute-start.3 = (bf16[192,512]{1,0:T(8,128)(2,1)}, bf16[192,512]{1,0:T(8,128)(2,1)S(1)}, u32[]{:S(2)}, u32[]{:S(2)}) collective-permute-start(bf16[192,512]{1,0:T(8,128)(2,1)} %get-tuple-element.27), channel_id=1, source_target_pairs={{0,3},{3,0},{4,7},{7,4},{8,11},{11,8},{12,15},{15,12},{16,19},{19,... | collective-permute-start | bytes 589832 | tf_op jit(solution)/shard_map/ppermute | solution.py:41
  18.5 20.8 %collective-permute-done.2.refs_0_ = bf16[192,512]{1,0:T(8,128)(2,1)S(1)} collective-permute-done((bf16[192,512]{1,0:T(8,128)(2,1)}, bf16[192,512]{1,0:T(8,128)(2,1)S(1)}, u32[]{:S(2)}, u32[]{:S(2)}) %collective-permute-start.2) | collective-permute-done | bytes 196640 | tf_op jit(solution)/shard_map/ppermute | solution.py:41
  39.3 0.4 stack.1.near.refs_4_
  39.6 1.6 %collective-permute-start.7 = (bf16[4,192,512]{2,1,0:T(8,128)(2,1)S(1)}, bf16[4,192,512]{2,1,0:T(8,128)(2,1)S(1)}, u32[]{:S(2)}, u32[]{:S(2)}) collective-permute-start(bf16[4,192,512]{2,1,0:T(8,128)(2,1)S(1)} %stack.1.near.refs_4_), channel_id=1, source_target_pairs={{0,8},{4,20},{8,0},{12,28},{16,24},{20,4},{24,16},{28,12},{1,9},{5... | collective-permute-start | bytes 2359304 | tf_op jit(solution)/shard_map/ppermute | solution.py:392
  41.2 1.5 %collective-permute-start.8 = (bf16[4,192,512]{2,1,0:T(8,128)(2,1)S(1)}, bf16[4,192,512]{2,1,0:T(8,128)(2,1)S(1)}, u32[]{:S(2)}, u32[]{:S(2)}) collective-permute-start(bf16[4,192,512]{2,1,0:T(8,128)(2,1)S(1)} %stack.1.near.refs_4_), channel_id=1, source_target_pairs={{0,16},{4,12},{8,24},{12,4},{16,0},{20,28},{24,8},{28,20},{1,17},{... | collective-permute-start | bytes 2359304 | tf_op jit(solution)/shard_map/ppermute | solution.py:392
  42.7 0.1 hand_on.2
  42.8 1.9 %collective-permute-start.4 = (bf16[576,512]{1,0:T(8,128)(2,1)S(1)}, bf16[576,512]{1,0:T(8,128)(2,1)S(1)}, u32[]{:S(2)}, u32[]{:S(2)}) collective-permute-start(bf16[576,512]{1,0:T(8,128)(2,1)S(1)} %get-tuple-element.28), channel_id=1, source_target_pairs={{0,1},{1,0},{2,3},{3,2},{5,6},{6,5},{8,9},{9,8},{10,11},{11,10},{1... | collective-permute-start | bytes 1769480 | tf_op jit(solution)/shard_map/ppermute | solution.py:27
  44.7 0.0 copy-start.1
  44.7 0.8 %collective-permute-start.5 = (bf16[576,512]{1,0:T(8,128)(2,1)S(1)}, bf16[576,512]{1,0:T(8,128)(2,1)S(1)}, u32[]{:S(2)}, u32[]{:S(2)}) collective-permute-start(bf16[576,512]{1,0:T(8,128)(2,1)S(1)} %get-tuple-element.29), channel_id=1, source_target_pairs={{1,2},{2,1},{4,5},{5,4},{6,7},{7,6},{9,10},{10,9},{12,13},{13,12},... | collective-permute-start | bytes 1769480 | tf_op jit(solution)/shard_map/ppermute | solution.py:27
  45.6 0.1 collective-permute-start.6
  45.6 11.3 %collective-permute-done.8.refs_8_ = bf16[4,192,512]{2,1,0:T(8,128)(2,1)S(1)} collective-permute-done((bf16[4,192,512]{2,1,0:T(8,128)(2,1)S(1)}, bf16[4,192,512]{2,1,0:T(8,128)(2,1)S(1)}, u32[]{:S(2)}, u32[]{:S(2)}) %collective-permute-start.8) | collective-permute-done | bytes 786464 | tf_op jit(solution)/shard_map/ppermute | solution.py:392
  57.0 1.2 %collective-permute-done.7.refs_6_ = bf16[4,192,512]{2,1,0:T(8,128)(2,1)S(1)} collective-permute-done((bf16[4,192,512]{2,1,0:T(8,128)(2,1)S(1)}, bf16[4,192,512]{2,1,0:T(8,128)(2,1)S(1)}, u32[]{:S(2)}, u32[]{:S(2)}) %collective-permute-start.7) | collective-permute-done | bytes 786464 | tf_op jit(solution)/shard_map/ppermute | solution.py:392
  58.2 0.1 hand_on.3
  58.3 2.3 %collective-permute-start.15 = (bf16[576,512]{1,0:T(8,128)(2,1)S(1)}, bf16[576,512]{1,0:T(8,128)(2,1)S(1)}, u32[]{:S(2)}, u32[]{:S(2)}) collective-permute-start(bf16[576,512]{1,0:T(8,128)(2,1)S(1)} %get-tuple-element.31), channel_id=1, source_target_pairs={{0,1},{1,0},{2,3},{3,2},{8,9},{9,8},{10,11},{11,10},{16,17},{17,16... | collective-permute-start | bytes 1769480 | tf_op jit(solution)/shard_map/ppermute | solution.py:27
  60.7 0.7 collective-permute-start.16
  61.4 0.1 fusion
  61.5 0.6 collective-permute-start.11
  62.0 1.5 %collective-permute-start.12 = (bf16[2,192,512]{2,1,0:T(8,128)(2,1)S(1)}, bf16[2,192,512]{2,1,0:T(8,128)(2,1)S(1)}, u32[]{:S(2)}, u32[]{:S(2)}) collective-permute-start(bf16[2,192,512]{2,1,0:T(8,128)(2,1)S(1)} %get-tuple-element.41), channel_id=1, source_target_pairs={{0,16},{4,12},{8,24},{12,4},{16,0},{20,28},{24,8},{28,20},{1,17},{... | collective-permute-start | bytes 1179656 | tf_op jit(solution)/shard_map/ppermute | solution.py:392
  63.6 6.2 %early.1 = (f32[1152,768]{1,0:T(8,128)S(1)}, bf16[1152,512]{1,0:T(8,128)(2,1)S(1)}, bf16[768,1536]{1,0:T(8,128)(2,1)S(1)}) custom-call(bf16[768,512]{1,0:T(8,128)(2,1)S(1)} %copy-done.1, bf16[4,192,512]{2,1,0:T(8,128)(2,1)S(1)} %stack.1.near.refs_4_, bf16[768,512]{1,0:T(8,128)(2,1)S(1)} %collective-permute-done.first.refs_0_, ...), custom_call_target="tpu_custom_call" | custom-call | flops 12000000000 | tf_op jit(solution)/shard_map/early/pallas_call | solution.py:340
  69.8 0.1 collective-permute-start.13
  69.9 3.6 %collective-permute-done.12.refs_1_ = bf16[2,192,512]{2,1,0:T(8,128)(2,1)S(1)} collective-permute-done((bf16[2,192,512]{2,1,0:T(8,128)(2,1)S(1)}, bf16[2,192,512]{2,1,0:T(8,128)(2,1)S(1)}, u32[]{:S(2)}, u32[]{:S(2)}) %collective-permute-start.12) | collective-permute-done | bytes 393248 | tf_op jit(solution)/shard_map/ppermute | solution.py:392
  73.5 1.7 %collective-permute-done.14.refs_3_ = bf16[2,192,512]{2,1,0:T(8,128)(2,1)S(1)} collective-permute-done((bf16[2,192,512]{2,1,0:T(8,128)(2,1)S(1)}, bf16[2,192,512]{2,1,0:T(8,128)(2,1)S(1)}, u32[]{:S(2)}, u32[]{:S(2)}) %collective-permute-start.14) | collective-permute-done | bytes 393248 | tf_op jit(solution)/shard_map/ppermute | solution.py:392
  75.2 1.3 %middle.1 = (f32[384,768]{1,0:T(8,128)S(1)}, bf16[384,512]{1,0:T(8,128)(2,1)S(1)}) custom-call(bf16[768,1536]{1,0:T(8,128)(2,1)S(1)} %get-tuple-element.30.begun, bf16[2,192,512]{2,1,0:T(8,128)(2,1)S(1)} %collective-permute-done.11.refs_0_, bf16[2,192,512]{2,1,0:T(8,128)(2,1)S(1)} %collective-permute-done.12.refs_1_, ...), custom_call_target="tpu_custom_call" | custom-call | tf_op jit(solution)/shard_map/middle/pallas_call | solution.py:357
  76.5 0.2 last_block.1.block
  76.7 2.8 %late.1 = f32[1536,768]{1,0:T(8,128)} custom-call(bf16[768,512]{1,0:T(8,128)(2,1)S(1)} %last_block.1.block, f32[1152,768]{1,0:T(8,128)S(1)} %get-tuple-element.39.early, bf16[1152,512]{1,0:T(8,128)(2,1)S(1)} %get-tuple-element.34.early_rest, f32[384,768]{1,0:T(8,128)S(1)} %get-tuple-element.40.middle, bf16[384,512]{1,0:T(8,128)(2,1)S(1)} %get-tuple-element.37.middle_rest), custom_call_target="tpu_custom_call" | custom-call | tf_op jit(solution)/shard_map/late/pallas_call | solution.py:375
  (16 shorter events, 0.0 us)
Async XLA Ops:
  2.8 36.5 %collective-permute-start = (bf16[768,512]{1,0:T(8,128)(2,1)}, bf16[768,512]{1,0:T(8,128)(2,1)S(1)}, u32[]{:S(2)}, u32[]{:S(2)}) collective-permute-start(bf16[768,512]{1,0:T(8,128)(2,1)} %get-tuple-element.23.own), channel_id=1, source_target_pairs={{0,1},{1,0},{2,3},{3,2},{5,6},{6,5},{8,9},{9,8},{10,11},{11,10},{1... | collective-permute-start | bytes 2359304 | tf_op jit(solution)/shard_map/ppermute | solution.py:27
  7.7 31.6 %collective-permute-start.1 = (bf16[768,512]{1,0:T(8,128)(2,1)}, bf16[768,512]{1,0:T(8,128)(2,1)S(1)}, u32[]{:S(2)}, u32[]{:S(2)}) collective-permute-start(bf16[768,512]{1,0:T(8,128)(2,1)} %get-tuple-element.23.own), channel_id=1, source_target_pairs={{1,2},{2,1},{4,5},{5,4},{6,7},{7,6},{9,10},{10,9},{12,13},{13,12},... | collective-permute-start | bytes 2359304 | tf_op jit(solution)/shard_map/ppermute | solution.py:27
  8.4 1.1 %copy-start = (bf16[768,512]{1,0:T(8,128)(2,1)S(1)}, bf16[768,512]{1,0:T(8,128)(2,1)}, u32[]{:S(2)}) copy-start(bf16[768,512]{1,0:T(8,128)(2,1)} %get-tuple-element.23.own) | copy-start | bytes 2359300
  9.8 29.5 %collective-permute-start.2 = (bf16[192,512]{1,0:T(8,128)(2,1)}, bf16[192,512]{1,0:T(8,128)(2,1)S(1)}, u32[]{:S(2)}, u32[]{:S(2)}) collective-permute-start(bf16[192,512]{1,0:T(8,128)(2,1)} %get-tuple-element.25), channel_id=1, source_target_pairs={{0,2},{1,3},{2,0},{3,1},{4,6},{5,7},{6,4},{7,5},{8,10},{9,11},{10,... | collective-permute-start | bytes 589832 | tf_op jit(solution)/shard_map/ppermute | solution.py:41
  13.7 25.6 %collective-permute-start.3 = (bf16[192,512]{1,0:T(8,128)(2,1)}, bf16[192,512]{1,0:T(8,128)(2,1)S(1)}, u32[]{:S(2)}, u32[]{:S(2)}) collective-permute-start(bf16[192,512]{1,0:T(8,128)(2,1)} %get-tuple-element.27), channel_id=1, source_target_pairs={{0,3},{3,0},{4,7},{7,4},{8,11},{11,8},{12,15},{15,12},{16,19},{19,... | collective-permute-start | bytes 589832 | tf_op jit(solution)/shard_map/ppermute | solution.py:41
  39.6 18.6 %collective-permute-start.7 = (bf16[4,192,512]{2,1,0:T(8,128)(2,1)S(1)}, bf16[4,192,512]{2,1,0:T(8,128)(2,1)S(1)}, u32[]{:S(2)}, u32[]{:S(2)}) collective-permute-start(bf16[4,192,512]{2,1,0:T(8,128)(2,1)S(1)} %stack.1.near.refs_4_), channel_id=1, source_target_pairs={{0,8},{4,20},{8,0},{12,28},{16,24},{20,4},{24,16},{28,12},{1,9},{5... | collective-permute-start | bytes 2359304 | tf_op jit(solution)/shard_map/ppermute | solution.py:392
  41.2 15.8 %collective-permute-start.8 = (bf16[4,192,512]{2,1,0:T(8,128)(2,1)S(1)}, bf16[4,192,512]{2,1,0:T(8,128)(2,1)S(1)}, u32[]{:S(2)}, u32[]{:S(2)}) collective-permute-start(bf16[4,192,512]{2,1,0:T(8,128)(2,1)S(1)} %stack.1.near.refs_4_), channel_id=1, source_target_pairs={{0,16},{4,12},{8,24},{12,4},{16,0},{20,28},{24,8},{28,20},{1,17},{... | collective-permute-start | bytes 2359304 | tf_op jit(solution)/shard_map/ppermute | solution.py:392
  42.8 15.4 %collective-permute-start.4 = (bf16[576,512]{1,0:T(8,128)(2,1)S(1)}, bf16[576,512]{1,0:T(8,128)(2,1)S(1)}, u32[]{:S(2)}, u32[]{:S(2)}) collective-permute-start(bf16[576,512]{1,0:T(8,128)(2,1)S(1)} %get-tuple-element.28), channel_id=1, source_target_pairs={{0,1},{1,0},{2,3},{3,2},{5,6},{6,5},{8,9},{9,8},{10,11},{11,10},{1... | collective-permute-start | bytes 1769480 | tf_op jit(solution)/shard_map/ppermute | solution.py:27
  44.7 18.8 %copy-start.1 = (bf16[768,512]{1,0:T(8,128)(2,1)S(1)}, bf16[768,512]{1,0:T(8,128)(2,1)}, u32[]{:S(2)}) copy-start(bf16[768,512]{1,0:T(8,128)(2,1)} %get-tuple-element.23.own) | copy-start | bytes 2359300
  44.7 13.5 %collective-permute-start.5 = (bf16[576,512]{1,0:T(8,128)(2,1)S(1)}, bf16[576,512]{1,0:T(8,128)(2,1)S(1)}, u32[]{:S(2)}, u32[]{:S(2)}) collective-permute-start(bf16[576,512]{1,0:T(8,128)(2,1)S(1)} %get-tuple-element.29), channel_id=1, source_target_pairs={{1,2},{2,1},{4,5},{5,4},{6,7},{7,6},{9,10},{10,9},{12,13},{13,12},... | collective-permute-start | bytes 1769480 | tf_op jit(solution)/shard_map/ppermute | solution.py:27
  45.6 15.9 %collective-permute-start.6 = (bf16[4,192,512]{2,1,0:T(8,128)(2,1)S(1)}, bf16[4,192,512]{2,1,0:T(8,128)(2,1)S(1)}, u32[]{:S(2)}, u32[]{:S(2)}) collective-permute-start(bf16[4,192,512]{2,1,0:T(8,128)(2,1)S(1)} %stack.1.near.refs_4_), channel_id=1, source_target_pairs={{0,4},{4,0},{8,12},{12,8},{16,20},{20,16},{24,28},{28,24},{1,5},{5... | collective-permute-start | bytes 2359304 | tf_op jit(solution)/shard_map/ppermute | solution.py:392
  57.0 5.1 %collective-permute-start.9 = (bf16[4,192,512]{2,1,0:T(8,128)(2,1)S(1)}, bf16[4,192,512]{2,1,0:T(8,128)(2,1)S(1)}, u32[]{:S(2)}, u32[]{:S(2)}) collective-permute-start(bf16[4,192,512]{2,1,0:T(8,128)(2,1)S(1)} %collective-permute-done.8.refs_8_), channel_id=1, source_target_pairs={{0,4},{4,0},{8,12},{12,8},{16,20},{20,16},{24,28},{28,24},{1,5},{5... | collective-permute-start | bytes 2359304 | tf_op jit(solution)/shard_map/ppermute | solution.py:392
  58.2 5.4 %collective-permute-start.10 = (bf16[4,192,512]{2,1,0:T(8,128)(2,1)S(1)}, bf16[4,192,512]{2,1,0:T(8,128)(2,1)S(1)}, u32[]{:S(2)}, u32[]{:S(2)}) collective-permute-start(bf16[4,192,512]{2,1,0:T(8,128)(2,1)S(1)} %collective-permute-done.7.refs_6_), channel_id=1, source_target_pairs={{0,4},{4,0},{8,12},{12,8},{16,20},{20,16},{24,28},{28,24},{1,5},{5... | collective-permute-start | bytes 2359304 | tf_op jit(solution)/shard_map/ppermute | solution.py:392
  58.3 18.2 %collective-permute-start.15 = (bf16[576,512]{1,0:T(8,128)(2,1)S(1)}, bf16[576,512]{1,0:T(8,128)(2,1)S(1)}, u32[]{:S(2)}, u32[]{:S(2)}) collective-permute-start(bf16[576,512]{1,0:T(8,128)(2,1)S(1)} %get-tuple-element.31), channel_id=1, source_target_pairs={{0,1},{1,0},{2,3},{3,2},{8,9},{9,8},{10,11},{11,10},{16,17},{17,16... | collective-permute-start | bytes 1769480 | tf_op jit(solution)/shard_map/ppermute | solution.py:27
  60.7 15.9 %collective-permute-start.16 = (bf16[576,512]{1,0:T(8,128)(2,1)S(1)}, bf16[576,512]{1,0:T(8,128)(2,1)S(1)}, u32[]{:S(2)}, u32[]{:S(2)}) collective-permute-start(bf16[576,512]{1,0:T(8,128)(2,1)S(1)} %get-tuple-element.32), channel_id=1, source_target_pairs={{4,5},{5,4},{6,7},{7,6},{12,13},{13,12},{14,15},{15,14},{20,21},{2... | collective-permute-start | bytes 1769480 | tf_op jit(solution)/shard_map/ppermute | solution.py:27
  61.5 8.3 %collective-permute-start.11 = (bf16[2,192,512]{2,1,0:T(8,128)(2,1)S(1)}, bf16[2,192,512]{2,1,0:T(8,128)(2,1)S(1)}, u32[]{:S(2)}, u32[]{:S(2)}) collective-permute-start(bf16[2,192,512]{2,1,0:T(8,128)(2,1)S(1)} %get-tuple-element.42), channel_id=1, source_target_pairs={{0,16},{4,12},{8,24},{12,4},{16,0},{20,28},{24,8},{28,20},{1,17},{... | collective-permute-start | bytes 1179656 | tf_op jit(solution)/shard_map/ppermute | solution.py:392
  62.0 11.5 %collective-permute-start.12 = (bf16[2,192,512]{2,1,0:T(8,128)(2,1)S(1)}, bf16[2,192,512]{2,1,0:T(8,128)(2,1)S(1)}, u32[]{:S(2)}, u32[]{:S(2)}) collective-permute-start(bf16[2,192,512]{2,1,0:T(8,128)(2,1)S(1)} %get-tuple-element.41), channel_id=1, source_target_pairs={{0,16},{4,12},{8,24},{12,4},{16,0},{20,28},{24,8},{28,20},{1,17},{... | collective-permute-start | bytes 1179656 | tf_op jit(solution)/shard_map/ppermute | solution.py:392
  69.8 3.7 %collective-permute-start.13 = (bf16[2,192,512]{2,1,0:T(8,128)(2,1)S(1)}, bf16[2,192,512]{2,1,0:T(8,128)(2,1)S(1)}, u32[]{:S(2)}, u32[]{:S(2)}) collective-permute-start(bf16[2,192,512]{2,1,0:T(8,128)(2,1)S(1)} %collective-permute-done.11.refs_0_), channel_id=1, source_target_pairs={{0,4},{4,0},{8,12},{12,8},{16,20},{20,16},{24,28},{28,24},{1,5},{5... | collective-permute-start | bytes 1179656 | tf_op jit(solution)/shard_map/ppermute | solution.py:392
  73.5 1.7 %collective-permute-start.14 = (bf16[2,192,512]{2,1,0:T(8,128)(2,1)S(1)}, bf16[2,192,512]{2,1,0:T(8,128)(2,1)S(1)}, u32[]{:S(2)}, u32[]{:S(2)}) collective-permute-start(bf16[2,192,512]{2,1,0:T(8,128)(2,1)S(1)} %collective-permute-done.12.refs_1_), channel_id=1, source_target_pairs={{0,4},{4,0},{8,12},{12,8},{16,20},{20,16},{24,28},{28,24},{1,5},{5... | collective-permute-start | bytes 1179656 | tf_op jit(solution)/shard_map/ppermute | solution.py:392

commit v6 on v5

--- a/solution.py
+++ b/solution.py
@@ -47,7 +47,7 @@
 
 
 def standardize_kernel(n, dosages_ref, allele_ref, called_ref, own, *refs):
-    panels, (dosages, allele, called, sem) = refs[: n - 2], refs[n - 2 :]
+    panels, (dosages, allele, called, block, sem, out_sem) = refs[: n - 2], refs[n - 2 :]
     z = lax.axis_index("narrow")
     snps, cols = dosages.shape
     sub = cols // n
@@ -65,6 +65,7 @@
     for copy in counts:
         copy.wait()
 
+    outs = []
     for i, start in enumerate(starts):
         doses[i].wait()
         lanes = pl.ds(start, LANES)
@@ -72,9 +73,15 @@
         scale = lax.rsqrt(2.0 * freq * (1.0 - freq))
         dose = dosages[lanes, :].astype(jnp.float32).T
         values = jnp.where(dose == 3.0, 0.0, (dose - 2.0 * freq) * scale).astype(jnp.bfloat16)
-        own[:, lanes] = values
+        block[:, lanes] = values
+        outs.append(pltpu.make_async_copy(block.at[:, lanes], own.at[:, lanes], out_sem.at[i]))
+        outs[-1].start()
     for m, ref in enumerate(panels, 2):
-        ref[...] = own[pl.ds(pl.multiple_of((z ^ m) * sub, sub), sub), :]
+        rows = pl.ds(pl.multiple_of((z ^ m) * sub, sub), sub)
+        outs.append(pltpu.make_async_copy(block.at[rows, :], ref, out_sem.at[len(outs)]))
+        outs[-1].start()
+    for copy in outs:
+        copy.wait()
 
 
 def standardize(dosages, allele_counts, called_counts, n):
@@ -84,12 +91,15 @@
     outs = pl.pallas_call(
         functools.partial(standardize_kernel, n),
         out_shape=[jax.ShapeDtypeStruct(shape, jnp.bfloat16) for shape in shapes],
-        in_specs=[pl.BlockSpec(memory_space=pltpu.HBM)] * 3,
+        in_specs=[HBM] * 3,
+        out_specs=[ANY] * len(shapes),
         scratch_shapes=[
             pltpu.VMEM((snps, cols), jnp.int32),
             pltpu.VMEM((1, snps), jnp.int32),
             pltpu.VMEM((1, snps), jnp.int32),
+            pltpu.VMEM((cols, snps), jnp.bfloat16),
             pltpu.SemaphoreType.DMA((2 + snps // LANES,)),
+            pltpu.SemaphoreType.DMA((snps // LANES + n - 2,)),
         ],
         compiler_params=pltpu.CompilerParams(vmem_limit_bytes=60 * 2**20),
         name="standardize",
@@ -418,7 +428,7 @@
     own, panels = standardize(dosages, allele_counts, called_counts, n)
     got = {(swapped, 1): trade(own, swapped, 1) for swapped in range(2)}
     mine = pick(own, sub)
-    pieces = [far_swap(after(value, mine), m) for m, value in enumerate(panels, 2)]
+    pieces = [far_swap(after(value, mine) if m > 2 else value, m) for m, value in enumerate(panels, 2)]
     near = stack(mine, got[0, 1], got[1, 1], pieces)
     ready = []
     for step in range(2, n):

time: 79.8 us -> 79.7 us (level)
  no operation moved by 1% of the time
where the time goes in v6:
time: 79.7 us; the launch traced here: 79.4 us
  waiting for transfers between devices  38.7 us (49%)
  starting transfers between devices  25.4 us (32%)
  Pallas kernels  13.8 us (17%)
  local copies, waits for them, and re-layouts  1.19 us (1%)
    ppermute x2, waiting for transfers between devices, far_swap(): lax.ppermute(value, 'narrow', [(i, j) for i, j in pairs if abs(i - j) > 1])  20.8 us
    ppermute x9, waiting for transfers between devices, flip(): lax.ppermute(value, 'wide', [(i, i ^ masks[i & 1]) for i in range(size)])  17.9 us
    ppermute x6, starting transfers between devices, trade(): return lax.ppermute(value, ('wide', 'narrow'), pairs)  11.4 us
    ppermute x2, starting transfers between devices, far_swap(): lax.ppermute(value, 'narrow', [(i, j) for i, j in pairs if abs(i - j) > 1])  8.68 us
    pallas_call x1, Pallas kernels, multiply(): pl.pallas_call(functools.partial(early_kernel, n, plan), out_shape=outs,...  6.21 us
    ppermute x9, starting transfers between devices, flip(): lax.ppermute(value, 'wide', [(i, i ^ masks[i & 1]) for i in range(size)])  5.32 us
    pallas_call x1, Pallas kernels, multiply(): pl.pallas_call(functools.partial(late_kernel, n, keys), out_shape=jax.Sha...  2.82 us
    pallas_call x1, Pallas kernels, standardize(): pl.pallas_call(functools.partial(standardize_kernel, n), out_shape=[jax.S...  2.63 us
  transfers between devices with their start and end apart: 17, of which 5 were waited for; matrix products, arithmetic and copies ran while one was open for 0% of the time, Pallas kernels for 10%

profile of v6, /device:TPU:0, one launch (start us, length us, event | category | flops | bytes accessed | tf_op | source)
XLA Modules:
  0.0 79.4 jit_solution(187620019873709615)
XLA Ops:
  0.0 2.6 %standardize.1 = (bf16[768,512]{1,0:T(8,128)(2,1)}, bf16[192,512]{1,0:T(8,128)(2,1)}, bf16[192,512]{1,0:T(8,128)(2,1)}) custom-call(s32[512,768]{1,0:T(8,128)} %dosages_ref.1, s32[1,512]{1,0:T(1,128)} %bitcast.5, s32[1,512]{1,0:T(1,128)} %bitcast.6), custom_call_target="tpu_custom_call" | custom-call | tf_op jit(solution)/shard_map/standardize/pallas_call | solution.py:91
  2.6 4.9 %collective-permute-start = (bf16[768,512]{1,0:T(8,128)(2,1)}, bf16[768,512]{1,0:T(8,128)(2,1)S(1)}, u32[]{:S(2)}, u32[]{:S(2)}) collective-permute-start(bf16[768,512]{1,0:T(8,128)(2,1)} %get-tuple-element.22.own), channel_id=1, source_target_pairs={{0,1},{1,0},{2,3},{3,2},{5,6},{6,5},{8,9},{9,8},{10,11},{11,10},{1... | collective-permute-start | bytes 2359304 | tf_op jit(solution)/shard_map/ppermute | solution.py:27
  7.6 0.7 collective-permute-start.1
  8.3 3.9 %collective-permute-start.2 = (bf16[192,512]{1,0:T(8,128)(2,1)}, bf16[192,512]{1,0:T(8,128)(2,1)S(1)}, u32[]{:S(2)}, u32[]{:S(2)}) collective-permute-start(bf16[192,512]{1,0:T(8,128)(2,1)} %get-tuple-element.23), channel_id=1, source_target_pairs={{0,2},{1,3},{2,0},{3,1},{4,6},{5,7},{6,4},{7,5},{8,10},{9,11},{10,... | collective-permute-start | bytes 589832 | tf_op jit(solution)/shard_map/ppermute | solution.py:41
  12.2 1.1 %copy-done = bf16[768,512]{1,0:T(8,128)(2,1)S(1)} copy-done((bf16[768,512]{1,0:T(8,128)(2,1)S(1)}, bf16[768,512]{1,0:T(8,128)(2,1)}, u32[]{:S(2)}) %copy-start) | copy-done | bytes 786456
  13.3 0.2 pick.1.mine
  13.5 4.8 %collective-permute-start.3 = (bf16[192,512]{1,0:T(8,128)(2,1)}, bf16[192,512]{1,0:T(8,128)(2,1)S(1)}, u32[]{:S(2)}, u32[]{:S(2)}) collective-permute-start(bf16[192,512]{1,0:T(8,128)(2,1)} %get-tuple-element.25), channel_id=1, source_target_pairs={{0,3},{3,0},{4,7},{7,4},{8,11},{11,8},{12,15},{15,12},{16,19},{19,... | collective-permute-start | bytes 589832 | tf_op jit(solution)/shard_map/ppermute | solution.py:41
  18.4 20.8 %collective-permute-done.2.refs_0_ = bf16[192,512]{1,0:T(8,128)(2,1)S(1)} collective-permute-done((bf16[192,512]{1,0:T(8,128)(2,1)}, bf16[192,512]{1,0:T(8,128)(2,1)S(1)}, u32[]{:S(2)}, u32[]{:S(2)}) %collective-permute-start.2) | collective-permute-done | bytes 196640 | tf_op jit(solution)/shard_map/ppermute | solution.py:41
  39.1 0.0 collective-permute-done.3.refs_1_
  39.1 0.4 stack.1.near.refs_4_
  39.5 1.6 %collective-permute-start.7 = (bf16[4,192,512]{2,1,0:T(8,128)(2,1)S(1)}, bf16[4,192,512]{2,1,0:T(8,128)(2,1)S(1)}, u32[]{:S(2)}, u32[]{:S(2)}) collective-permute-start(bf16[4,192,512]{2,1,0:T(8,128)(2,1)S(1)} %stack.1.near.refs_4_), channel_id=1, source_target_pairs={{0,8},{4,20},{8,0},{12,28},{16,24},{20,4},{24,16},{28,12},{1,9},{5... | collective-permute-start | bytes 2359304 | tf_op jit(solution)/shard_map/ppermute | solution.py:402
  41.1 1.5 %collective-permute-start.8 = (bf16[4,192,512]{2,1,0:T(8,128)(2,1)S(1)}, bf16[4,192,512]{2,1,0:T(8,128)(2,1)S(1)}, u32[]{:S(2)}, u32[]{:S(2)}) collective-permute-start(bf16[4,192,512]{2,1,0:T(8,128)(2,1)S(1)} %stack.1.near.refs_4_), channel_id=1, source_target_pairs={{0,16},{4,12},{8,24},{12,4},{16,0},{20,28},{24,8},{28,20},{1,17},{... | collective-permute-start | bytes 2359304 | tf_op jit(solution)/shard_map/ppermute | solution.py:402
  42.6 0.1 hand_on.2
  42.7 1.9 %collective-permute-start.4 = (bf16[576,512]{1,0:T(8,128)(2,1)S(1)}, bf16[576,512]{1,0:T(8,128)(2,1)S(1)}, u32[]{:S(2)}, u32[]{:S(2)}) collective-permute-start(bf16[576,512]{1,0:T(8,128)(2,1)S(1)} %get-tuple-element.26), channel_id=1, source_target_pairs={{0,1},{1,0},{2,3},{3,2},{5,6},{6,5},{8,9},{9,8},{10,11},{11,10},{1... | collective-permute-start | bytes 1769480 | tf_op jit(solution)/shard_map/ppermute | solution.py:27
  44.6 0.0 copy-start.1
  44.6 0.8 %collective-permute-start.5 = (bf16[576,512]{1,0:T(8,128)(2,1)S(1)}, bf16[576,512]{1,0:T(8,128)(2,1)S(1)}, u32[]{:S(2)}, u32[]{:S(2)}) collective-permute-start(bf16[576,512]{1,0:T(8,128)(2,1)S(1)} %get-tuple-element.27), channel_id=1, source_target_pairs={{1,2},{2,1},{4,5},{5,4},{6,7},{7,6},{9,10},{10,9},{12,13},{13,12},... | collective-permute-start | bytes 1769480 | tf_op jit(solution)/shard_map/ppermute | solution.py:27
  45.4 0.1 collective-permute-start.6
  45.5 11.3 %collective-permute-done.8.refs_8_ = bf16[4,192,512]{2,1,0:T(8,128)(2,1)S(1)} collective-permute-done((bf16[4,192,512]{2,1,0:T(8,128)(2,1)S(1)}, bf16[4,192,512]{2,1,0:T(8,128)(2,1)S(1)}, u32[]{:S(2)}, u32[]{:S(2)}) %collective-permute-start.8) | collective-permute-done | bytes 786464 | tf_op jit(solution)/shard_map/ppermute | solution.py:402
  56.8 1.2 %collective-permute-done.7.refs_6_ = bf16[4,192,512]{2,1,0:T(8,128)(2,1)S(1)} collective-permute-done((bf16[4,192,512]{2,1,0:T(8,128)(2,1)S(1)}, bf16[4,192,512]{2,1,0:T(8,128)(2,1)S(1)}, u32[]{:S(2)}, u32[]{:S(2)}) %collective-permute-start.7) | collective-permute-done | bytes 786464 | tf_op jit(solution)/shard_map/ppermute | solution.py:402
  58.1 0.1 hand_on.3
  58.2 2.3 %collective-permute-start.15 = (bf16[576,512]{1,0:T(8,128)(2,1)S(1)}, bf16[576,512]{1,0:T(8,128)(2,1)S(1)}, u32[]{:S(2)}, u32[]{:S(2)}) collective-permute-start(bf16[576,512]{1,0:T(8,128)(2,1)S(1)} %get-tuple-element.29), channel_id=1, source_target_pairs={{0,1},{1,0},{2,3},{3,2},{8,9},{9,8},{10,11},{11,10},{16,17},{17,16... | collective-permute-start | bytes 1769480 | tf_op jit(solution)/shard_map/ppermute | solution.py:27
  60.5 0.7 collective-permute-start.16
  61.2 0.1 fusion
  61.3 0.6 collective-permute-start.11
  61.9 1.5 %collective-permute-start.12 = (bf16[2,192,512]{2,1,0:T(8,128)(2,1)S(1)}, bf16[2,192,512]{2,1,0:T(8,128)(2,1)S(1)}, u32[]{:S(2)}, u32[]{:S(2)}) collective-permute-start(bf16[2,192,512]{2,1,0:T(8,128)(2,1)S(1)} %get-tuple-element.39), channel_id=1, source_target_pairs={{0,16},{4,12},{8,24},{12,4},{16,0},{20,28},{24,8},{28,20},{1,17},{... | collective-permute-start | bytes 1179656 | tf_op jit(solution)/shard_map/ppermute | solution.py:402
  63.4 6.2 %early.1 = (f32[1152,768]{1,0:T(8,128)S(1)}, bf16[1152,512]{1,0:T(8,128)(2,1)S(1)}, bf16[768,1536]{1,0:T(8,128)(2,1)S(1)}) custom-call(bf16[768,512]{1,0:T(8,128)(2,1)S(1)} %copy-done.1, bf16[4,192,512]{2,1,0:T(8,128)(2,1)S(1)} %stack.1.near.refs_4_, bf16[768,512]{1,0:T(8,128)(2,1)S(1)} %collective-permute-done.first.refs_0_, ...), custom_call_target="tpu_custom_call" | custom-call | flops 12000000000 | tf_op jit(solution)/shard_map/early/pallas_call | solution.py:350
  69.6 0.1 collective-permute-start.13
  69.7 3.6 %collective-permute-done.12.refs_1_ = bf16[2,192,512]{2,1,0:T(8,128)(2,1)S(1)} collective-permute-done((bf16[2,192,512]{2,1,0:T(8,128)(2,1)S(1)}, bf16[2,192,512]{2,1,0:T(8,128)(2,1)S(1)}, u32[]{:S(2)}, u32[]{:S(2)}) %collective-permute-start.12) | collective-permute-done | bytes 393248 | tf_op jit(solution)/shard_map/ppermute | solution.py:402
  73.4 1.7 %collective-permute-done.14.refs_3_ = bf16[2,192,512]{2,1,0:T(8,128)(2,1)S(1)} collective-permute-done((bf16[2,192,512]{2,1,0:T(8,128)(2,1)S(1)}, bf16[2,192,512]{2,1,0:T(8,128)(2,1)S(1)}, u32[]{:S(2)}, u32[]{:S(2)}) %collective-permute-start.14) | collective-permute-done | bytes 393248 | tf_op jit(solution)/shard_map/ppermute | solution.py:402
  75.1 1.3 %middle.1 = (f32[384,768]{1,0:T(8,128)S(1)}, bf16[384,512]{1,0:T(8,128)(2,1)S(1)}) custom-call(bf16[768,1536]{1,0:T(8,128)(2,1)S(1)} %get-tuple-element.28.begun, bf16[2,192,512]{2,1,0:T(8,128)(2,1)S(1)} %collective-permute-done.11.refs_0_, bf16[2,192,512]{2,1,0:T(8,128)(2,1)S(1)} %collective-permute-done.12.refs_1_, ...), custom_call_target="tpu_custom_call" | custom-call | tf_op jit(solution)/shard_map/middle/pallas_call | solution.py:367
  76.4 0.2 last_block.1.block
  76.6 2.8 %late.1 = f32[1536,768]{1,0:T(8,128)} custom-call(bf16[768,512]{1,0:T(8,128)(2,1)S(1)} %last_block.1.block, f32[1152,768]{1,0:T(8,128)S(1)} %get-tuple-element.37.early, bf16[1152,512]{1,0:T(8,128)(2,1)S(1)} %get-tuple-element.32.early_rest, f32[384,768]{1,0:T(8,128)S(1)} %get-tuple-element.38.middle, bf16[384,512]{1,0:T(8,128)(2,1)S(1)} %get-tuple-element.35.middle_rest), custom_call_target="tpu_custom_call" | custom-call | tf_op jit(solution)/shard_map/late/pallas_call | solution.py:385
  (16 shorter events, 0.0 us)
Async XLA Ops:
  2.6 36.5 %collective-permute-start = (bf16[768,512]{1,0:T(8,128)(2,1)}, bf16[768,512]{1,0:T(8,128)(2,1)S(1)}, u32[]{:S(2)}, u32[]{:S(2)}) collective-permute-start(bf16[768,512]{1,0:T(8,128)(2,1)} %get-tuple-element.22.own), channel_id=1, source_target_pairs={{0,1},{1,0},{2,3},{3,2},{5,6},{6,5},{8,9},{9,8},{10,11},{11,10},{1... | collective-permute-start | bytes 2359304 | tf_op jit(solution)/shard_map/ppermute | solution.py:27
  7.6 31.6 %collective-permute-start.1 = (bf16[768,512]{1,0:T(8,128)(2,1)}, bf16[768,512]{1,0:T(8,128)(2,1)S(1)}, u32[]{:S(2)}, u32[]{:S(2)}) collective-permute-start(bf16[768,512]{1,0:T(8,128)(2,1)} %get-tuple-element.22.own), channel_id=1, source_target_pairs={{1,2},{2,1},{4,5},{5,4},{6,7},{7,6},{9,10},{10,9},{12,13},{13,12},... | collective-permute-start | bytes 2359304 | tf_op jit(solution)/shard_map/ppermute | solution.py:27
  8.3 30.8 %collective-permute-start.2 = (bf16[192,512]{1,0:T(8,128)(2,1)}, bf16[192,512]{1,0:T(8,128)(2,1)S(1)}, u32[]{:S(2)}, u32[]{:S(2)}) collective-permute-start(bf16[192,512]{1,0:T(8,128)(2,1)} %get-tuple-element.23), channel_id=1, source_target_pairs={{0,2},{1,3},{2,0},{3,1},{4,6},{5,7},{6,4},{7,5},{8,10},{9,11},{10,... | collective-permute-start | bytes 589832 | tf_op jit(solution)/shard_map/ppermute | solution.py:41
  12.2 1.1 %copy-start = (bf16[768,512]{1,0:T(8,128)(2,1)S(1)}, bf16[768,512]{1,0:T(8,128)(2,1)}, u32[]{:S(2)}) copy-start(bf16[768,512]{1,0:T(8,128)(2,1)} %get-tuple-element.22.own) | copy-start | bytes 2359300
  13.5 25.6 %collective-permute-start.3 = (bf16[192,512]{1,0:T(8,128)(2,1)}, bf16[192,512]{1,0:T(8,128)(2,1)S(1)}, u32[]{:S(2)}, u32[]{:S(2)}) collective-permute-start(bf16[192,512]{1,0:T(8,128)(2,1)} %get-tuple-element.25), channel_id=1, source_target_pairs={{0,3},{3,0},{4,7},{7,4},{8,11},{11,8},{12,15},{15,12},{16,19},{19,... | collective-permute-start | bytes 589832 | tf_op jit(solution)/shard_map/ppermute | solution.py:41
  39.5 18.6 %collective-permute-start.7 = (bf16[4,192,512]{2,1,0:T(8,128)(2,1)S(1)}, bf16[4,192,512]{2,1,0:T(8,128)(2,1)S(1)}, u32[]{:S(2)}, u32[]{:S(2)}) collective-permute-start(bf16[4,192,512]{2,1,0:T(8,128)(2,1)S(1)} %stack.1.near.refs_4_), channel_id=1, source_target_pairs={{0,8},{4,20},{8,0},{12,28},{16,24},{20,4},{24,16},{28,12},{1,9},{5... | collective-permute-start | bytes 2359304 | tf_op jit(solution)/shard_map/ppermute | solution.py:402
  41.1 15.8 %collective-permute-start.8 = (bf16[4,192,512]{2,1,0:T(8,128)(2,1)S(1)}, bf16[4,192,512]{2,1,0:T(8,128)(2,1)S(1)}, u32[]{:S(2)}, u32[]{:S(2)}) collective-permute-start(bf16[4,192,512]{2,1,0:T(8,128)(2,1)S(1)} %stack.1.near.refs_4_), channel_id=1, source_target_pairs={{0,16},{4,12},{8,24},{12,4},{16,0},{20,28},{24,8},{28,20},{1,17},{... | collective-permute-start | bytes 2359304 | tf_op jit(solution)/shard_map/ppermute | solution.py:402
  42.7 15.4 %collective-permute-start.4 = (bf16[576,512]{1,0:T(8,128)(2,1)S(1)}, bf16[576,512]{1,0:T(8,128)(2,1)S(1)}, u32[]{:S(2)}, u32[]{:S(2)}) collective-permute-start(bf16[576,512]{1,0:T(8,128)(2,1)S(1)} %get-tuple-element.26), channel_id=1, source_target_pairs={{0,1},{1,0},{2,3},{3,2},{5,6},{6,5},{8,9},{9,8},{10,11},{11,10},{1... | collective-permute-start | bytes 1769480 | tf_op jit(solution)/shard_map/ppermute | solution.py:27
  44.6 18.8 %copy-start.1 = (bf16[768,512]{1,0:T(8,128)(2,1)S(1)}, bf16[768,512]{1,0:T(8,128)(2,1)}, u32[]{:S(2)}) copy-start(bf16[768,512]{1,0:T(8,128)(2,1)} %get-tuple-element.22.own) | copy-start | bytes 2359300
  44.6 13.5 %collective-permute-start.5 = (bf16[576,512]{1,0:T(8,128)(2,1)S(1)}, bf16[576,512]{1,0:T(8,128)(2,1)S(1)}, u32[]{:S(2)}, u32[]{:S(2)}) collective-permute-start(bf16[576,512]{1,0:T(8,128)(2,1)S(1)} %get-tuple-element.27), channel_id=1, source_target_pairs={{1,2},{2,1},{4,5},{5,4},{6,7},{7,6},{9,10},{10,9},{12,13},{13,12},... | collective-permute-start | bytes 1769480 | tf_op jit(solution)/shard_map/ppermute | solution.py:27
  45.4 15.9 %collective-permute-start.6 = (bf16[4,192,512]{2,1,0:T(8,128)(2,1)S(1)}, bf16[4,192,512]{2,1,0:T(8,128)(2,1)S(1)}, u32[]{:S(2)}, u32[]{:S(2)}) collective-permute-start(bf16[4,192,512]{2,1,0:T(8,128)(2,1)S(1)} %stack.1.near.refs_4_), channel_id=1, source_target_pairs={{0,4},{4,0},{8,12},{12,8},{16,20},{20,16},{24,28},{28,24},{1,5},{5... | collective-permute-start | bytes 2359304 | tf_op jit(solution)/shard_map/ppermute | solution.py:402
  56.8 5.1 %collective-permute-start.9 = (bf16[4,192,512]{2,1,0:T(8,128)(2,1)S(1)}, bf16[4,192,512]{2,1,0:T(8,128)(2,1)S(1)}, u32[]{:S(2)}, u32[]{:S(2)}) collective-permute-start(bf16[4,192,512]{2,1,0:T(8,128)(2,1)S(1)} %collective-permute-done.8.refs_8_), channel_id=1, source_target_pairs={{0,4},{4,0},{8,12},{12,8},{16,20},{20,16},{24,28},{28,24},{1,5},{5... | collective-permute-start | bytes 2359304 | tf_op jit(solution)/shard_map/ppermute | solution.py:402
  58.1 5.4 %collective-permute-start.10 = (bf16[4,192,512]{2,1,0:T(8,128)(2,1)S(1)}, bf16[4,192,512]{2,1,0:T(8,128)(2,1)S(1)}, u32[]{:S(2)}, u32[]{:S(2)}) collective-permute-start(bf16[4,192,512]{2,1,0:T(8,128)(2,1)S(1)} %collective-permute-done.7.refs_6_), channel_id=1, source_target_pairs={{0,4},{4,0},{8,12},{12,8},{16,20},{20,16},{24,28},{28,24},{1,5},{5... | collective-permute-start | bytes 2359304 | tf_op jit(solution)/shard_map/ppermute | solution.py:402
  58.2 18.2 %collective-permute-start.15 = (bf16[576,512]{1,0:T(8,128)(2,1)S(1)}, bf16[576,512]{1,0:T(8,128)(2,1)S(1)}, u32[]{:S(2)}, u32[]{:S(2)}) collective-permute-start(bf16[576,512]{1,0:T(8,128)(2,1)S(1)} %get-tuple-element.29), channel_id=1, source_target_pairs={{0,1},{1,0},{2,3},{3,2},{8,9},{9,8},{10,11},{11,10},{16,17},{17,16... | collective-permute-start | bytes 1769480 | tf_op jit(solution)/shard_map/ppermute | solution.py:27
  60.5 15.8 %collective-permute-start.16 = (bf16[576,512]{1,0:T(8,128)(2,1)S(1)}, bf16[576,512]{1,0:T(8,128)(2,1)S(1)}, u32[]{:S(2)}, u32[]{:S(2)}) collective-permute-start(bf16[576,512]{1,0:T(8,128)(2,1)S(1)} %get-tuple-element.30), channel_id=1, source_target_pairs={{4,5},{5,4},{6,7},{7,6},{12,13},{13,12},{14,15},{15,14},{20,21},{2... | collective-permute-start | bytes 1769480 | tf_op jit(solution)/shard_map/ppermute | solution.py:27
  61.3 8.3 %collective-permute-start.11 = (bf16[2,192,512]{2,1,0:T(8,128)(2,1)S(1)}, bf16[2,192,512]{2,1,0:T(8,128)(2,1)S(1)}, u32[]{:S(2)}, u32[]{:S(2)}) collective-permute-start(bf16[2,192,512]{2,1,0:T(8,128)(2,1)S(1)} %get-tuple-element.40), channel_id=1, source_target_pairs={{0,16},{4,12},{8,24},{12,4},{16,0},{20,28},{24,8},{28,20},{1,17},{... | collective-permute-start | bytes 1179656 | tf_op jit(solution)/shard_map/ppermute | solution.py:402
  61.9 11.5 %collective-permute-start.12 = (bf16[2,192,512]{2,1,0:T(8,128)(2,1)S(1)}, bf16[2,192,512]{2,1,0:T(8,128)(2,1)S(1)}, u32[]{:S(2)}, u32[]{:S(2)}) collective-permute-start(bf16[2,192,512]{2,1,0:T(8,128)(2,1)S(1)} %get-tuple-element.39), channel_id=1, source_target_pairs={{0,16},{4,12},{8,24},{12,4},{16,0},{20,28},{24,8},{28,20},{1,17},{... | collective-permute-start | bytes 1179656 | tf_op jit(solution)/shard_map/ppermute | solution.py:402
  69.6 3.7 %collective-permute-start.13 = (bf16[2,192,512]{2,1,0:T(8,128)(2,1)S(1)}, bf16[2,192,512]{2,1,0:T(8,128)(2,1)S(1)}, u32[]{:S(2)}, u32[]{:S(2)}) collective-permute-start(bf16[2,192,512]{2,1,0:T(8,128)(2,1)S(1)} %collective-permute-done.11.refs_0_), channel_id=1, source_target_pairs={{0,4},{4,0},{8,12},{12,8},{16,20},{20,16},{24,28},{28,24},{1,5},{5... | collective-permute-start | bytes 1179656 | tf_op jit(solution)/shard_map/ppermute | solution.py:402
  73.4 1.7 %collective-permute-start.14 = (bf16[2,192,512]{2,1,0:T(8,128)(2,1)S(1)}, bf16[2,192,512]{2,1,0:T(8,128)(2,1)S(1)}, u32[]{:S(2)}, u32[]{:S(2)}) collective-permute-start(bf16[2,192,512]{2,1,0:T(8,128)(2,1)S(1)} %collective-permute-done.12.refs_1_), channel_id=1, source_target_pairs={{0,4},{4,0},{8,12},{12,8},{16,20},{20,16},{24,28},{28,24},{1,5},{5... | collective-permute-start | bytes 1179656 | tf_op jit(solution)/shard_map/ppermute | solution.py:402
